TPU v7x, 32 devices: a whole 2x2x4 slice. The times are simulated.
32 devices in a mesh: section: 2 (over y), dp: 16 (over z, x, core).
Axes of the slice: x: 2, y: 2, z: 4, core: 2. Of those that a mesh axis runs over, the one named last changes fastest.
Arguments:
- tokens: bfloat16 [2, 32768, 512], P('section', 'dp'), may hold values from -6 to 6
- cotangent: bfloat16 [2, 32768, 512], P('section', 'dp'), may hold values from -6 to 6
- lengths: int32 [2, 64], P(None, 'dp'), may hold values from 256 to 512, as said below
- owners: int32 [2, 9], P('section'), may hold values from 0 to 15, as said below
- master_sq: float32 [2, 16, 6, 512, 512], P('section', 'dp'), may hold values from -1.06066017 to 1.06066017, as said below
- mom1_sq: float32 [2, 16, 6, 512, 512], P('section', 'dp'), may hold values from -256 to 256
- mom2_sq: float32 [2, 16, 6, 512, 512], P('section', 'dp'), may hold values from 983.04 to 8192
- master_vec: float32 [2, 16, 11, 512], P('section', 'dp'), may hold values from -0.9 to 1.75, as said below
- mom1_vec: float32 [2, 16, 11, 512], P('section', 'dp'), may hold values from -256 to 256
- mom2_vec: float32 [2, 16, 11, 512], P('section', 'dp'), may hold values from 983.04 to 8192
Outputs:
- hidden: bfloat16 [2, 32768, 512], P('section', 'dp')
- d_tokens: float32 [2, 32768, 512], P('section', 'dp')
- new_master_sq: float32 [2, 16, 6, 512, 512], P('section', 'dp')
- new_mom1_sq: float32 [2, 16, 6, 512, 512], P('section', 'dp')
- new_mom2_sq: float32 [2, 16, 6, 512, 512], P('section', 'dp')
- new_master_vec: float32 [2, 16, 11, 512], P('section', 'dp')
- new_mom1_vec: float32 [2, 16, 11, 512], P('section', 'dp')
- new_mom2_vec: float32 [2, 16, 11, 512], P('section', 'dp')
Inputs may be any that keep to these rules, and one draw needn't show every extreme that they name: `lengths`: positions from the length to 512 are padding; each row has a block of exactly 512. `owners`: the matrix units that one device owns fill at most 6 slots; in each section some device fills all 6. `master_sq`: slots that hold no unit by slot_map are not read. `master_vec`: only the owner's pack is read.
All inputs are finite; a program needn't handle non-finite values.
Results may differ from a plain program's by a relative error of at most 0.012.
Values may be sent and summed in bfloat16 or wider, within the bound.
A program may use at most 448 MiB of HBM per device.

v0:
```python
import jax
import jax.numpy as jnp
import numpy as np
from jax import lax
from jax.sharding import PartitionSpec as P

D = 512
HEADS = 8
FF = 2048
STEP = 5


highest = lax.Precision.HIGHEST
matrix_rate = 0.04
vector_rate = 0.25
matrix_decay = 0.01


def broadcast(value, axis, source):
    kept = jnp.where(lax.axis_index(axis) == source, value, 0).astype(value.dtype)
    return lax.psum(kept, axis)


def as_sent(value):

    def short(part):
        return part.astype(jnp.bfloat16) if part.dtype == jnp.float32 else part

    return jax.tree.map(short, value)


def shifted(block, axis, distance):
    devices = range(lax.axis_size(axis))
    route = [(i - distance, i) for i in devices if i - distance in devices]
    return lax.ppermute(block, axis, route)


def plain_round(value):
    return lax.optimization_barrier(value.astype(jnp.bfloat16)).astype(jnp.float32)


def value_rounder():

    def value_forward_rule(value):
        return (plain_round(value), None)

    def value_backward_rule(kept, grad):
        return (grad,)

    rounder = jax.custom_vjp(plain_round)
    rounder.defvjp(value_forward_rule, value_backward_rule)
    return rounder


def same_value(value):
    return value


def grad_rounder():

    def grad_forward_rule(value):
        return (value, None)

    def grad_backward_rule(kept, grad):
        return (plain_round(grad),)

    rounder = jax.custom_vjp(same_value)
    rounder.defvjp(grad_forward_rule, grad_backward_rule)
    return rounder


def low(value):
    return value_rounder()(value)


def low_back(value):
    return grad_rounder()(value)


def rounded(value):
    return low(low_back(value))


def dense_product(left, right):
    return jnp.dot(left, right, preferred_element_type=jnp.float32)


def normalize(value, gain, shift):
    centred = value - jnp.mean(value, axis=-1, keepdims=True)
    spread = jnp.mean(centred * centred, axis=-1, keepdims=True)
    return centred * lax.rsqrt(spread + 1e-05) * gain + shift


def attention(queries, keys_in, values_in, allowed):
    block_count, block_rows, model_width = queries.shape
    head_size = model_width // HEADS
    query_heads = queries.reshape(block_count, block_rows, HEADS, head_size)
    key_heads = keys_in.reshape(block_count, keys_in.shape[1], HEADS, head_size)
    value_heads = values_in.reshape(block_count, values_in.shape[1], HEADS, head_size)
    scores = jnp.einsum(
        "bqhd,bkhd->bhqk", query_heads, key_heads, preferred_element_type=jnp.float32
    ) * head_size ** (-0.5)
    scores = low_back(scores)
    scores = jnp.where(allowed[:, None], scores, -1000000000.0)
    row_max = jnp.max(scores, axis=-1, keepdims=True)
    exponent = jnp.exp(scores - row_max)
    softmax_weights = low(exponent / jnp.sum(exponent, axis=-1, keepdims=True))
    attended = jnp.einsum(
        "bhqk,bkhd->bqhd", softmax_weights, value_heads, preferred_element_type=jnp.float32
    )
    return rounded(attended.reshape(block_count, block_rows, model_width))


def self_branch(source, squares, allowed, block_count):
    entry_rounded = low(source)
    queries = rounded(dense_product(entry_rounded, squares[0]))
    keys_made = rounded(dense_product(entry_rounded, squares[1]))
    values_made = rounded(dense_product(entry_rounded, squares[2]))
    block_shape = (block_count, -1, source.shape[-1])
    attended = attention(
        queries.reshape(block_shape),
        keys_made.reshape(block_shape),
        values_made.reshape(block_shape),
        allowed,
    )
    return low_back(dense_product(attended.reshape(source.shape), squares[3]))


def feed_forward(source, up_matrix, down_matrix, vector):
    pre_active = low_back(dense_product(low(source), up_matrix) + vector[7:].reshape(-1))
    active = low(jax.nn.gelu(pre_active, approximate=True))
    return low_back(dense_product(active, down_matrix) + vector[6])


def encoder(source_tokens, squares, up_matrix, down_matrix, vector, allowed, block_count):
    entry_norm = normalize(source_tokens, vector[0], vector[3])
    settled = normalize(
        entry_norm + self_branch(entry_norm, squares, allowed, block_count), vector[1], vector[4]
    )
    memory = normalize(
        settled + feed_forward(settled, up_matrix, down_matrix, vector), vector[2], vector[5]
    )
    source = low(memory)
    return (
        memory,
        rounded(dense_product(source, squares[4])),
        rounded(dense_product(source, squares[5])),
    )


def decoder_lower(source_tokens, squares, vector, allowed, block_count):
    return normalize(
        source_tokens + self_branch(source_tokens, squares, allowed, block_count),
        vector[0],
        vector[3],
    )


def decoder_upper(
    lower_out, keys_in, values_in, squares, up_matrix, down_matrix, vector, allowed, block_count
):
    queries = rounded(dense_product(low(lower_out), squares[4]))
    block_shape = (block_count, -1, lower_out.shape[-1])
    attended = attention(
        queries.reshape(block_shape),
        keys_in.reshape(block_shape),
        values_in.reshape(block_shape),
        allowed,
    )
    crossed = normalize(
        lower_out + low_back(dense_product(attended.reshape(lower_out.shape), squares[5])),
        vector[1],
        vector[4],
    )
    return normalize(
        crossed + feed_forward(crossed, up_matrix, down_matrix, vector), vector[2], vector[5]
    )


def build_masks(enc_lengths, dec_lengths, block_rows):
    positions = jnp.arange(block_rows, dtype=jnp.int32)
    key_pos = positions[None, None, :]
    query_pos = positions[None, :, None]
    enc_allowed = jnp.broadcast_to(
        key_pos < enc_lengths[:, None, None], (enc_lengths.shape[0], block_rows, block_rows)
    )
    dec_allowed = (key_pos <= query_pos) & (key_pos < dec_lengths[:, None, None])
    return (enc_allowed, dec_allowed)


def unit_tables(owner_row):
    ratio_units = FF // D
    tensor_sizes = np.array([1] * 6 + [ratio_units, ratio_units], dtype=np.int32)
    tensor_of = np.repeat(np.arange(8), tensor_sizes)
    first_unit = np.concatenate([np.zeros(1, np.int32), np.cumsum(tensor_sizes)[:-1]]).astype(
        np.int32
    )
    owned_by = owner_row[:8]
    earlier = (owned_by[:, None] == owned_by[None, :]) & jnp.asarray(
        np.arange(8)[None, :] < np.arange(8)[:, None]
    )
    prior_units = jnp.sum(jnp.where(earlier, jnp.asarray(tensor_sizes)[None, :], 0), axis=1).astype(
        jnp.int32
    )
    unit_owner = owned_by[tensor_of]
    unit_slot = prior_units[tensor_of] + jnp.asarray(
        np.arange(tensor_of.shape[0]) - first_unit[tensor_of], dtype=jnp.int32
    )
    return (unit_owner, unit_slot)


def ownership(unit_owner, unit_slot, dp_index, slot_count):
    slot_ids = jnp.arange(slot_count, dtype=jnp.int32)[:, None]
    return ((unit_owner[None, :] == dp_index) & (unit_slot[None, :] == slot_ids)).astype(
        jnp.float32
    )


def split_units(unit_stack):
    ratio_units = FF // D
    squares = unit_stack[:6]
    up_matrix = unit_stack[6 : 6 + ratio_units].transpose(1, 0, 2).reshape(D, FF)
    down_matrix = unit_stack[6 + ratio_units :].reshape(FF, D)
    return (squares, up_matrix, down_matrix)


def join_units(squares, up_matrix, down_matrix):
    ratio_units = FF // D
    return jnp.concatenate(
        [
            squares,
            up_matrix.reshape(D, ratio_units, D).transpose(1, 0, 2),
            down_matrix.reshape(ratio_units, D, D),
        ],
        axis=0,
    )


def adam_update(weight, moment_old, square_old, gradient, learn_rate, decay_rate):
    moment_one = 0.5 * moment_old + 0.5 * gradient
    moment_two = 0.5 * square_old + 0.5 * gradient * gradient
    correction = 1.0 - 0.5**STEP
    adam_step = moment_one / correction / (jnp.sqrt(moment_two / correction) + 1e-08)
    return (weight - learn_rate * (adam_step + decay_rate * weight), moment_one, moment_two)


def local(
    tokens, cotangent, lengths, owners, master_sq, mom1_sq, mom2_sq, master_vec, mom1_vec, mom2_vec
):
    section_index = lax.axis_index("section")
    dp_index = lax.axis_index("dp")
    first_section = section_index == 0
    owner_row = owners[0]
    unit_owner, unit_slot = unit_tables(owner_row)
    slot_store = master_sq[0, 0]
    vec_store = master_vec[0, 0]
    unit_count = unit_owner.shape[0]
    choose = ownership(unit_owner, unit_slot, dp_index, slot_store.shape[0])

    def copy_unit(unit_index, gathered):
        piece = lax.dynamic_index_in_dim(
            slot_store, unit_slot[unit_index], 0, keepdims=False
        ).astype(jnp.bfloat16)
        piece = broadcast(piece, "dp", unit_owner[unit_index])
        return lax.dynamic_update_index_in_dim(gathered, piece, unit_index, 0)

    unit_stack = lax.fori_loop(
        0, unit_count, copy_unit, jnp.zeros((unit_count, D, D), jnp.bfloat16)
    )
    vector = broadcast(vec_store, "dp", owner_row[8])
    squares, up_matrix, down_matrix = split_units(unit_stack.astype(jnp.float32))
    block_count = lengths.shape[1]
    block_rows = tokens.shape[1] // block_count
    enc_len = lengths[0]
    dec_len = lengths[1]
    enc_allowed, dec_allowed = build_masks(enc_len, dec_len, block_rows)
    own_len = jnp.where(first_section, enc_len, dec_len)
    row_mask = (
        (jnp.arange(block_rows, dtype=jnp.int32)[None, :] < own_len[:, None])
        .astype(jnp.float32)
        .reshape(-1, 1)
    )
    own_input = tokens[0].astype(jnp.float32)
    own_ct = cotangent[0].astype(jnp.float32) * row_mask
    zero_rows = jnp.zeros(own_input.shape, jnp.float32)
    zero_half = jnp.zeros(own_input.shape, jnp.bfloat16)
    zero_grads = (
        jnp.zeros(squares.shape, jnp.float32),
        jnp.zeros(up_matrix.shape, jnp.float32),
        jnp.zeros(down_matrix.shape, jnp.float32),
        jnp.zeros(vector.shape, jnp.float32),
    )

    def encode(source, square_in, up_in, down_in, vector_in):
        return encoder(source, square_in, up_in, down_in, vector_in, enc_allowed, block_count)

    def lower_pass(source, square_in, vector_in):
        return decoder_lower(source, square_in, vector_in, dec_allowed, block_count)

    def upper_pass(lower_out, keys_in, values_in, square_in, up_in, down_in, vector_in):
        return decoder_upper(
            lower_out,
            keys_in,
            values_in,
            square_in,
            up_in,
            down_in,
            vector_in,
            enc_allowed,
            block_count,
        )

    def whole_decoder(source, keys_in, values_in, square_in, up_in, down_in, vector_in):
        return upper_pass(
            lower_pass(source, square_in, vector_in),
            keys_in,
            values_in,
            square_in,
            up_in,
            down_in,
            vector_in,
        )

    def encode_keys():
        memory, keys_made, values_made = encode(own_input, squares, up_matrix, down_matrix, vector)
        return (keys_made.astype(jnp.bfloat16), values_made.astype(jnp.bfloat16), zero_rows)

    def begin_decoder():
        return (zero_half, zero_half, zero_rows)

    cross_keys, cross_values, lower_out = lax.cond(first_section, encode_keys, begin_decoder)
    cross_keys, cross_values = (
        shifted(as_sent(cross_keys), "section", 1).astype(cross_keys.dtype),
        shifted(as_sent(cross_values), "section", 1).astype(cross_values.dtype),
    )
    keys_float = cross_keys.astype(jnp.float32)
    values_float = cross_values.astype(jnp.float32)

    def spare_encoder():
        return (zero_rows, zero_rows, zero_half, zero_half, zero_grads)

    def finish_decoder():
        output, pullback = jax.vjp(
            whole_decoder,
            own_input,
            keys_float,
            values_float,
            squares,
            up_matrix,
            down_matrix,
            vector,
        )
        input_grad, keys_grad, values_grad, square_grad, up_grad, down_grad, vector_grad = pullback(
            own_ct
        )
        return (
            output,
            input_grad,
            keys_grad.astype(jnp.bfloat16),
            values_grad.astype(jnp.bfloat16),
            (square_grad, up_grad, down_grad, vector_grad),
        )

    output, carried_grad, keys_back, values_back, late_grads = lax.cond(
        first_section, spare_encoder, finish_decoder
    )
    keys_back, values_back = (
        shifted(as_sent(keys_back), "section", -1).astype(keys_back.dtype),
        shifted(as_sent(values_back), "section", -1).astype(values_back.dtype),
    )

    def back_encoder():
        primal, pullback = jax.vjp(encode, own_input, squares, up_matrix, down_matrix, vector)
        input_grad, square_grad, up_grad, down_grad, vector_grad = pullback(
            (own_ct, keys_back.astype(jnp.float32), values_back.astype(jnp.float32))
        )
        return (primal[0], input_grad, (square_grad, up_grad, down_grad, vector_grad))

    def back_decoder():
        return (zero_rows, carried_grad, zero_grads)

    memory, input_grad, early_grads = lax.cond(first_section, back_encoder, back_decoder)
    hidden = (memory + output).astype(jnp.bfloat16)
    gradients = jax.tree.map(
        lambda early_part, late_part: early_part + late_part, early_grads, late_grads
    )
    square_grad, up_grad, down_grad, vector_grad = gradients
    grad_units = join_units(square_grad, up_grad, down_grad)
    total_units, total_vector = lax.psum((grad_units, vector_grad), "dp")
    is_taken = jnp.sum(choose, axis=1)[:, None, None] > 0.5
    grad_slots = jnp.einsum("cu,uxy->cxy", choose, total_units, precision=highest)
    updated = adam_update(
        slot_store, mom1_sq[0, 0], mom2_sq[0, 0], grad_slots, matrix_rate, matrix_decay
    )
    slot_results = [
        jnp.where(is_taken, fresh_value, stale_value)[None, None]
        for fresh_value, stale_value in zip(updated, (slot_store, mom1_sq[0, 0], mom2_sq[0, 0]))
    ]
    owns_vector = owner_row[8] == dp_index
    vector_new = adam_update(
        vec_store, mom1_vec[0, 0], mom2_vec[0, 0], total_vector, vector_rate, 0.0
    )
    vector_results = [
        jnp.where(owns_vector, fresh_value, stale_value)[None, None]
        for fresh_value, stale_value in zip(vector_new, (vec_store, mom1_vec[0, 0], mom2_vec[0, 0]))
    ]
    return (
        hidden[None],
        input_grad[None],
        slot_results[0],
        slot_results[1],
        slot_results[2],
        vector_results[0],
        vector_results[1],
        vector_results[2],
    )


def solution(mesh):
    return jax.shard_map(
        local,
        mesh=mesh,
        in_specs=(
            P("section", "dp", None),
            P("section", "dp", None),
            P(None, "dp"),
            P("section", None),
            P("section", "dp", None, None, None),
            P("section", "dp", None, None, None),
            P("section", "dp", None, None, None),
            P("section", "dp", None, None),
            P("section", "dp", None, None),
            P("section", "dp", None, None),
        ),
        out_specs=(
            P("section", "dp", None),
            P("section", "dp", None),
            P("section", "dp", None, None, None),
            P("section", "dp", None, None, None),
            P("section", "dp", None, None, None),
            P("section", "dp", None, None),
            P("section", "dp", None, None),
            P("section", "dp", None, None),
        ),
        check_vma=False,
    )
```

profile of v0, /device:TPU:1, one launch (start us, length us, event | category | flops | bytes accessed | tf_op | source)
XLA Modules:
  0.0 3181.6 jit_solution(9666773715744531533)
XLA Ops:
  16.0 1368.2 %while.15 = (s32[]{:T(128)}, bf16[14,512,512]{2,1,0:T(8,128)(2,1)}, s32[14]{0:T(128)S(1)}, s32[14]{0:T(128)S(1)}, bf16[6,512,512]{2,1,0:T(8,128)(2,1)S(1)}, /*index=5*/s32[]{:T(128)}, s32[]{:T(128)}, s32[]{:T(128)}, u32[]{:T(128)}) while((s32[]{:T(128)}, bf16[14,512,512]{2,1,0:T(8,128)(2,1)}, s32[14]{0:T(128)S(1)}, s32[14]{0:T(128)S(1)}, ...), condition=%wide.region_3.4_spmd, body=%wide.region_1.3_spmd.sunk | while | flops 524296 | bytes 5243117 | solution.py:267
  20.7 93.4 %all-reduce.33.cloned.1.call-done = bf16[1,512,512]{2,1,0:T(8,128)(2,1)} async-done(((bf16[1,512,512]{2,1,0:T(8,128)(2,1)}), bf16[1,512,512]{2,1,0:T(8,128)(2,1)}) %all-reduce.33.cloned.1.call-update) | async-done | bytes 524304 | tf_op jit(solution)/shard_map/while/body/eval_jaxpr/psum | solution.py:21
  120.5 91.2 %all-reduce.33.cloned.1.call-done = bf16[1,512,512]{2,1,0:T(8,128)(2,1)} async-done(((bf16[1,512,512]{2,1,0:T(8,128)(2,1)}), bf16[1,512,512]{2,1,0:T(8,128)(2,1)}) %all-reduce.33.cloned.1.call-update) | async-done | bytes 524304 | tf_op jit(solution)/shard_map/while/body/eval_jaxpr/psum | solution.py:21
  218.2 91.2 %all-reduce.33.cloned.1.call-done = bf16[1,512,512]{2,1,0:T(8,128)(2,1)} async-done(((bf16[1,512,512]{2,1,0:T(8,128)(2,1)}), bf16[1,512,512]{2,1,0:T(8,128)(2,1)}) %all-reduce.33.cloned.1.call-update) | async-done | bytes 524304 | tf_op jit(solution)/shard_map/while/body/eval_jaxpr/psum | solution.py:21
  315.9 90.9 %all-reduce.33.cloned.1.call-done = bf16[1,512,512]{2,1,0:T(8,128)(2,1)} async-done(((bf16[1,512,512]{2,1,0:T(8,128)(2,1)}), bf16[1,512,512]{2,1,0:T(8,128)(2,1)}) %all-reduce.33.cloned.1.call-update) | async-done | bytes 524304 | tf_op jit(solution)/shard_map/while/body/eval_jaxpr/psum | solution.py:21
  413.3 90.9 %all-reduce.33.cloned.1.call-done = bf16[1,512,512]{2,1,0:T(8,128)(2,1)} async-done(((bf16[1,512,512]{2,1,0:T(8,128)(2,1)}), bf16[1,512,512]{2,1,0:T(8,128)(2,1)}) %all-reduce.33.cloned.1.call-update) | async-done | bytes 524304 | tf_op jit(solution)/shard_map/while/body/eval_jaxpr/psum | solution.py:21
  510.7 90.9 %all-reduce.33.cloned.1.call-done = bf16[1,512,512]{2,1,0:T(8,128)(2,1)} async-done(((bf16[1,512,512]{2,1,0:T(8,128)(2,1)}), bf16[1,512,512]{2,1,0:T(8,128)(2,1)}) %all-reduce.33.cloned.1.call-update) | async-done | bytes 524304 | tf_op jit(solution)/shard_map/while/body/eval_jaxpr/psum | solution.py:21
  608.1 91.2 %all-reduce.33.cloned.1.call-done = bf16[1,512,512]{2,1,0:T(8,128)(2,1)} async-done(((bf16[1,512,512]{2,1,0:T(8,128)(2,1)}), bf16[1,512,512]{2,1,0:T(8,128)(2,1)}) %all-reduce.33.cloned.1.call-update) | async-done | bytes 524304 | tf_op jit(solution)/shard_map/while/body/eval_jaxpr/psum | solution.py:21
  705.8 91.2 %all-reduce.33.cloned.1.call-done = bf16[1,512,512]{2,1,0:T(8,128)(2,1)} async-done(((bf16[1,512,512]{2,1,0:T(8,128)(2,1)}), bf16[1,512,512]{2,1,0:T(8,128)(2,1)}) %all-reduce.33.cloned.1.call-update) | async-done | bytes 524304 | tf_op jit(solution)/shard_map/while/body/eval_jaxpr/psum | solution.py:21
  803.5 91.2 %all-reduce.33.cloned.1.call-done = bf16[1,512,512]{2,1,0:T(8,128)(2,1)} async-done(((bf16[1,512,512]{2,1,0:T(8,128)(2,1)}), bf16[1,512,512]{2,1,0:T(8,128)(2,1)}) %all-reduce.33.cloned.1.call-update) | async-done | bytes 524304 | tf_op jit(solution)/shard_map/while/body/eval_jaxpr/psum | solution.py:21
  901.2 90.9 %all-reduce.33.cloned.1.call-done = bf16[1,512,512]{2,1,0:T(8,128)(2,1)} async-done(((bf16[1,512,512]{2,1,0:T(8,128)(2,1)}), bf16[1,512,512]{2,1,0:T(8,128)(2,1)}) %all-reduce.33.cloned.1.call-update) | async-done | bytes 524304 | tf_op jit(solution)/shard_map/while/body/eval_jaxpr/psum | solution.py:21
  998.6 91.2 %all-reduce.33.cloned.1.call-done = bf16[1,512,512]{2,1,0:T(8,128)(2,1)} async-done(((bf16[1,512,512]{2,1,0:T(8,128)(2,1)}), bf16[1,512,512]{2,1,0:T(8,128)(2,1)}) %all-reduce.33.cloned.1.call-update) | async-done | bytes 524304 | tf_op jit(solution)/shard_map/while/body/eval_jaxpr/psum | solution.py:21
  1096.3 90.9 %all-reduce.33.cloned.1.call-done = bf16[1,512,512]{2,1,0:T(8,128)(2,1)} async-done(((bf16[1,512,512]{2,1,0:T(8,128)(2,1)}), bf16[1,512,512]{2,1,0:T(8,128)(2,1)}) %all-reduce.33.cloned.1.call-update) | async-done | bytes 524304 | tf_op jit(solution)/shard_map/while/body/eval_jaxpr/psum | solution.py:21
  1193.7 91.2 %all-reduce.33.cloned.1.call-done = bf16[1,512,512]{2,1,0:T(8,128)(2,1)} async-done(((bf16[1,512,512]{2,1,0:T(8,128)(2,1)}), bf16[1,512,512]{2,1,0:T(8,128)(2,1)}) %all-reduce.33.cloned.1.call-update) | async-done | bytes 524304 | tf_op jit(solution)/shard_map/while/body/eval_jaxpr/psum | solution.py:21
  1291.4 90.9 %all-reduce.33.cloned.1.call-done = bf16[1,512,512]{2,1,0:T(8,128)(2,1)} async-done(((bf16[1,512,512]{2,1,0:T(8,128)(2,1)}), bf16[1,512,512]{2,1,0:T(8,128)(2,1)}) %all-reduce.33.cloned.1.call-update) | async-done | bytes 524304 | tf_op jit(solution)/shard_map/while/body/eval_jaxpr/psum | solution.py:21
  1392.7 55.0 %psum.35 = f32[11,512]{1,0:T(8,128)S(1)} all-reduce(f32[11,512]{1,0:T(8,128)S(1)} %bitcast_select_fusion.4), channel_id=1, replica_groups=mesh['section'=2,'dp'=16] {'dp'}, use_global_device_ids=true, to_apply=%region_4.5 | all-reduce | flops 5632 | bytes 45056 | tf_op jit(solution)/shard_map/psum | solution.py:21
  1457.5 158.0 %conditional.3 = (bf16[2048,512]{1,0:T(8,128)(2,1)}, bf16[2048,512]{1,0:T(8,128)(2,1)}) conditional(s32[]{:T(128)} %convert_element_type.386, () %tuple.63, (f32[2048,512]{0,1:T(8,128)}, f32[11,512]{1,0:T(8,128)S(1)}, bf16[6,512,512]{2,1,0:T(8,128)(2,1)S(1)}, pred[4,1,512]{2,0,1:T(4,128)(4,1)S(1)}, bf16[512,2048]{1,0:T(8,128)(2,1)}, ...), branch_computations={%region_5.6_spmd, %region_6.15_spmd} | conditional | flops 17329821696 | bytes 353849536 | solution.py:331
  1493.7 19.1 fusion.14
  1512.7 37.9 %fusion.184 = (f32[4,8,512]{2,1,0:T(8,128)S(1)}, f32[4,8,512,512]{2,3,1,0:T(8,128)}) fusion(f32[4,8,512,512]{2,3,1,0:T(8,128)} %fusion.14, pred[4,512]{1,0:T(4,128)(4,1)S(1)} %bitcast.537), kind=kOutput, calls=%fused_computation.387 | output fusion | flops 50332160 | bytes 67176448 | tf_op jit(solution)/shard_map/cond/branch_1_fun/sub | solution.py:106
  1636.8 24.5 collective-permute-done.1
  1661.3 44.9 %collective-permute-done = bf16[2048,512]{0,1:T(8,128)(2,1)} collective-permute-done((bf16[2048,512]{0,1:T(8,128)(2,1)}, bf16[2048,512]{0,1:T(8,128)(2,1)}, u32[]{:S(2)}, u32[]{:S(2)}) %collective-permute-start) | collective-permute-done | bytes 2097184 | tf_op jit(solution)/shard_map/ppermute | solution.py:35
  1706.4 20.2 conditional.4
  1739.2 633.4 %collective-permute-done.3 = bf16[2048,512]{1,0:T(8,128)(2,1)} collective-permute-done((bf16[2048,512]{1,0:T(8,128)(2,1)}, bf16[2048,512]{1,0:T(8,128)(2,1)}, u32[]{:S(2)}, u32[]{:S(2)}) %collective-permute-start.3) | collective-permute-done | bytes 2097184 | tf_op jit(solution)/shard_map/ppermute | solution.py:35
  2372.6 44.9 %collective-permute-done.2 = bf16[2048,512]{1,0:T(8,128)(2,1)} collective-permute-done((bf16[2048,512]{1,0:T(8,128)(2,1)}, bf16[2048,512]{1,0:T(8,128)(2,1)}, u32[]{:S(2)}, u32[]{:S(2)}) %collective-permute-start.2) | collective-permute-done | bytes 2097184 | tf_op jit(solution)/shard_map/ppermute | solution.py:35
  2417.5 394.1 %conditional.5 = (f32[2048,512]{0,1:T(8,128)}, f32[2048,512]{0,1:T(8,128)}, f32[6,512,512]{2,1,0:T(8,128)}, f32[2048,512]{1,0:T(8,128)}, f32[11,512]{1,0:T(8,128)}, /*index=5*/f32[512,2048]{0,1:T(8,128)}) conditional(s32[]{:T(128)} %convert_element_type.386, f32[2048,512]{0,1:T(8,128)} %copy-done.28, (f32[2048,512]{0,1:T(8,128)}, ...), branch_computations={%region_47.48_spmd, %region_48.74_spmd} | conditional | flops 49952669696 | bytes 1303195904 | solution.py:382
  2593.1 19.9 fusion.117
  2690.9 25.4 multiply_reduce_fusion.14
  2716.3 33.0 %fusion.179 = (f32[4,8,512]{2,1,0:T(8,128)S(1)}, f32[4,8,512,512]{2,3,1,0:T(8,128)}) fusion(f32[4,8,512]{2,1,0:T(8,128)S(1)} %copy-done.76, f32[4,8,512,512]{2,3,1,0:T(8,128)} %get-tuple-element.511, pred[4,512]{1,0:T(4,128)(4,1)S(1)} %bitcast.548, f32[4,8,512]{2,1,0:T(8,128)S(1)} %neg.42, f32[4,8,512,512]{2,3,1,0:T(8,128)} %get-tuple-element.521, ...), kind=kLoop, calls=%fused_computation.383 | loop fusion | flops 58703872 | bytes 100927488 | tf_op jit(solution)/shard_map/cond/branch_1_fun/transpose(jvp())/reduce_sum | solution.py:106
  2749.3 21.1 select_convert_fusion.2
  2846.8 67.6 %psum.37 = f32[11,512]{1,0:T(8,128)S(1)} all-reduce(f32[11,512]{1,0:T(8,128)S(1)} %add.444), channel_id=1, replica_groups=mesh['section'=2,'dp'=16] {'dp'}, use_global_device_ids=true, to_apply=%region_76.77 | all-reduce | flops 5632 | bytes 45056 | tf_op jit(solution)/shard_map/psum | solution.py:389
  2927.4 184.2 %all-reduce.31.cloned.1.call-done = f32[14,512,512]{2,1,0:T(8,128)} async-done(((f32[14,512,512]{2,1,0:T(8,128)}), f32[14,512,512]{2,1,0:T(8,128)}) %all-reduce.31.cloned.1.call-update) | async-done | bytes 14680080 | tf_op jit(solution)/shard_map/psum | solution.py:389
  3111.5 40.1 %fusion.157 = (f32[1,1,6,512,512]{4,2,3,1,0:T(8,128)}, f32[1,1,6,512,512]{4,2,3,1,0:T(8,128)}, f32[1,1,6,512,512]{4,2,3,1,0:T(8,128)S(1)}) fusion(f32[1,1,6,512,512]{4,3,2,1,0:T(8,128)} %param.30, pred[6]{0:T(512)(128)(4,1)S(1)} %broadcast_compare_fusion, f32[1,1,6,512,512]{4,3,2,1,0:T(8,128)} %param.29, f32[1,1,6,512,512]{4,3,2,1,0:T(8,128)} %param.28, ...), kind=kOutput, calls=%fused_computation.336 | convolution fusion | flops 290980000 | bytes 52428876 | tf_op jit(solution)/shard_map/cu,uxy->cxy/dot_general | solution.py:391
  (402 shorter events, 593.3 us)
Async XLA Ops:
  16.0 98.0 %all-reduce.33.cloned.1.call-start = ((), (), s32[]{:S(2)}) async-start(), calls=%async_computation.1 | async-start | bytes 1048576 | tf_op jit(solution)/shard_map/while/body/eval_jaxpr/psum | solution.py:21
  115.9 95.8 %all-reduce.33.cloned.1.call-start = ((), (), s32[]{:S(2)}) async-start(), calls=%async_computation.1 | async-start | bytes 1048576 | tf_op jit(solution)/shard_map/while/body/eval_jaxpr/psum | solution.py:21
  213.6 95.8 %all-reduce.33.cloned.1.call-start = ((), (), s32[]{:S(2)}) async-start(), calls=%async_computation.1 | async-start | bytes 1048576 | tf_op jit(solution)/shard_map/while/body/eval_jaxpr/psum | solution.py:21
  311.3 95.5 %all-reduce.33.cloned.1.call-start = ((), (), s32[]{:S(2)}) async-start(), calls=%async_computation.1 | async-start | bytes 1048576 | tf_op jit(solution)/shard_map/while/body/eval_jaxpr/psum | solution.py:21
  408.7 95.5 %all-reduce.33.cloned.1.call-start = ((), (), s32[]{:S(2)}) async-start(), calls=%async_computation.1 | async-start | bytes 1048576 | tf_op jit(solution)/shard_map/while/body/eval_jaxpr/psum | solution.py:21
  506.1 95.5 %all-reduce.33.cloned.1.call-start = ((), (), s32[]{:S(2)}) async-start(), calls=%async_computation.1 | async-start | bytes 1048576 | tf_op jit(solution)/shard_map/while/body/eval_jaxpr/psum | solution.py:21
  603.5 95.8 %all-reduce.33.cloned.1.call-start = ((), (), s32[]{:S(2)}) async-start(), calls=%async_computation.1 | async-start | bytes 1048576 | tf_op jit(solution)/shard_map/while/body/eval_jaxpr/psum | solution.py:21
  701.2 95.8 %all-reduce.33.cloned.1.call-start = ((), (), s32[]{:S(2)}) async-start(), calls=%async_computation.1 | async-start | bytes 1048576 | tf_op jit(solution)/shard_map/while/body/eval_jaxpr/psum | solution.py:21
  798.9 95.8 %all-reduce.33.cloned.1.call-start = ((), (), s32[]{:S(2)}) async-start(), calls=%async_computation.1 | async-start | bytes 1048576 | tf_op jit(solution)/shard_map/while/body/eval_jaxpr/psum | solution.py:21
  896.6 95.5 %all-reduce.33.cloned.1.call-start = ((), (), s32[]{:S(2)}) async-start(), calls=%async_computation.1 | async-start | bytes 1048576 | tf_op jit(solution)/shard_map/while/body/eval_jaxpr/psum | solution.py:21
  994.0 95.8 %all-reduce.33.cloned.1.call-start = ((), (), s32[]{:S(2)}) async-start(), calls=%async_computation.1 | async-start | bytes 1048576 | tf_op jit(solution)/shard_map/while/body/eval_jaxpr/psum | solution.py:21
  1091.7 95.5 %all-reduce.33.cloned.1.call-start = ((), (), s32[]{:S(2)}) async-start(), calls=%async_computation.1 | async-start | bytes 1048576 | tf_op jit(solution)/shard_map/while/body/eval_jaxpr/psum | solution.py:21
  1189.1 95.8 %all-reduce.33.cloned.1.call-start = ((), (), s32[]{:S(2)}) async-start(), calls=%async_computation.1 | async-start | bytes 1048576 | tf_op jit(solution)/shard_map/while/body/eval_jaxpr/psum | solution.py:21
  1286.8 95.5 %all-reduce.33.cloned.1.call-start = ((), (), s32[]{:S(2)}) async-start(), calls=%async_computation.1 | async-start | bytes 1048576 | tf_op jit(solution)/shard_map/while/body/eval_jaxpr/psum | solution.py:21
  1384.2 1727.4 %all-reduce.31.cloned.1.call-start = ((), (), s32[]{:S(2)}) async-start(), calls=%async_computation | async-start | bytes 29360128 | tf_op jit(solution)/shard_map/psum | solution.py:389
  1386.3 320.1 %copy-start.19 = (bf16[6,512,512]{2,1,0:T(8,128)(2,1)}, bf16[6,512,512]{2,1,0:T(8,128)(2,1)S(1)}, u32[]{:S(2)}) copy-start(bf16[6,512,512]{2,1,0:T(8,128)(2,1)S(1)} %slice.161) | copy-start | bytes 9437188
  1447.7 258.8 %copy-start.95 = (f32[11,512]{1,0:T(8,128)}, f32[11,512]{1,0:T(8,128)S(1)}, u32[]{:S(2)}) copy-start(f32[11,512]{1,0:T(8,128)S(1)} %psum.35) | copy-start | bytes 67588
  1619.5 41.8 %collective-permute-start.1 = (bf16[2048,512]{0,1:T(8,128)(2,1)}, bf16[2048,512]{0,1:T(8,128)(2,1)}, u32[]{:S(2)}, u32[]{:S(2)}) collective-permute-start(bf16[2048,512]{0,1:T(8,128)(2,1)} %copy.474), channel_id=1, source_target_pairs={{0,16},{1,17},{2,18},{3,19},{4,20},{5,21},{6,22},{7,23},{8,24},{9,... | collective-permute-start | bytes 6291464 | tf_op jit(solution)/shard_map/ppermute | solution.py:35
  1626.0 80.2 %collective-permute-start = (bf16[2048,512]{0,1:T(8,128)(2,1)}, bf16[2048,512]{0,1:T(8,128)(2,1)}, u32[]{:S(2)}, u32[]{:S(2)}) collective-permute-start(bf16[2048,512]{0,1:T(8,128)(2,1)} %copy.473), channel_id=1, source_target_pairs={{0,16},{1,17},{2,18},{3,19},{4,20},{5,21},{6,22},{7,23},{8,24},{9,... | collective-permute-start | bytes 6291464 | tf_op jit(solution)/shard_map/ppermute | solution.py:35
  1728.6 688.9 %copy-start.20 = (bf16[6,512,512]{2,1,0:T(8,128)(2,1)S(1)}, bf16[6,512,512]{2,1,0:T(8,128)(2,1)}, u32[]{:S(2)}) copy-start(bf16[6,512,512]{2,1,0:T(8,128)(2,1)} %copy-done.19) | copy-start | bytes 9437188
  1728.6 688.9 %copy-start.96 = (f32[11,512]{1,0:T(8,128)S(1)}, f32[11,512]{1,0:T(8,128)}, u32[]{:S(2)}) copy-start(f32[11,512]{1,0:T(8,128)} %copy-done.95) | copy-start | bytes 67588
  1736.6 636.0 %collective-permute-start.3 = (bf16[2048,512]{1,0:T(8,128)(2,1)}, bf16[2048,512]{1,0:T(8,128)(2,1)}, u32[]{:S(2)}, u32[]{:S(2)}) collective-permute-start(bf16[2048,512]{1,0:T(8,128)(2,1)} %copy.477), channel_id=1, source_target_pairs={{16,0},{17,1},{18,2},{19,3},{20,4},{21,5},{22,6},{23,7},{24,8},{25... | collective-permute-start | bytes 6291464 | tf_op jit(solution)/shard_map/ppermute | solution.py:35
  1737.9 679.6 %collective-permute-start.2 = (bf16[2048,512]{1,0:T(8,128)(2,1)}, bf16[2048,512]{1,0:T(8,128)(2,1)}, u32[]{:S(2)}, u32[]{:S(2)}) collective-permute-start(bf16[2048,512]{1,0:T(8,128)(2,1)} %copy.476), channel_id=1, source_target_pairs={{16,0},{17,1},{18,2},{19,3},{20,4},{21,5},{22,6},{23,7},{24,8},{25... | collective-permute-start | bytes 6291464 | tf_op jit(solution)/shard_map/ppermute | solution.py:35
  2417.5 90.3 %copy-start.79 = (pred[4,1,512]{2,0,1:T(4,128)(4,1)}, pred[4,1,512]{2,0,1:T(4,128)(4,1)S(1)}, u32[]{:S(2)}) copy-start(pred[4,1,512]{2,0,1:T(4,128)(4,1)S(1)} %get-tuple-element.220) | copy-start | bytes 6148 | tf_op jit(solution)/shard_map/cond
  2418.2 126.1 %copy-start.119 = (f32[1,512]{1,0:T(1,128)}, f32[1,512]{1,0:T(1,128)S(1)}, u32[]{:S(2)}) copy-start(f32[1,512]{1,0:T(1,128)S(1)} %get-tuple-element.509) | copy-start | bytes 6148 | tf_op jit(solution)/shard_map/cond
  2420.6 123.6 %copy-start.97 = (f32[2048]{0:T(1024)}, f32[2048]{0:T(1024)S(1)}, u32[]{:S(2)}) copy-start(f32[2048]{0:T(1024)S(1)} %broadcast_multiply_fusion.8) | copy-start | bytes 24580 | tf_op jit(solution)/shard_map/cond
  2424.0 120.2 %copy-start.111 = (f32[2048]{0:T(1024)}, f32[2048]{0:T(1024)S(1)}, u32[]{:S(2)}) copy-start(f32[2048]{0:T(1024)S(1)} %fusion.147) | copy-start | bytes 24580 | tf_op jit(solution)/shard_map/cond
  2690.9 25.4 copy-start.92
  2716.3 33.0 %copy-start.99 = (f32[4,8,512]{2,1,0:T(8,128)S(1)}, f32[4,8,512]{2,1,0:T(8,128)}, u32[]{:S(2)}) copy-start(f32[4,8,512]{2,1,0:T(8,128)} %get-tuple-element.453) | copy-start | bytes 196612 | tf_op jit(solution)/shard_map/cond
  2840.6 73.8 %copy-start.114 = (f32[1,1,11,512]{3,1,2,0:T(1,128)S(1)}, f32[1,1,11,512]{3,1,2,0:T(1,128)}, u32[]{:S(2)}) copy-start(f32[1,1,11,512]{3,1,2,0:T(1,128)} %param.31) | copy-start | bytes 67588
  2840.7 73.8 %copy-start.123 = (f32[1,1,11,512]{3,1,2,0:T(1,128)S(1)}, f32[1,1,11,512]{3,1,2,0:T(1,128)}, u32[]{:S(2)}) copy-start(f32[1,1,11,512]{3,1,2,0:T(1,128)} %param.33) | copy-start | bytes 67588
  2840.7 73.8 %copy-start.124 = (f32[1,1,11,512]{3,1,2,0:T(1,128)S(1)}, f32[1,1,11,512]{3,1,2,0:T(1,128)}, u32[]{:S(2)}) copy-start(f32[1,1,11,512]{3,1,2,0:T(1,128)} %param.32) | copy-start | bytes 67588
  (61 other events, 353.1 us)
Sparse Core Ops, SparseCore 0:
  21.2 92.7 all-reduce.32
  121.1 90.5 all-reduce.32
  218.8 90.5 all-reduce.32
  316.2 90.5 all-reduce.32
  413.6 90.5 all-reduce.32
  511.0 90.5 all-reduce.32
  608.7 90.5 all-reduce.32
  706.4 90.5 all-reduce.32
  804.1 90.5 all-reduce.32
  901.4 90.5 all-reduce.32
  999.1 90.5 all-reduce.32
  1096.5 90.5 all-reduce.32
  1194.2 90.5 all-reduce.32
  1291.6 90.5 all-reduce.32
Sparse Core Ops, SparseCore 1:
  2839.9 271.5 all-reduce.30
where the time goes:
time: 3190 us; the launch traced here: 3180 us
  waiting for transfers between devices  2210 us (69%)
  matrix products  310 us (10%)
  other arithmetic  239 us (7%)
  local copies, waits for them, and re-layouts  232 us (7%)
  blocking collectives  123 us (4%)
  loops' own time  43.4 us (1%)
    psum x14, waiting for transfers between devices, broadcast(): return lax.psum(kept, axis)  1280 us
    ppermute x4, waiting for transfers between devices, shifted(): return lax.ppermute(block, axis, route)  748 us
    psum x1, waiting for transfers between devices, local(): total_units, total_vector = lax.psum((grad_units, vector_grad), 'dp')  184 us
    dot_general x29, matrix products, dense_product(): return jnp.dot(left, right, preferred_element_type=jnp.float32)  148 us
    psum x1, blocking collectives, local(): total_units, total_vector = lax.psum((grad_units, vector_grad), 'dp')  67.6 us
  transfers between devices with their start and end apart: 19, of which 19 were waited for; matrix products, arithmetic and copies ran while one was open for 1% of the time, Pallas kernels for 0%

commit v1 on v0

v1 whole, which is shorter than its diff:
```python
import functools
import jax
import jax.numpy as jnp
import numpy as np
from jax import lax
from jax.experimental import pallas as pl
from jax.experimental.pallas import tpu as pltpu
from jax.sharding import PartitionSpec as P

D = 512
HEADS = 8
HS = D // HEADS
FF = 2048
RU = FF // D
STEP = 5
LANES = 128
F32 = jnp.float32
BF = jnp.bfloat16
NEG = -1e30


def nn(a, b):
    return jnp.dot(a, b, preferred_element_type=F32)


def nt(a, b):
    return lax.dot_general(a, b, (((1,), (1,)), ((), ())), preferred_element_type=F32)


def tn(a, b):
    return lax.dot_general(a, b, (((0,), (0,)), ((), ())), preferred_element_type=F32)


def lane_loop(count, body):
    def step(i, carry):
        body(pl.ds(pl.multiple_of(i * LANES, LANES), LANES))
        return carry

    lax.fori_loop(0, count // LANES, step, 0)


def norm_parts(value):
    mean = jnp.mean(value, axis=0, keepdims=True)
    centred = value - mean
    inv = lax.rsqrt(jnp.mean(centred * centred, axis=0, keepdims=True) + 1e-05)
    return centred * inv, inv


def norm_grad(grad, normed, inv, gain):
    scaled = grad * gain
    mean_one = jnp.mean(scaled, axis=0, keepdims=True)
    mean_two = jnp.mean(scaled * normed, axis=0, keepdims=True)
    return (scaled - mean_one - normed * mean_two) * inv


def fill_bias(bias, length, causal):
    rows = bias.shape[0]

    def body(lanes):
        key = lax.broadcasted_iota(jnp.int32, (rows, LANES), 0)
        query = lax.broadcasted_iota(jnp.int32, (rows, LANES), 1) + lanes.start
        allowed = key < length
        if causal is not None:
            allowed = allowed & ((key <= query) | jnp.logical_not(causal))
        bias[:, lanes] = jnp.where(allowed, 0.0, NEG)

    lane_loop(bias.shape[1], body)


def head_rows(h):
    return pl.ds(pl.multiple_of(h * HS, HS), HS)


def attend(qt, kt, vt, bias, ot, lse, pair):
    def score(h, out):
        rows = head_rows(h)
        out[...] = tn(kt[rows, :], qt[rows, :] * BF(0.125))

    def finish(h, scores):
        rows = head_rows(h)
        biased = scores[...] + bias[...]
        top = jnp.max(biased, axis=0, keepdims=True)
        weights = jnp.exp(biased - top).astype(BF)
        values = jnp.concatenate([vt[rows, :], jnp.ones((16, vt.shape[1]), BF)], axis=0)
        out = nn(values, weights)
        total = out[HS : HS + 1]
        ot[rows, :] = (out[:HS] * (1.0 / total)).astype(BF)
        lse[pl.ds(h, 1), :] = top + jnp.log(total)

    one, two = pair.at[0], pair.at[1]
    score(0, one)

    def body(i, carry):
        score(2 * i + 1, two)
        finish(2 * i, one)
        score(jnp.minimum(2 * i + 2, HEADS - 1), one)
        finish(2 * i + 1, two)
        return carry

    lax.fori_loop(0, HEADS // 2, body, 0, unroll=True)


def attend_back(qt, kt, vt, bias, ot, lse, dot, dqt, dkt, dvt):
    def head(h, carry):
        rows = head_rows(h)
        keys, grads = kt[rows, :], dot[rows, :]
        queries = qt[rows, :] * BF(0.125)
        delta = jnp.sum(grads.astype(F32) * ot[rows, :].astype(F32), axis=0, keepdims=True)
        probs = jnp.exp(tn(keys, queries) + bias[...] - lse[pl.ds(h, 1), :])
        dscores = (probs * (tn(vt[rows, :], grads) - delta)).astype(BF)
        dvt[rows, :] = nt(grads, probs.astype(BF)).astype(BF)
        dkt[rows, :] = nt(queries, dscores).astype(BF)
        dqt[rows, :] = (nn(keys, dscores) * 0.125).astype(BF)
        return carry

    lax.fori_loop(0, HEADS, head, 0, unroll=4)


def self_forward(x, sq, vec, causal, length, ut, n0, r0, qt, kt, vt, ot, lse, n1, r1, y, bias, et, pair):
    first = jnp.logical_not(causal)
    tokens = x.shape[0]
    et[...] = x[...].astype(F32).T

    def entry(lanes):
        value = et[:, lanes]
        normed, inv = norm_parts(value)
        n0[:, lanes] = normed.astype(BF)
        r0[:, lanes] = inv
        value = jnp.where(first, normed * vec[:, 0:1] + vec[:, 1:2], value)
        et[:, lanes] = value
        ut[:, lanes] = value.astype(BF)

    lane_loop(tokens, entry)
    fill_bias(bias, length, causal)
    for index, out in enumerate((qt, kt, vt)):
        out[...] = tn(sq[index][...], ut[...]).astype(BF)
    attend(qt, kt, vt, bias, ot, lse, pair)
    et[...] += tn(sq[3][...], ot[...])

    def leave(lanes):
        normed, inv = norm_parts(et[:, lanes])
        n1[:, lanes] = normed.astype(BF)
        r1[:, lanes] = inv
        y[:, lanes] = normed * vec[:, 2:3] + vec[:, 3:4]

    lane_loop(tokens, leave)


def self_backward(dy, sq, vec, causal, length, ut, n0, r0, qt, kt, vt, ot, lse, n1, r1, dx, bias, dsa, dot, dqt, dkt, dvt, dsq, dvec, vacc):
    first = jnp.logical_not(causal)
    tokens = dy.shape[1]
    vacc[...] = jnp.zeros(vacc.shape, F32)

    def leave(lanes):
        grad, normed = dy[:, lanes], n1[:, lanes].astype(F32)
        vacc[2] += grad * normed
        vacc[3] += grad
        grad = norm_grad(grad, normed, r1[:, lanes], vec[:, 2:3])
        dy[:, lanes] = grad
        dsa[:, lanes] = grad.astype(BF)

    lane_loop(tokens, leave)
    fill_bias(bias, length, causal)
    dot[...] = nn(sq[3][...], dsa[...]).astype(BF)
    dsq[3] += nt(ot[...], dsa[...])
    attend_back(qt, kt, vt, bias, ot, lse, dot, dqt, dkt, dvt)
    for index, grad in enumerate((dqt, dkt, dvt)):
        dsq[index] += nt(ut[...], grad[...])
        dy[...] += nn(sq[index][...], grad[...])

    def entry(lanes):
        grad, normed = dy[:, lanes], n0[:, lanes].astype(F32)
        vacc[0] += grad * normed
        vacc[1] += grad
        dy[:, lanes] = jnp.where(first, norm_grad(grad, normed, r0[:, lanes], vec[:, 0:1]), grad)

    lane_loop(tokens, entry)
    dx[...] = dy[...].T
    for index in range(4):
        dvec[:, index : index + 1] += jnp.sum(vacc[index], axis=1, keepdims=True)


def gelu_parts(z):
    root = 0.7978845608028654
    square = z * z
    t = jnp.tanh(z * (root + (root * 0.044715) * square))
    half = 0.5 + 0.5 * t
    act = z * half
    slope = half + act * (1.0 - t) * (root + (3.0 * root * 0.044715) * square)
    return act, slope


def feed_forward(h, units, vec, hb, act, slope, n2, r2, out):
    hb[...] = h[...].astype(BF)
    for c in range(RU):
        rows = slice(c * D, (c + 1) * D)
        a, s = gelu_parts(tn(units[c][...], hb[...]) + vec[:, c : c + 1])
        act[rows, :] = a.astype(BF)
        slope[rows, :] = s.astype(BF)
    for c in range(RU):
        rows = slice(c * D, (c + 1) * D)
        h[...] += tn(units[RU + c][...], act[rows, :])

    def leave(lanes):
        normed, inv = norm_parts(h[:, lanes] + vec[:, RU : RU + 1])
        n2[:, lanes] = normed.astype(BF)
        r2[:, lanes] = inv
        out[:, lanes] = normed * vec[:, RU + 1 : RU + 2] + vec[:, RU + 2 : RU + 3]

    lane_loop(h.shape[1], leave)


def feed_backward(dm, units, vec, hb, act, slope, n2, r2, dfb, dz, dunits, dvec, vacc):
    vacc[...] = jnp.zeros(vacc.shape, F32)

    def leave(lanes):
        grad, normed = dm[:, lanes], n2[:, lanes].astype(F32)
        vacc[RU + 1] += grad * normed
        vacc[RU + 2] += grad
        grad = norm_grad(grad, normed, r2[:, lanes], vec[:, RU + 1 : RU + 2])
        dm[:, lanes] = grad
        short = grad.astype(BF)
        vacc[RU] += short.astype(F32)
        dfb[:, lanes] = short

    lane_loop(dm.shape[1], leave)
    for c in range(RU):
        rows = slice(c * D, (c + 1) * D)
        dz[rows, :] = (nn(units[RU + c][...], dfb[...]) * slope[rows, :].astype(F32)).astype(BF)
        dunits[RU + c][...] += nt(act[rows, :], dfb[...])
    for c in range(RU):
        rows = slice(c * D, (c + 1) * D)
        dm[...] += nn(units[c][...], dz[rows, :])
        dunits[c][...] += nt(hb[...], dz[rows, :])
        for lanes in range(0, dm.shape[1], LANES):
            vacc[c] += dz[rows, lanes : lanes + LANES].astype(F32)
    for index in range(RU + 3):
        dvec[:, index : index + 1] += jnp.sum(vacc[index], axis=1, keepdims=True)


def cross_forward(a, sq, vec, length, ab, cqt, kt, vt, ot, lse, n1, r1, bias, pair):
    ab[...] = a[...].astype(BF)
    cqt[...] = tn(sq[0][...], ab[...]).astype(BF)
    fill_bias(bias, length, None)
    attend(cqt, kt, vt, bias, ot, lse, pair)
    a[...] += tn(sq[1][...], ot[...])

    def leave(lanes):
        normed, inv = norm_parts(a[:, lanes])
        n1[:, lanes] = normed.astype(BF)
        r1[:, lanes] = inv
        a[:, lanes] = normed * vec[:, 0:1] + vec[:, 1:2]

    lane_loop(a.shape[1], leave)


def cross_backward(
    dbq, sq, vec, ab, cqt, kt, vt, ot, lse, n1, r1, bias, dca, dot, dqt, dkt, dvt, dsq, dvec, vacc
):
    vacc[0] = jnp.zeros(vacc.shape[1:], F32)
    vacc[1] = jnp.zeros(vacc.shape[1:], F32)

    def leave(lanes):
        grad, normed = dbq[:, lanes], n1[:, lanes].astype(F32)
        vacc[0] += grad * normed
        vacc[1] += grad
        grad = norm_grad(grad, normed, r1[:, lanes], vec[:, 0:1])
        dbq[:, lanes] = grad
        dca[:, lanes] = grad.astype(BF)

    lane_loop(dbq.shape[1], leave)
    dot[...] = nn(sq[1][...], dca[...]).astype(BF)
    dsq[1][...] += nt(ot[...], dca[...])
    attend_back(cqt, kt, vt, bias, ot, lse, dot, dqt, dkt, dvt)
    dsq[0][...] += nt(ab[...], dqt[...])
    dbq[...] += nn(sq[0][...], dqt[...])
    for index in range(2):
        dvec[:, index : index + 1] += jnp.sum(vacc[index], axis=1, keepdims=True)


SUB = 256
HALF = SUB // 2
QUART = SUB // 4
UNITS = 6 + 2 * RU
SUBS = UNITS * (D // SUB) + 1
MESH = pl.DeviceIdType.MESH
TENSOR_OF = (0, 1, 2, 3, 4, 5) + (6,) * RU + (7,) * RU
TENSOR_SIZE = (1,) * 6 + (RU, RU)
FIRST_UNIT = (0, 1, 2, 3, 4, 5, 6, 6 + RU)


def any_space():
    return pl.BlockSpec(memory_space=pl.ANY)


def vmem_space():
    return pl.BlockSpec(memory_space=pltpu.VMEM)


def smem_space():
    return pl.BlockSpec(memory_space=pltpu.SMEM)


def shape32(*dims):
    return jax.ShapeDtypeStruct(dims, F32)


def shape16(*dims):
    return jax.ShapeDtypeStruct(dims, BF)


def total_over_dp(n_dp, prepare, src, out, core_in, half, x_in, quart, right_in, left_in, right_out, left_out, sems):
    length = n_dp // 4
    section = lax.axis_index("section")
    dp = lax.axis_index("dp")
    core, x, z = dp % 2, (dp // 2) % 2, dp // 4
    sibling, beside = dp + 1 - 2 * core, dp + 2 - 4 * x
    has_left, has_right = z > 0, z < length - 1

    barrier = pltpu.get_barrier_semaphore()

    def greet(index):
        pl.semaphore_signal(barrier, inc=1, device_id=(section, index), device_id_type=MESH)

    greet(sibling)
    greet(beside)
    pl.when(has_left)(lambda: greet(dp - 4))
    pl.when(has_right)(lambda: greet(dp + 4))
    pl.semaphore_wait(barrier, 2 + has_left.astype(jnp.int32) + has_right.astype(jnp.int32))

    def block(t):
        return (t + SUBS - 1) % SUBS

    def base(t):
        return block(t) * SUB

    def rows(start, size):
        return pl.ds(pl.multiple_of(start, QUART), size)

    def send(step, t, source, target, index):
        return pltpu.make_async_remote_copy(
            src_ref=source,
            dst_ref=target,
            send_sem=sems.at[0, step, t],
            recv_sem=sems.at[1, step, t],
            device_id=(section, index),
            device_id_type=MESH,
        )

    def copy_core(t):
        return send(0, t, src.at[rows(base(t) + HALF * (1 - core), HALF)], core_in.at[t], sibling)

    def copy_x(t):
        return send(1, t, half.at[t, rows(QUART * (1 - x), QUART)], x_in.at[t], beside)

    def copy_right(t, source):
        return send(2, t, source.at[t], right_in.at[t], dp + 4)

    def copy_left(t, source):
        return send(3, t, source.at[t], left_in.at[t], dp - 4)

    def copy_back_x(t):
        place = rows(base(t) + HALF * core + QUART * x, QUART)
        return send(4, t, out.at[place], out.at[place], beside)

    def copy_back_core(t):
        place = rows(base(t) + HALF * core, HALF)
        return send(5, t, out.at[place], out.at[place], sibling)

    def add(one, two):
        return (one.astype(F32) + two.astype(F32)).astype(BF)

    def step_core(t):
        prepare(block(t))
        copy_core(t).start()

    def step_x(t):
        copy_core(t).wait_recv()
        half[t] = add(src[rows(base(t) + HALF * core, HALF), :], core_in[t])
        copy_x(t).start()

    def step_quart(t):
        copy_x(t).wait_recv()
        quart[t] = add(half[t, rows(QUART * x, QUART), :], x_in[t])

        @pl.when(jnp.logical_not(has_left) & has_right)
        def _():
            copy_right(t, quart).start()

        @pl.when(jnp.logical_not(has_right) & has_left)
        def _():
            copy_left(t, quart).start()

    def step_right(t):
        @pl.when(has_left)
        def _():
            copy_right(t, right_out).wait_recv()

            @pl.when(has_right)
            def _():
                right_out[t] = add(quart[t], right_in[t])
                copy_right(t, right_out).start()

    def step_left(t):
        @pl.when(has_right)
        def _():
            copy_left(t, left_out).wait_recv()

            @pl.when(has_left)
            def _():
                left_out[t] = add(quart[t], left_in[t])
                copy_left(t, left_out).start()

    def step_total(t):
        place = rows(base(t) + HALF * core + QUART * x, QUART)
        mine = quart[t].astype(F32)
        mine += jnp.where(has_left, right_in[t].astype(F32), 0.0)
        mine += jnp.where(has_right, left_in[t].astype(F32), 0.0)
        out[place, :] = mine.astype(BF)
        copy_back_x(t).start()

    def step_back(t):
        copy_back_x(t).wait_recv()
        copy_back_core(t).start()

    last = length - 1
    lags = (
        (step_core, 0),
        (step_x, 1),
        (step_quart, 2),
        (step_right, 2 + z),
        (step_left, 2 + last - z),
        (step_total, 2 + jnp.maximum(z, last - z)),
        (step_back, 3 + jnp.maximum(z, last - z)),
    )

    def tick(t, carry):
        for step, lag in lags:
            at = t - lag

            @pl.when((at >= 0) & (at < SUBS))
            def _(step=step, at=at):
                step(at)

        return carry

    lax.fori_loop(0, SUBS + 3 + last, tick, 0)

    def settle(t, carry):
        copy_back_core(t).wait_recv()
        copy_core(t).wait_send()
        copy_x(t).wait_send()
        pl.when(has_right)(lambda: copy_right(t, right_out).wait_send())
        pl.when(has_left)(lambda: copy_left(t, left_out).wait_send())
        copy_back_x(t).wait_send()
        copy_back_core(t).wait_send()
        return carry

    lax.fori_loop(0, SUBS, settle, 0)


def total_scratch():
    return [
        pltpu.VMEM((SUBS, HALF, D), BF),
        pltpu.VMEM((SUBS, HALF, D), BF),
        pltpu.VMEM((SUBS, QUART, D), BF),
        pltpu.VMEM((SUBS, QUART, D), BF),
        pltpu.VMEM((SUBS, QUART, D), BF),
        pltpu.VMEM((SUBS, QUART, D), BF),
        pltpu.VMEM((SUBS, QUART, D), BF),
        pltpu.VMEM((SUBS, QUART, D), BF),
        pltpu.SemaphoreType.DMA((2, 6, SUBS)),
    ]


def weights_kernel(n_dp, owners, slots, pack, out, src, *scratch):
    dp = lax.axis_index("dp")

    def slot_of(tensor):
        prior = jnp.int32(0)
        for earlier in range(tensor):
            prior += jnp.where(owners[0, earlier] == owners[0, tensor], TENSOR_SIZE[earlier], 0)
        return prior

    def prepare(sub):
        @pl.when(sub == SUBS - 1)
        def _():
            src[pl.ds((SUBS - 1) * SUB, SUB), :] = pack[...]

        for unit in range(UNITS):

            @pl.when(sub // 2 == unit)
            def _(unit=unit):
                tensor = TENSOR_OF[unit]
                slot = jnp.minimum(slot_of(tensor) + (unit - FIRST_UNIT[tensor]), slots.shape[0] - 1)
                start = pl.multiple_of((sub % 2) * SUB, SUB)
                kept = jnp.where(owners[0, tensor] == dp, slots[slot, pl.ds(start, SUB), :], 0.0)
                src[pl.ds(pl.multiple_of(sub * SUB, SUB), SUB), :] = kept.astype(BF)

    total_over_dp(n_dp, prepare, src, out, *scratch)


def gather_weights(n_dp, owners, slots, pack):
    return pl.pallas_call(
        functools.partial(weights_kernel, n_dp),
        name="gather_weights",
        out_shape=shape16(SUBS * SUB, D),
        in_specs=[smem_space(), vmem_space(), vmem_space()],
        out_specs=vmem_space(),
        scratch_shapes=[pltpu.VMEM((SUBS * SUB, D), BF)] + total_scratch(),
        compiler_params=pltpu.CompilerParams(
            collective_id=0, has_side_effects=True, vmem_limit_bytes=56 * 2**20
        ),
    )(owners, slots, pack)


def gradients_kernel(n_dp, src, out, *scratch):
    total_over_dp(n_dp, lambda sub: None, src, out, *scratch)


def sum_gradients(n_dp, grads):
    return pl.pallas_call(
        functools.partial(gradients_kernel, n_dp),
        name="sum_gradients",
        out_shape=shape16(SUBS * SUB, D),
        in_specs=[vmem_space()],
        out_specs=vmem_space(),
        scratch_shapes=total_scratch(),
        compiler_params=pltpu.CompilerParams(
            collective_id=1, has_side_effects=True, vmem_limit_bytes=56 * 2**20
        ),
    )(grads)


def self_forward_kernel(info, x, sq, vec, ut, n0, r0, qt, kt, vt, ot, lse, n1, r1, y, *scratch):
    block = pl.program_id(0)
    squares = [sq.at[pl.ds(i * D, D)] for i in range(4)]
    saved = [ref.at[0] for ref in (ut, n0, r0, qt, kt, vt, ot, lse, n1, r1, y)]
    self_forward(x, squares, vec, info[0] == 1, info[1 + block], *saved, *scratch)


def block_spec(*dims):
    return pl.BlockSpec((1,) + dims, lambda b, info: (b,) + (0,) * len(dims))


def fixed_spec(*dims):
    return pl.BlockSpec(dims, lambda b, info: (0,) * len(dims))


def saved_shapes(count, tokens):
    wide = shape16(count, D, tokens)
    row = shape32(count, 1, tokens)
    return [wide, wide, row, wide, wide, wide, wide, shape32(count, HEADS, tokens), wide, row]


def call_self_forward(info, x, weights, vec, count, tokens):
    shapes = saved_shapes(count, tokens) + [shape32(count, D, tokens)]
    return pl.pallas_call(
        self_forward_kernel,
        name="self_forward",
        out_shape=shapes,
        grid_spec=pltpu.PrefetchScalarGridSpec(
            num_scalar_prefetch=1,
            grid=(count,),
            in_specs=[
                pl.BlockSpec((tokens, D), lambda b, info: (b, 0)),
                fixed_spec(4 * D, D),
                fixed_spec(D, LANES),
            ],
            out_specs=[block_spec(*s.shape[1:]) for s in shapes],
            scratch_shapes=[
                pltpu.VMEM((tokens, tokens), F32),
                pltpu.VMEM((D, tokens), F32),
                pltpu.VMEM((2, tokens, tokens), F32),
            ],
        ),
        compiler_params=pltpu.CompilerParams(vmem_limit_bytes=56 * 2**20),
    )(info, x, weights, vec)


def self_backward_kernel(info, dy, sq, vec, *refs):
    block = pl.program_id(0)
    saved = [ref.at[0] for ref in refs[:10]]
    dx, dsq_out, dvec, dys, bias, dsa, dot, dqt, dkt, dvt, dsq, vacc = refs[10:]
    squares = [sq.at[pl.ds(i * D, D)] for i in range(4)]

    @pl.when(block == 0)
    def _():
        dsq[...] = jnp.zeros(dsq.shape, F32)
        dvec[...] = jnp.zeros(dvec.shape, F32)

    dys[...] = dy[0]
    self_backward(
        dys, squares, vec, info[0] == 1, info[1 + block], *saved, dx, bias, dsa, dot, dqt, dkt, dvt, dsq, dvec, vacc
    )

    @pl.when(block == pl.num_programs(0) - 1)
    def _():
        for i in range(4):
            dsq_out[i * D : (i + 1) * D, :] = dsq[i].astype(BF)


def call_self_backward(info, dy, weights, vec, saved, count, tokens):
    return pl.pallas_call(
        self_backward_kernel,
        name="self_backward",
        out_shape=[shape32(count * tokens, D), shape16(4 * D, D), shape32(D, LANES)],
        grid_spec=pltpu.PrefetchScalarGridSpec(
            num_scalar_prefetch=1,
            grid=(count,),
            in_specs=[block_spec(D, tokens), fixed_spec(4 * D, D), fixed_spec(D, LANES)]
            + [block_spec(*s.shape[1:]) for s in saved],
            out_specs=[
                pl.BlockSpec((tokens, D), lambda b, info: (b, 0)),
                fixed_spec(4 * D, D),
                fixed_spec(D, LANES),
            ],
            scratch_shapes=[pltpu.VMEM((D, tokens), F32), pltpu.VMEM((tokens, tokens), F32)]
            + [pltpu.VMEM((D, tokens), BF)] * 5
            + [pltpu.VMEM((4, D, D), F32), pltpu.VMEM((4, D, LANES), F32)],
        ),
        compiler_params=pltpu.CompilerParams(vmem_limit_bytes=56 * 2**20),
    )(info, dy, weights, vec, *saved)


def middle_kernel(
    info, vec, y, cot, weights, hidden, dy, grads, dvec,
    wts, acc, sent, got, h, mem, hb, act, slope, n2, r2, dfb, dz, vacc, fvec_acc,
    ab, cqt, kt, vt, ot, lse, n1, r1, bias, dca, dot, dqt, pair, tok, stage, sems, load_sem,
):
    section = lax.axis_index("section")
    dp = lax.axis_index("dp")
    count, tokens = y.shape[0], y.shape[2]
    other = 1 - section
    barrier = pltpu.get_barrier_semaphore()
    pl.semaphore_signal(barrier, inc=1, device_id=(other, dp), device_id_type=MESH)
    pl.semaphore_wait(barrier, 1)

    def move(source, target):
        copy = pltpu.make_async_copy(source, target, load_sem)
        copy.start()
        copy.wait()

    def swap(b):
        return pltpu.make_async_remote_copy(
            src_ref=sent.at[b],
            dst_ref=got.at[b],
            send_sem=sems.at[0, b],
            recv_sem=sems.at[1, b],
            device_id=(other, dp),
            device_id_type=MESH,
        )

    def each(body):
        def step(b, carry):
            body(b)
            return carry

        lax.fori_loop(0, count, step, 0)

    move(weights.at[pl.ds(4 * D, 10 * D)], wts)
    unit = [wts.at[pl.ds(i * D, D)] for i in range(10)]
    s4, s5, ffn = unit[0], unit[1], unit[2:]
    gain = vec.at[:, pl.ds(0, LANES)]
    cross_vec = vec.at[:, pl.ds(LANES, LANES)]
    acc[...] = jnp.zeros(acc.shape, F32)
    fvec_acc[...] = jnp.zeros(fvec_acc.shape, F32)
    cross_acc = [acc.at[i] for i in range(2)]
    ffn_acc = [acc.at[2 + i] for i in range(8)]

    def run_feed_forward():
        feed_forward(h, ffn, gain, hb, act, slope, n2, r2, mem)

    def emit_hidden(b):
        tok[...] = mem[...].T.astype(BF)
        move(tok, hidden.at[pl.ds(pl.multiple_of(b * tokens, tokens), tokens)])

    def load_cotangent(b):
        move(cot.at[pl.ds(pl.multiple_of(b * tokens, tokens), tokens)], tok)
        token = lax.broadcasted_iota(jnp.int32, (D, tokens), 1)
        h[...] = jnp.where(token < info[1 + b], tok[...].astype(F32).T, 0.0)

    def run_feed_backward():
        feed_backward(h, ffn, gain, hb, act, slope, n2, r2, dfb, dz, ffn_acc, fvec_acc.at[0], vacc)

    @pl.when(section == 0)
    def _():
        def ahead(b):
            move(y.at[b], h)
            run_feed_forward()
            emit_hidden(b)
            short = mem[...].astype(BF)
            sent[b, 0] = tn(s4[...], short).astype(BF)
            sent[b, 1] = tn(s5[...], short).astype(BF)
            swap(b).start()

        each(ahead)

        def back(b):
            move(y.at[b], h)
            run_feed_forward()
            ab[...] = mem[...].astype(BF)
            load_cotangent(b)
            swap(b).wait_recv()
            for i, matrix in enumerate((s4, s5)):
                h[...] += nn(matrix[...], got[b, i])
                acc[i] += nt(ab[...], got[b, i])
            run_feed_backward()
            move(h, dy.at[b])

        each(back)

    @pl.when(section == 1)
    def _():
        def both(b):
            move(y.at[b], h)
            swap(b).wait_recv()
            kt[...] = got[b, 0]
            vt[...] = got[b, 1]
            cross_forward(h, (s4, s5), cross_vec, info[1 + count + b], ab, cqt, kt, vt, ot, lse, n1, r1, bias, pair)
            run_feed_forward()
            emit_hidden(b)
            load_cotangent(b)
            run_feed_backward()
            cross_backward(
                h, (s4, s5), cross_vec, ab, cqt, kt, vt, ot, lse, n1, r1, bias, dca, dot, dqt,
                sent.at[b, 0], sent.at[b, 1], cross_acc, fvec_acc.at[1], vacc,
            )
            swap(b).start()
            move(h, dy.at[b])

        each(both)

    def finish(b):
        swap(b).wait_send()

    each(finish)
    for i in range(10):
        stage[...] = acc[i].astype(BF)
        move(stage, grads.at[pl.ds(i * D, D)])
    dvec[...] = fvec_acc[...]


def call_middle(info, vec, y, cot, weights, count, tokens):
    wide16 = pltpu.VMEM((D, tokens), BF)
    wide32 = pltpu.VMEM((D, tokens), F32)
    row = pltpu.VMEM((1, tokens), F32)
    return pl.pallas_call(
        middle_kernel,
        name="middle",
        out_shape=[
            shape16(count * tokens, D),
            shape32(count, D, tokens),
            shape16(10 * D, D),
            shape32(2, D, LANES),
        ],
        in_specs=[smem_space(), vmem_space(), any_space(), any_space(), any_space()],
        out_specs=[any_space(), any_space(), any_space(), vmem_space()],
        scratch_shapes=[
            pltpu.VMEM((10 * D, D), BF),
            pltpu.VMEM((10, D, D), F32),
            pltpu.VMEM((count, 2, D, tokens), BF),
            pltpu.VMEM((count, 2, D, tokens), BF),
            wide32, wide32, wide16,
            pltpu.VMEM((FF, tokens), BF), pltpu.VMEM((FF, tokens), BF),
            wide16, row, wide16,
            pltpu.VMEM((FF, tokens), BF),
            pltpu.VMEM((RU + 3, D, LANES), F32),
            pltpu.VMEM((2, D, LANES), F32),
            wide16, wide16, wide16, wide16, wide16,
            pltpu.VMEM((HEADS, tokens), F32),
            wide16, row,
            pltpu.VMEM((tokens, tokens), F32),
            wide16, wide16, wide16,
            pltpu.VMEM((2, tokens, tokens), F32),
            pltpu.VMEM((tokens, D), BF),
            pltpu.VMEM((D, D), BF),
            pltpu.SemaphoreType.DMA((2, count)),
            pltpu.SemaphoreType.DMA,
        ],
        compiler_params=pltpu.CompilerParams(
            collective_id=2, has_side_effects=True, vmem_limit_bytes=60 * 2**20
        ),
    )(info, vec, y, cot, weights)


matrix_rate = 0.04
vector_rate = 0.25
matrix_decay = 0.01


def adam_update(weight, moment_old, square_old, gradient, learn_rate, decay_rate):
    moment_one = 0.5 * moment_old + 0.5 * gradient
    moment_two = 0.5 * square_old + 0.5 * gradient * gradient
    correction = 1.0 - 0.5**STEP
    adam_step = moment_one / correction / (jnp.sqrt(moment_two / correction) + 1e-08)
    return (weight - learn_rate * (adam_step + decay_rate * weight), moment_one, moment_two)


def adam_kernel(place, grad, weight, first, second, weight_out, first_out, second_out):
    taken = place[pl.program_id(0)] >= 0
    fresh = adam_update(weight[0], first[0], second[0], grad[...].astype(F32), matrix_rate, matrix_decay)
    for new, old, out in zip(fresh, (weight, first, second), (weight_out, first_out, second_out)):
        out[0] = jnp.where(taken, new, old[0])


def call_adam(place, grads, weight, first, second):
    slots = weight.shape[0]
    spec = block_spec(D, D)
    out = shape32(slots, D, D)
    return pl.pallas_call(
        adam_kernel,
        name="adam",
        out_shape=[out] * 3,
        grid_spec=pltpu.PrefetchScalarGridSpec(
            num_scalar_prefetch=1,
            grid=(slots,),
            in_specs=[pl.BlockSpec((D, D), lambda s, place: (jnp.maximum(place[s], 0), 0))] + [spec] * 3,
            out_specs=[spec] * 3,
        ),
    )(place, grads, weight, first, second)


def unit_tables(owner_row):
    tensor_of = np.array(TENSOR_OF)
    first_unit = np.array(FIRST_UNIT)
    owned_by = owner_row[:8]
    earlier = (owned_by[:, None] == owned_by[None, :]) & jnp.asarray(
        np.arange(8)[None, :] < np.arange(8)[:, None]
    )
    prior = jnp.sum(jnp.where(earlier, jnp.array(TENSOR_SIZE, jnp.int32)[None, :], 0), axis=1)
    unit_owner = owned_by[tensor_of]
    unit_slot = prior[tensor_of] + jnp.asarray(np.arange(UNITS) - first_unit[tensor_of], jnp.int32)
    return unit_owner, unit_slot.astype(jnp.int32)


def slot_units(owner_row, dp, slots):
    unit_owner, unit_slot = unit_tables(owner_row)
    hit = (unit_owner[None, :] == dp) & (unit_slot[None, :] == jnp.arange(slots, dtype=jnp.int32)[:, None])
    return jnp.sum(jnp.where(hit, jnp.arange(UNITS, dtype=jnp.int32)[None, :] + 1, 0), axis=1) - 1


def three_pieces(value):
    high = value.astype(BF)
    rest = value - high.astype(F32)
    mid = rest.astype(BF)
    low = (rest - mid.astype(F32)).astype(BF)
    return jnp.concatenate([high, mid, low], axis=0)


def pad_rows(value, rows):
    return jnp.pad(value, ((0, rows - value.shape[0]), (0, 0)))


def columns(rows):
    stacked = jnp.stack(rows, axis=1)
    return jnp.pad(stacked, ((0, 0), (0, LANES - stacked.shape[1])))


def local(n_dp, tokens, cotangent, lengths, owners, master_sq, mom1_sq, mom2_sq, master_vec, mom1_vec, mom2_vec):
    section = lax.axis_index("section")
    dp = lax.axis_index("dp")
    first = section == 0
    count = lengths.shape[1]
    width = tokens.shape[1] // count
    vec_store = master_vec[0, 0]
    vrows = vec_store.shape[0]
    owns_vector = owners[0, 8] == dp
    pack = pad_rows(three_pieces(jnp.where(owns_vector, vec_store, 0.0)), SUB)
    weights = gather_weights(n_dp, owners, master_sq[0, 0], pack)
    pieces = weights[UNITS * D : UNITS * D + 3 * vrows].astype(F32)
    vector = pieces[:vrows] + pieces[vrows : 2 * vrows] + pieces[2 * vrows :]
    own = jnp.where(first, lengths[0], lengths[1])
    info = jnp.concatenate([section[None].astype(jnp.int32), own, lengths[0]])
    after = [jnp.where(first, vector[1], vector[0]), jnp.where(first, vector[4], vector[3])]
    self_vec = columns([vector[0], vector[3]] + after)
    ffn_vec = columns([vector[7], vector[8], vector[9], vector[10], vector[6], vector[2], vector[5]])
    cross_vec = columns([vector[1], vector[4]])
    saved = call_self_forward(info, tokens[0], weights, self_vec, count, width)
    hidden, dy, late, late_vec = call_middle(
        info, jnp.concatenate([ffn_vec, cross_vec], axis=1), saved[10], cotangent[0], weights, count, width
    )
    dx, early, early_vec = call_self_backward(info, dy, weights, self_vec, saved[:10], count, width)
    ffn_grad, cross_grad = late_vec[0], late_vec[1]
    vector_grad = jnp.stack(
        [
            jnp.where(first, early_vec[:, 0], early_vec[:, 2]),
            jnp.where(first, early_vec[:, 2], cross_grad[:, 0]),
            ffn_grad[:, RU + 1],
            jnp.where(first, early_vec[:, 1], early_vec[:, 3]),
            jnp.where(first, early_vec[:, 3], cross_grad[:, 1]),
            ffn_grad[:, RU + 2],
            ffn_grad[:, RU],
        ]
        + [ffn_grad[:, i] for i in range(RU)]
    )
    grads = jnp.concatenate([early, late, pad_rows(three_pieces(vector_grad), SUB)], axis=0)
    total = sum_gradients(n_dp, grads)
    pieces = total[UNITS * D : UNITS * D + 3 * vrows].astype(F32)
    total_vector = pieces[:vrows] + pieces[vrows : 2 * vrows] + pieces[2 * vrows :]
    place = slot_units(owners[0], dp, master_sq.shape[2])
    squares_new = call_adam(place, total, master_sq[0, 0], mom1_sq[0, 0], mom2_sq[0, 0])
    vector_new = adam_update(vec_store, mom1_vec[0, 0], mom2_vec[0, 0], total_vector, vector_rate, 0.0)
    vector_new = [
        jnp.where(owns_vector, new, old)
        for new, old in zip(vector_new, (vec_store, mom1_vec[0, 0], mom2_vec[0, 0]))
    ]
    return (
        hidden[None],
        dx[None],
        *[value[None, None] for value in squares_new],
        *[value[None, None] for value in vector_new],
    )


def solution(mesh):
    n_dp = mesh.shape["dp"]
    slots = P("section", "dp", None, None, None)
    packs = P("section", "dp", None, None)
    rows = P("section", "dp", None)
    return jax.shard_map(
        functools.partial(local, n_dp),
        mesh=mesh,
        in_specs=(rows, rows, P(None, "dp"), P("section", None), slots, slots, slots, packs, packs, packs),
        out_specs=(rows, rows, slots, slots, slots, packs, packs, packs),
        check_vma=False,
    )
```

time: 3190 us -> 551 us (0.17)
  waiting for transfers between devices: 2210 us -> 0 us
  Pallas kernels: 0 us -> 521 us
  matrix products: 310 us -> 0 us
  local copies, waits for them, and re-layouts: 232 us -> 9.16 us
  other arithmetic: 239 us -> 18.1 us
  blocking collectives: 123 us -> 0 us
  loops' own time: 43.4 us -> 0 us
    psum x15 -> x0, waiting for transfers between devices: 1460 us -> none  [the longest x14 1280 us: broadcast(): return lax.psum(kept, axis)]
    ppermute x4 -> x0, waiting for transfers between devices: 748 us -> none  [shifted(): return lax.ppermute(block, axis, route)]
    pallas_call x0 -> x6, Pallas kernels: none -> 521 us  [the longest x1 190 us: call_middle(): pl.pallas_call(middle_kernel, name='middle', out_shape=[shape16(count * t...]
    dot_general x38 -> x0, matrix products: 298 us -> none  [the longest x29 148 us: dense_product(): return jnp.dot(left, right, preferred_element_type=jnp.float32)]
    psum x2 -> x0, blocking collectives: 123 us -> none  [the longest x1 67.6 us: local(): total_units, total_vector = lax.psum((grad_units, vector_grad), 'dp')]
    reduce_sum x18 -> x2, other arithmetic: 93.7 us -> 0.98 us  [the longest x1 0.86 us: unit_tables(): jnp.sum(jnp.where(earlier, jnp.array(TENSOR_SIZE, jnp.int32)[None, :], 0)...]
    reshape x12 -> x0, local copies, waits for them, and re-layouts: 60.2 us -> none  [the longest x3 17.9 us: attention(): key_heads = keys_in.reshape(block_count, keys_in.shape[1], HEADS, head_size)]
    convert_element_type x10 -> x5, other arithmetic: 50.3 us -> 3.06 us  [the longest x1 0.79 us: local(): pieces = weights[UNITS * D:UNITS * D + 3 * vrows].astype(F32)]
  transfers between devices with their start and end apart: 19 -> 0, of which waited for: 19 -> 0; matrix products, arithmetic and copies ran while one was open for 1% -> 0% of each run, Pallas kernels for 0% -> 0%
where the time goes in v1:
time: 551 us; the launch traced here: 549 us
  Pallas kernels  521 us (95%)
  other arithmetic  18.1 us (3%)
  local copies, waits for them, and re-layouts  9.16 us (2%)
    pallas_call x1, Pallas kernels, call_middle(): pl.pallas_call(middle_kernel, name='middle', out_shape=[shape16(count * t...  190 us
    pallas_call x1, Pallas kernels, gather_weights(): pl.pallas_call(functools.partial(weights_kernel, n_dp), name='gather_weig...  116 us
    pallas_call x1, Pallas kernels, sum_gradients(): pl.pallas_call(functools.partial(gradients_kernel, n_dp), name='sum_gradi...  116 us
    pallas_call x1, Pallas kernels, call_self_backward(): pl.pallas_call(self_backward_kernel, name='self_backward', out_shape=[sha...  51.4 us
    pallas_call x1, Pallas kernels, call_self_forward(): pl.pallas_call(self_forward_kernel, name='self_forward', out_shape=shapes...  31.5 us
    pallas_call x1, Pallas kernels, call_adam(): pl.pallas_call(adam_kernel, name='adam', out_shape=[out] * 3, grid_spec=p...  16 us

profile of v1, /device:TPU:1, one launch (start us, length us, event | category | flops | bytes accessed | tf_op | source)
XLA Modules:
  0.0 549.4 jit_solution(11562833183453991978)
XLA Ops:
  0.6 1.2 slice.126
  2.5 0.7 slice_bitcast_fusion.13
  3.2 0.9 select_reduce_fusion.3
  4.1 0.8 broadcast_select_fusion.2
  4.8 0.7 slice_bitcast_fusion.14
  5.5 0.6 pad_add_fusion.info
  6.1 0.7 pad_clamp_fusion
  6.7 0.7 gather_fusion.1
  7.4 0.7 gather_fusion
  8.1 0.7 add.56
  8.9 0.5 broadcast_add_fusion.place
  9.4 0.7 fusion.17
  10.1 0.7 fusion.20
  10.9 0.7 fusion.7.pack
  11.6 116.4 %gather_weights.1.sq.weights = bf16[7424,512]{1,0:T(8,128)(2,1)} custom-call(s32[1,9]{1,0:T(1,128)} %owners.1, f32[6,512,512]{2,1,0:T(8,128)} %bitcast.109, bf16[256,512]{1,0:T(8,128)(2,1)} %fusion.7.pack), custom_call_target="tpu_custom_call" | custom-call | tf_op jit(solution)/shard_map/gather_weights/pallas_call | solution.py:504
  128.0 0.8 slice_convert_fusion.1
  129.0 0.1 copy.58
  129.1 0.9 select_maximum_fusion.vec
  130.7 1.0 select_maximum_fusion.1.vec
  131.7 31.5 %self_forward.1 = (bf16[4,512,512]{2,1,0:T(8,128)(2,1)}, bf16[4,512,512]{2,1,0:T(8,128)(2,1)}, f32[4,1,512]{2,1,0:T(1,128)}, bf16[4,512,512]{2,1,0:T(8,128)(2,1)...) custom-call(s32[9]{0:T(128)} %pad_add_fusion.info, ...), custom_call_target="tpu_custom_call" | custom-call | tf_op jit(solution)/shard_map/self_forward/pallas_call | solution.py:558
  163.2 189.5 %middle.1 = (bf16[2048,512]{1,0:T(8,128)(2,1)}, f32[4,512,512]{2,1,0:T(8,128)}, bf16[5120,512]{1,0:T(8,128)(2,1)}, f32[2,512,128]{2,1,0:T(8,128)}) custom-call(s32[9]{0:T(128)} %pad_add_fusion.info, f32[512,256]{1,0:T(8,128)} %select_maximum_fusion.vec, f32[4,512,512]{2,1,0:T(8,128)} %get-tuple-element.29.y, bf16[2048,512]{1,0:T(8,128)(2,1)} %bitcast.115, ...), custom_call_target="tpu_custom_call" | custom-call | tf_op jit(solution)/shard_map/middle/pallas_call | solution.py:748
  352.7 51.4 %self_backward.1 = (f32[2048,512]{1,0:T(8,128)}, bf16[2048,512]{1,0:T(8,128)(2,1)}, f32[512,128]{1,0:T(8,128)}) custom-call(s32[9]{0:T(128)} %pad_add_fusion.info, f32[4,512,512]{2,1,0:T(8,128)} %get-tuple-element.31.dy, bf16[7424,512]{1,0:T(8,128)(2,1)} %gather_weights.1.sq.weights, f32[512,128]{1,0:T(8,128)} %select_maximum_fusion.1.vec, ...), custom_call_target="tpu_custom_call" | custom-call | tf_op jit(solution)/shard_map/self_backward/pallas_call | solution.py:604
  404.2 2.0 fusion.10
  406.2 1.0 slice_reduce_fusion
  407.3 6.1 %pad_maximum_fusion.src = bf16[7424,512]{1,0:T(8,128)(2,1)} fusion(bf16[256,512]{1,0:T(8,128)(2,1)S(1)} %fusion.9, bf16[5120,512]{1,0:T(8,128)(2,1)} %get-tuple-element.44, bf16[2048,512]{1,0:T(8,128)(2,1)S(1)} %copy-done.1), kind=kLoop, calls=%fused_computation.2 | loop fusion | flops 22806528 | bytes 15204352 | tf_op jit(solution)/shard_map/concatenate | solution.py:897
  413.4 115.9 %sum_gradients.1.grad = bf16[7424,512]{1,0:T(8,128)(2,1)} custom-call(bf16[7424,512]{1,0:T(8,128)(2,1)} %pad_maximum_fusion.src), custom_call_target="tpu_custom_call" | custom-call | tf_op jit(solution)/shard_map/sum_gradients/pallas_call | solution.py:522
  529.3 0.8 slice_convert_fusion
  530.1 0.6 copy.67
  530.8 0.6 copy.66
  531.5 0.6 copy.65
  532.1 16.0 %adam.1 = (f32[6,512,512]{2,1,0:T(8,128)}, f32[6,512,512]{2,1,0:T(8,128)}, f32[6,512,512]{2,1,0:T(8,128)}) custom-call(s32[6]{0:T(128)} %broadcast_add_fusion.place, bf16[7424,512]{1,0:T(8,128)(2,1)} %sum_gradients.1.grad, f32[6,512,512]{2,1,0:T(8,128)} %bitcast.110, f32[6,512,512]{2,1,0:T(8,128)} %bitcast.111, f32[6,512,512]{2,1,0:T(8,128)} %bitcast.112), custom_call_target="tpu_custom_call" | custom-call | tf_op jit(solution)/shard_map/adam/pallas_call | solution.py:811
  548.1 1.3 copy.115
  (31 shorter events, 1.2 us)
Async XLA Ops:
  352.7 51.4 %copy-start.2 = (f32[2,512,128]{2,1,0:T(8,128)S(1)}, f32[2,512,128]{2,1,0:T(8,128)}, u32[]{:S(2)}) copy-start(f32[2,512,128]{2,1,0:T(8,128)} %get-tuple-element.46) | copy-start | bytes 1572868
  404.1 3.1 copy-start.1
  413.4 116.7 %copy-start.4 = (f32[1,1,11,512]{3,1,2,0:T(1,128)S(1)}, f32[1,1,11,512]{3,1,2,0:T(1,128)}, u32[]{:S(2)}) copy-start(f32[1,1,11,512]{3,1,2,0:T(1,128)} %param.25) | copy-start | bytes 67588
  413.4 117.4 %copy-start.3 = (f32[1,1,11,512]{3,1,2,0:T(1,128)S(1)}, f32[1,1,11,512]{3,1,2,0:T(1,128)}, u32[]{:S(2)}) copy-start(f32[1,1,11,512]{3,1,2,0:T(1,128)} %param.23) | copy-start | bytes 67588
  413.4 117.4 %copy-start.5 = (f32[1,1,11,512]{3,1,2,0:T(1,128)S(1)}, f32[1,1,11,512]{3,1,2,0:T(1,128)}, u32[]{:S(2)}) copy-start(f32[1,1,11,512]{3,1,2,0:T(1,128)} %param.24) | copy-start | bytes 67588
  532.1 16.0 %copy-start = (bf16[2048,512]{1,0:T(8,128)(2,1)S(1)}, bf16[2048,512]{1,0:T(8,128)(2,1)}, u32[]{:S(2)}) copy-start(bf16[2048,512]{1,0:T(8,128)(2,1)} %get-tuple-element.30) | copy-start | bytes 6291460

commit v2 on v1

v2 whole, which is shorter than its diff:
```python
import functools
import jax
import jax.numpy as jnp
import numpy as np
from jax import lax
from jax.experimental import pallas as pl
from jax.experimental.pallas import tpu as pltpu
from jax.sharding import PartitionSpec as P

D = 512
HEADS = 8
HS = D // HEADS
FF = 2048
RU = FF // D
STEP = 5
LANES = 128
F32 = jnp.float32
BF = jnp.bfloat16
NEG = -1e30


def nn(a, b):
    return jnp.dot(a, b, preferred_element_type=F32)


def nt(a, b):
    return lax.dot_general(a, b, (((1,), (1,)), ((), ())), preferred_element_type=F32)


def tn(a, b):
    return lax.dot_general(a, b, (((0,), (0,)), ((), ())), preferred_element_type=F32)


def lane_loop(count, body):
    def step(i, carry):
        body(pl.ds(pl.multiple_of(i * LANES, LANES), LANES))
        return carry

    lax.fori_loop(0, count // LANES, step, 0)


def norm_parts(value):
    mean = jnp.mean(value, axis=0, keepdims=True)
    centred = value - mean
    inv = lax.rsqrt(jnp.mean(centred * centred, axis=0, keepdims=True) + 1e-05)
    return centred * inv, inv


def norm_grad(grad, normed, inv, gain):
    scaled = grad * gain
    mean_one = jnp.mean(scaled, axis=0, keepdims=True)
    mean_two = jnp.mean(scaled * normed, axis=0, keepdims=True)
    return (scaled - mean_one - normed * mean_two) * inv


def fill_bias(bias, length, causal):
    rows = bias.shape[0]

    def body(lanes):
        key = lax.broadcasted_iota(jnp.int32, (rows, LANES), 0)
        query = lax.broadcasted_iota(jnp.int32, (rows, LANES), 1) + lanes.start
        allowed = key < length
        if causal is not None:
            allowed = allowed & ((key <= query) | jnp.logical_not(causal))
        bias[:, lanes] = jnp.where(allowed, 0.0, NEG)

    lane_loop(bias.shape[1], body)


def head_rows(h):
    return pl.ds(pl.multiple_of(h * HS, HS), HS)


def attend(qt, kt, vt, bias, ot, lse, pair, pause=None):
    def score(h, out):
        rows = head_rows(h)
        out[...] = tn(kt[rows, :], qt[rows, :] * BF(0.125))

    def finish(h, scores):
        rows = head_rows(h)
        biased = scores[...] + bias[...]
        top = jnp.max(biased, axis=0, keepdims=True)
        weights = jnp.exp(biased - top).astype(BF)
        values = jnp.concatenate([vt[rows, :], jnp.ones((16, vt.shape[1]), BF)], axis=0)
        out = nn(values, weights)
        total = out[HS : HS + 1]
        ot[rows, :] = (out[:HS] * (1.0 / total)).astype(BF)
        lse[pl.ds(h, 1), :] = top + jnp.log(total)

    one, two = pair.at[0], pair.at[1]
    score(0, one)

    def body(i, carry):
        score(2 * i + 1, two)
        finish(2 * i, one)
        score(jnp.minimum(2 * i + 2, HEADS - 1), one)
        finish(2 * i + 1, two)
        return carry

    if pause is None:
        lax.fori_loop(0, HEADS // 2, body, 0, unroll=True)
    else:
        lax.fori_loop(0, HEADS // 4, body, 0, unroll=True)
        pause()
        lax.fori_loop(HEADS // 4, HEADS // 2, body, 0, unroll=True)


def attend_back(qt, kt, vt, bias, ot, lse, dot, dqt, dkt, dvt, pause=None):
    def head(h, carry):
        rows = head_rows(h)
        keys, grads = kt[rows, :], dot[rows, :]
        queries = qt[rows, :] * BF(0.125)
        delta = jnp.sum(grads.astype(F32) * ot[rows, :].astype(F32), axis=0, keepdims=True)
        probs = jnp.exp(tn(keys, queries) + bias[...] - lse[pl.ds(h, 1), :])
        dscores = (probs * (tn(vt[rows, :], grads) - delta)).astype(BF)
        dvt[rows, :] = nt(grads, probs.astype(BF)).astype(BF)
        dkt[rows, :] = nt(queries, dscores).astype(BF)
        dqt[rows, :] = (nn(keys, dscores) * 0.125).astype(BF)
        return carry

    if pause is None:
        lax.fori_loop(0, HEADS, head, 0, unroll=4)
    else:
        def half(i, carry):
            lax.fori_loop(4 * i, 4 * i + 4, head, 0, unroll=True)
            pause()
            return carry

        lax.fori_loop(0, HEADS // 4, half, 0)


GAIN, SHIFT, B2, B1 = 0, 3, 6, 7


def column(vec, index):
    return vec[:, index : index + 1]


def self_column(vec, first, row):
    return jnp.where(first, column(vec, row + 1), column(vec, row))


def add_column(dvec, index, acc):
    dvec[:, index : index + 1] += jnp.sum(acc, axis=1, keepdims=True)


def self_forward(x, sq, vec, first, length, ut, n0, r0, qt, kt, vt, ot, lse, n1, r1, y, bias, et, pair, pause):
    tokens = x.shape[0]
    et[...] = x[...].astype(F32).T

    def entry(lanes):
        value = et[:, lanes]
        normed, inv = norm_parts(value)
        n0[:, lanes] = normed.astype(BF)
        r0[:, lanes] = inv
        value = jnp.where(first, normed * column(vec, GAIN) + column(vec, SHIFT), value)
        et[:, lanes] = value
        ut[:, lanes] = value.astype(BF)

    lane_loop(tokens, entry)
    fill_bias(bias, length, jnp.logical_not(first))
    for index, out in enumerate((qt, kt, vt)):
        out[...] = tn(sq[index][...], ut[...]).astype(BF)
    pause()
    attend(qt, kt, vt, bias, ot, lse, pair, pause)
    pause()
    et[...] += tn(sq[3][...], ot[...])
    gain, shift = self_column(vec, first, GAIN), self_column(vec, first, SHIFT)

    def leave(lanes):
        normed, inv = norm_parts(et[:, lanes])
        n1[:, lanes] = normed.astype(BF)
        r1[:, lanes] = inv
        y[:, lanes] = normed * gain + shift

    lane_loop(tokens, leave)


def self_backward(
    dy, sq, vec, first, length, ut, n0, r0, qt, kt, vt, ot, lse, n1, r1, dx,
    bias, dsa, dot, dqt, dkt, dvt, dsq, dvec, vacc, pause,
):
    tokens = dy.shape[1]
    vacc[...] = jnp.zeros(vacc.shape, F32)
    gain = self_column(vec, first, GAIN)

    def leave(lanes):
        grad, normed = dy[:, lanes], n1[:, lanes].astype(F32)
        vacc[2] += grad * normed
        vacc[3] += grad
        grad = norm_grad(grad, normed, r1[:, lanes], gain)
        dy[:, lanes] = grad
        dsa[:, lanes] = grad.astype(BF)

    lane_loop(tokens, leave)
    fill_bias(bias, length, jnp.logical_not(first))
    dot[...] = nn(sq[3][...], dsa[...]).astype(BF)
    dsq[3] += nt(ot[...], dsa[...])
    pause()
    attend_back(qt, kt, vt, bias, ot, lse, dot, dqt, dkt, dvt, pause)
    for index, grad in enumerate((dqt, dkt, dvt)):
        dsq[index] += nt(ut[...], grad[...])
        dy[...] += nn(sq[index][...], grad[...])
    pause()
    entry_gain = column(vec, GAIN)

    def entry(lanes):
        grad, normed = dy[:, lanes], n0[:, lanes].astype(F32)
        vacc[0] += grad * normed
        vacc[1] += grad
        dy[:, lanes] = jnp.where(first, norm_grad(grad, normed, r0[:, lanes], entry_gain), grad)

    lane_loop(tokens, entry)
    dx[...] = dy[...].T

    @pl.when(first)
    def _():
        add_column(dvec, GAIN, vacc[0])
        add_column(dvec, SHIFT, vacc[1])
        add_column(dvec, GAIN + 1, vacc[2])
        add_column(dvec, SHIFT + 1, vacc[3])

    @pl.when(jnp.logical_not(first))
    def _():
        add_column(dvec, GAIN, vacc[2])
        add_column(dvec, SHIFT, vacc[3])


def gelu_parts(z):
    root = 0.7978845608028654
    square = z * z
    t = jnp.tanh(z * (root + (root * 0.044715) * square))
    half = 0.5 + 0.5 * t
    act = z * half
    slope = half + act * (1.0 - t) * (root + (3.0 * root * 0.044715) * square)
    return act, slope


def feed_forward(h, units, vec, hb, act, slope, n2, r2, out):
    hb[...] = h[...].astype(BF)
    for c in range(RU):
        rows = slice(c * D, (c + 1) * D)
        a, s = gelu_parts(tn(units[c][...], hb[...]) + column(vec, B1 + c))
        act[rows, :] = a.astype(BF)
        slope[rows, :] = s.astype(BF)
    for c in range(RU):
        rows = slice(c * D, (c + 1) * D)
        h[...] += tn(units[RU + c][...], act[rows, :])

    def leave(lanes):
        normed, inv = norm_parts(h[:, lanes] + column(vec, B2))
        n2[:, lanes] = normed.astype(BF)
        r2[:, lanes] = inv
        out[:, lanes] = normed * column(vec, GAIN + 2) + column(vec, SHIFT + 2)

    lane_loop(h.shape[1], leave)


def feed_backward(dm, units, vec, hb, act, slope, n2, r2, dfb, dz, dunits, dvec, vacc):
    vacc[...] = jnp.zeros(vacc.shape, F32)

    def leave(lanes):
        grad, normed = dm[:, lanes], n2[:, lanes].astype(F32)
        vacc[RU + 1] += grad * normed
        vacc[RU + 2] += grad
        grad = norm_grad(grad, normed, r2[:, lanes], column(vec, GAIN + 2))
        dm[:, lanes] = grad
        short = grad.astype(BF)
        vacc[RU] += short.astype(F32)
        dfb[:, lanes] = short

    lane_loop(dm.shape[1], leave)
    for c in range(RU):
        rows = slice(c * D, (c + 1) * D)
        dz[rows, :] = (nn(units[RU + c][...], dfb[...]) * slope[rows, :].astype(F32)).astype(BF)
        dunits[RU + c][...] += nt(act[rows, :], dfb[...])
    for c in range(RU):
        rows = slice(c * D, (c + 1) * D)
        dm[...] += nn(units[c][...], dz[rows, :])
        dunits[c][...] += nt(hb[...], dz[rows, :])
        for lanes in range(0, dm.shape[1], LANES):
            vacc[c] += dz[rows, lanes : lanes + LANES].astype(F32)
    for index in range(RU):
        add_column(dvec, B1 + index, vacc[index])
    add_column(dvec, B2, vacc[RU])
    add_column(dvec, GAIN + 2, vacc[RU + 1])
    add_column(dvec, SHIFT + 2, vacc[RU + 2])


def cross_forward(a, sq, vec, length, ab, cqt, kt, vt, ot, lse, n1, r1, bias, pair):
    ab[...] = a[...].astype(BF)
    cqt[...] = tn(sq[0][...], ab[...]).astype(BF)
    fill_bias(bias, length, None)
    attend(cqt, kt, vt, bias, ot, lse, pair)
    a[...] += tn(sq[1][...], ot[...])

    def leave(lanes):
        normed, inv = norm_parts(a[:, lanes])
        n1[:, lanes] = normed.astype(BF)
        r1[:, lanes] = inv
        a[:, lanes] = normed * column(vec, GAIN + 1) + column(vec, SHIFT + 1)

    lane_loop(a.shape[1], leave)


def cross_backward(
    dbq, sq, vec, ab, cqt, kt, vt, ot, lse, n1, r1, bias, dca, dot, dqt, dkt, dvt, dsq, dvec, vacc
):
    vacc[0] = jnp.zeros(vacc.shape[1:], F32)
    vacc[1] = jnp.zeros(vacc.shape[1:], F32)

    def leave(lanes):
        grad, normed = dbq[:, lanes], n1[:, lanes].astype(F32)
        vacc[0] += grad * normed
        vacc[1] += grad
        grad = norm_grad(grad, normed, r1[:, lanes], column(vec, GAIN + 1))
        dbq[:, lanes] = grad
        dca[:, lanes] = grad.astype(BF)

    lane_loop(dbq.shape[1], leave)
    dot[...] = nn(sq[1][...], dca[...]).astype(BF)
    dsq[1][...] += nt(ot[...], dca[...])
    attend_back(cqt, kt, vt, bias, ot, lse, dot, dqt, dkt, dvt)
    dsq[0][...] += nt(ab[...], dqt[...])
    dbq[...] += nn(sq[0][...], dqt[...])
    add_column(dvec, GAIN + 1, vacc[0])
    add_column(dvec, SHIFT + 1, vacc[1])


SUB = 256
HOP = 3
HALF = SUB // 2
QUART = SUB // 4
UNITS = 6 + 2 * RU
VEC_ROWS = 256
SUBS = (UNITS * D + VEC_ROWS) // SUB
MESH = pl.DeviceIdType.MESH


class Total:
    def __init__(self, n_dp, order, shorts, other, mine, out, core_in, half, x_in, right_in, left_in, passed, sems):
        self.length = n_dp // 4
        self.last = self.length - 1
        self.section = lax.axis_index("section")
        self.dp = lax.axis_index("dp")
        self.core, self.x, self.z = self.dp % 2, (self.dp // 2) % 2, self.dp // 4
        self.sibling, self.beside = self.dp + 1 - 2 * self.core, self.dp + 2 - 4 * self.x
        self.has_left, self.has_right = self.z > 0, self.z < self.last
        self.order, self.shorts, self.other, self.mine = order, shorts, other, mine
        self.out, self.core_in, self.half, self.x_in = out, core_in, half, x_in
        self.right_in, self.left_in, self.passed, self.sems = right_in, left_in, passed, sems
        far = self.last
        self.ticks = SUBS + HOP * (2 + far + far) + 1

    def greet(self):
        barrier = pltpu.get_barrier_semaphore()

        def signal(index):
            pl.semaphore_signal(barrier, inc=1, device_id=(self.section, index), device_id_type=MESH)

        signal(self.sibling)
        signal(self.beside)
        pl.when(self.has_left)(lambda: signal(self.dp - 4))
        pl.when(self.has_right)(lambda: signal(self.dp + 4))
        pl.semaphore_wait(barrier, 2 + self.has_left.astype(jnp.int32) + self.has_right.astype(jnp.int32))

    def short_route(self, t):
        return ((t & 1) == 0) | ((t >= self.shorts[0]) & (t < self.shorts[1]))

    def home(self, t):
        return (t >> 1) & self.last

    def place(self, t, start, size):
        return pl.ds(pl.multiple_of(self.order(t) * SUB + start, QUART), size)

    def send(self, step, t, source, target, index):
        return pltpu.make_async_remote_copy(
            src_ref=source,
            dst_ref=target,
            send_sem=self.sems.at[0, step, t],
            recv_sem=self.sems.at[1, step, t],
            device_id=(self.section, index),
            device_id_type=MESH,
        )

    def part(self, size, index):
        return pl.ds(pl.multiple_of(index * size, size), size)

    def copy_core(self, t):
        source = self.other(t, self.order(t), HALF * (1 - self.core))
        return self.send(0, t, source, self.core_in.at[t], self.sibling)

    def copy_x(self, t):
        rows = self.part(QUART, 1 - self.x)
        return self.send(1, t, self.half.at[t, rows], self.x_in.at[t, pl.ds(0, QUART)], self.beside)

    def copy_x_whole(self, t):
        return self.send(1, t, self.passed.at[t], self.x_in.at[t], self.beside)

    def copy_right(self, t, source):
        return self.send(2, t, source, self.right_in.at[t, pl.ds(0, QUART)], self.dp + 4)

    def copy_left(self, t, source):
        return self.send(3, t, source, self.left_in.at[t, pl.ds(0, QUART)], self.dp - 4)

    def copy_right_whole(self, t, source):
        return self.send(2, t, source, self.right_in.at[t], self.dp + 4)

    def copy_left_whole(self, t, source):
        return self.send(3, t, source, self.left_in.at[t], self.dp - 4)

    def copy_back_x(self, t):
        place = self.place(t, HALF * self.core + QUART * self.x, QUART)
        return self.send(4, t, self.out.at[place], self.out.at[place], self.beside)

    def copy_back_core(self, t):
        place = self.place(t, HALF * self.core, HALF)
        return self.send(5, t, self.out.at[place], self.out.at[place], self.sibling)

    def copy_back_right(self, t):
        place = self.place(t, HALF * self.core, HALF)
        return self.send(4, t, self.out.at[place], self.out.at[place], self.dp + 4)

    def copy_back_left(self, t):
        place = self.place(t, HALF * self.core, HALF)
        return self.send(6, t, self.out.at[place], self.out.at[place], self.dp - 4)

    def add(self, one, two):
        return one + two

    def own_quarter(self, t):
        return self.half.at[t, self.part(QUART, self.x)]

    def short_core(self, t):
        self.copy_core(t).wait_recv()
        self.half[t] = self.add(self.mine(t, self.order(t), HALF * self.core), self.core_in[t])
        self.copy_x(t).start()

    def short_x(self, t):
        self.copy_x(t).wait_recv()
        quart = self.own_quarter(t)
        quart[...] = self.add(quart[...], self.x_in[t, 0:QUART])

        @pl.when(jnp.logical_not(self.has_left) & self.has_right)
        def _():
            self.copy_right(t, quart).start()

        @pl.when(jnp.logical_not(self.has_right) & self.has_left)
        def _():
            self.copy_left(t, quart).start()

    def short_right(self, t):
        @pl.when(self.has_left)
        def _():
            target = self.passed.at[t, pl.ds(0, QUART)]
            self.copy_right(t, target).wait_recv()

            @pl.when(self.has_right)
            def _():
                target[...] = self.add(self.own_quarter(t)[...], self.right_in[t, 0:QUART])
                self.copy_right(t, target).start()

    def short_left(self, t):
        @pl.when(self.has_right)
        def _():
            target = self.passed.at[t, pl.ds(QUART, QUART)]
            self.copy_left(t, target).wait_recv()

            @pl.when(self.has_left)
            def _():
                target[...] = self.add(self.own_quarter(t)[...], self.left_in[t, 0:QUART])
                self.copy_left(t, target).start()

    def short_total(self, t):
        total = self.own_quarter(t)[...].astype(F32)
        total += jnp.where(self.has_left, self.right_in[t, 0:QUART].astype(F32), 0.0)
        total += jnp.where(self.has_right, self.left_in[t, 0:QUART].astype(F32), 0.0)
        self.out[self.place(t, HALF * self.core + QUART * self.x, QUART), :] = total.astype(BF)
        self.copy_back_x(t).start()

    def short_back(self, t):
        self.copy_back_x(t).wait_recv()
        self.copy_back_core(t).start()

    def long_core(self, t):
        self.copy_core(t).wait_recv()
        self.half[t] = self.add(self.mine(t, self.order(t), HALF * self.core), self.core_in[t])
        home = self.home(t)

        @pl.when(jnp.logical_not(self.has_left) & (home > 0))
        def _():
            self.copy_right_whole(t, self.half.at[t]).start()

        @pl.when(jnp.logical_not(self.has_right) & (home < self.last))
        def _():
            self.copy_left_whole(t, self.half.at[t]).start()

    def long_right(self, t):
        @pl.when(self.has_left & (self.z < self.home(t)))
        def _():
            self.copy_right_whole(t, self.passed.at[t]).wait_recv()
            self.passed[t] = self.add(self.half[t], self.right_in[t])
            self.copy_right_whole(t, self.passed.at[t]).start()

    def long_left(self, t):
        @pl.when(self.has_right & (self.z > self.home(t)))
        def _():
            self.copy_left_whole(t, self.passed.at[t]).wait_recv()
            self.passed[t] = self.add(self.half[t], self.left_in[t])
            self.copy_left_whole(t, self.passed.at[t]).start()

    def long_home(self, t):
        @pl.when(self.z == self.home(t))
        def _():
            pl.when(self.has_left)(lambda: self.copy_right_whole(t, self.half.at[t]).wait_recv())
            pl.when(self.has_right)(lambda: self.copy_left_whole(t, self.half.at[t]).wait_recv())
            total = self.half[t].astype(F32)
            total += jnp.where(self.has_left, self.right_in[t].astype(F32), 0.0)
            total += jnp.where(self.has_right, self.left_in[t].astype(F32), 0.0)
            self.passed[t] = total.astype(BF)
            self.copy_x_whole(t).start()

    def long_x(self, t):
        @pl.when(self.z == self.home(t))
        def _():
            self.copy_x_whole(t).wait_recv()
            self.out[self.place(t, HALF * self.core, HALF), :] = self.add(self.passed[t], self.x_in[t])
            pl.when(self.has_left)(lambda: self.copy_back_left(t).start())
            pl.when(self.has_right)(lambda: self.copy_back_right(t).start())
            self.copy_back_core(t).start()

    def long_back(self, t):
        home = self.home(t)

        @pl.when(self.z > home)
        def _():
            self.copy_back_right(t).wait_recv()
            pl.when(self.has_right)(lambda: self.copy_back_right(t).start())

        @pl.when(self.z < home)
        def _():
            self.copy_back_left(t).wait_recv()
            pl.when(self.has_left)(lambda: self.copy_back_left(t).start())

        pl.when(self.z != home)(lambda: self.copy_back_core(t).start())

    def tick(self, now, prepare):
        z, last = self.z, self.last
        far = jnp.maximum(z, last - z)
        prepared = now

        @pl.when(prepared < SUBS)
        def _():
            prepare(prepared)
            self.copy_core(prepared).start()

        def due(step, lag, short):
            t = now - HOP * lag
            fits = (t >= 0) & (t < SUBS)
            kind = self.short_route(t) if short else jnp.logical_not(self.short_route(t))
            pl.when(fits & kind)(lambda: step(t))

        due(self.short_core, 1, True)
        due(self.short_x, 2, True)
        due(self.short_right, 2 + z, True)
        due(self.short_left, 2 + last - z, True)
        due(self.short_total, 2 + far, True)
        due(self.short_back, 3 + far, True)
        due(self.long_core, 1, False)
        due(self.long_right, 1 + z, False)
        due(self.long_left, 1 + last - z, False)
        due(self.long_home, 1 + far, False)
        due(self.long_x, 2 + far, False)
        for home in range(self.length):
            lag = 2 + max(home, last - home) + jnp.abs(z - home)
            t = now - HOP * lag
            fits = (t >= 0) & (t < SUBS) & jnp.logical_not(self.short_route(t)) & (self.home(t) == home)
            pl.when(fits & (z != home))(lambda t=t: self.long_back(t))

    def arrive(self, t):
        self.copy_back_core(t).wait_recv()

    def settle(self, t):
        self.copy_core(t).wait_send()
        self.copy_back_core(t).wait_send()
        home = self.home(t)

        @pl.when(self.short_route(t))
        def _():
            self.copy_x(t).wait_send()
            pl.when(self.has_right)(lambda: self.copy_right(t, self.own_quarter(t)).wait_send())
            pl.when(self.has_left)(lambda: self.copy_left(t, self.own_quarter(t)).wait_send())
            self.copy_back_x(t).wait_send()

        @pl.when(jnp.logical_not(self.short_route(t)))
        def _():
            pl.when(self.z < home)(lambda: self.copy_right_whole(t, self.half.at[t]).wait_send())
            pl.when(self.z > home)(lambda: self.copy_left_whole(t, self.half.at[t]).wait_send())
            pl.when(self.z == home)(lambda: self.copy_x_whole(t).wait_send())
            pl.when(self.has_right & (self.z >= home))(lambda: self.copy_back_right(t).wait_send())
            pl.when(self.has_left & (self.z <= home))(lambda: self.copy_back_left(t).wait_send())


def loop(start, stop, body):
    def step(i, carry):
        body(i)
        return carry

    lax.fori_loop(start, stop, step, 0)


def total_scratch():
    return [pltpu.VMEM((SUBS, HALF, D), BF)] * 6 + [pltpu.SemaphoreType.DMA((2, 7, SUBS))]


def any_space():
    return pl.BlockSpec(memory_space=pl.ANY)


def vmem_space():
    return pl.BlockSpec(memory_space=pltpu.VMEM)


def smem_space():
    return pl.BlockSpec(memory_space=pltpu.SMEM)


def block_spec(*dims):
    return pl.BlockSpec((1,) + dims, lambda b, info: (b,) + (0,) * len(dims))


def shape32(*dims):
    return jax.ShapeDtypeStruct(dims, F32)


def shape16(*dims):
    return jax.ShapeDtypeStruct(dims, BF)


TENSOR_OF = (0, 1, 2, 3, 4, 5) + (6,) * RU + (7,) * RU
TENSOR_SIZE = (1,) * 6 + (RU, RU)
FIRST_UNIT = (0, 1, 2, 3, 4, 5, 6, 6 + RU)
VEC_BLOCKS = VEC_ROWS // SUB
EARLY = 4 * D // SUB + VEC_BLOCKS
PIECE = 16


def copies(sources, targets, sems):
    return [pltpu.make_async_copy(s, t, sems.at[i]) for i, (s, t) in enumerate(zip(sources, targets))]


def slot_of(owners, tensor):
    prior = jnp.int32(0)
    for earlier in range(tensor):
        prior += jnp.where(owners[0, earlier] == owners[0, tensor], TENSOR_SIZE[earlier], 0)
    return prior


def start_kernel(n_dp, info, owners, x, slots, pack, out, vec, *refs):
    saved_out, (y_out, stage, *comm), refs = refs[:10], refs[10:19], refs[19:]
    saved, (y, xb, bias, et, pair, places, counter, sems) = refs[:10], refs[10:]
    count, tokens = saved_out[0].shape[0], saved_out[0].shape[2]
    first = lax.axis_index("section") == 0
    dp = lax.axis_index("dp")
    for unit in range(UNITS):
        tensor = TENSOR_OF[unit]
        slot = jnp.minimum(slot_of(owners, tensor) + (unit - FIRST_UNIT[tensor]), slots.shape[0] - 1)
        places[0, unit] = slot
        places[1, unit] = (owners[0, tensor] == dp).astype(jnp.int32)

    def own(block, start):
        is_pack = block >= SUBS - VEC_BLOCKS
        unit = jnp.minimum(block * SUB // D, UNITS - 1)
        at = pl.multiple_of((block * SUB) % D + start, HALF)
        value = jnp.where(places[1, unit] == 1, slots[places[0, unit], pl.ds(at, HALF), :], 0.0).astype(BF)
        return jnp.where(is_pack, pack[pl.ds(pl.multiple_of(start, HALF), HALF), :], value)

    def order(t):
        return jnp.where(t < VEC_BLOCKS, t + SUBS - VEC_BLOCKS, t - VEC_BLOCKS)

    total = Total(
        n_dp,
        order,
        (0, EARLY),
        lambda t, block, start: stage.at[t],
        lambda t, block, start: own(block, start),
        out,
        *comm,
    )

    def prepare(t):
        stage[t] = own(order(t), HALF * (1 - total.core))

    def run(ticks):
        begin = counter[0]
        stop = jnp.minimum(begin + ticks, total.ticks)
        loop(begin, stop, lambda now: total.tick(now, prepare))
        counter[0] = stop

    total.greet()
    counter[0] = 0
    run(EARLY + HOP * (3 + total.last))
    loop(0, EARLY, total.arrive)
    rows = [out[pl.ds(UNITS * D + i * PIECE, PIECE), :].astype(F32) for i in range(3)]
    whole = jnp.concatenate([rows[0] + rows[1] + rows[2], jnp.zeros((LANES - PIECE, D), F32)], axis=0)
    vec[...] = whole.T
    squares = [out.at[pl.ds(i * D, D)] for i in range(4)]

    def outward(b):
        return copies(saved + (y,), [ref.at[b] for ref in saved_out + (y_out,)], sems)

    def block(b):
        load = pltpu.make_async_copy(x.at[pl.ds(pl.multiple_of(b * tokens, tokens), tokens)], xb, sems.at[11])
        load.start()

        @pl.when(b > 0)
        def _():
            for copy in outward(b - 1):
                copy.wait()

        load.wait()
        self_forward(
            xb, squares, vec, first, info[1 + b], *saved, y, bias, et, pair, lambda: run(2)
        )
        for copy in outward(b):
            copy.start()
        run(1)

    loop(0, count, block)
    run(total.ticks)
    for copy in outward(count - 1):
        copy.wait()
    loop(EARLY, SUBS, total.arrive)
    loop(0, SUBS, total.settle)


def saved_dims(tokens):
    wide, row = ((D, tokens), BF), ((1, tokens), F32)
    return [wide, wide, row, wide, wide, wide, wide, ((HEADS, tokens), F32), wide, row]


def call_start(n_dp, info, owners, x, slots, pack, count):
    tokens = x.shape[0] // count
    kept = saved_dims(tokens)
    scores = pltpu.VMEM((tokens, tokens), F32)
    return pl.pallas_call(
        functools.partial(start_kernel, n_dp),
        name="start",
        out_shape=[shape16(SUBS * SUB, D), shape32(D, LANES)]
        + [jax.ShapeDtypeStruct((count,) + dims, kind) for dims, kind in kept]
        + [shape32(count, D, tokens)],
        in_specs=[smem_space(), smem_space(), any_space(), vmem_space(), vmem_space()],
        out_specs=[vmem_space(), vmem_space()] + [any_space()] * 11,
        scratch_shapes=[pltpu.VMEM((SUBS, HALF, D), BF)]
        + total_scratch()
        + [pltpu.VMEM(dims, kind) for dims, kind in kept]
        + [
            pltpu.VMEM((D, tokens), F32),
            pltpu.VMEM((tokens, D), BF),
            scores,
            pltpu.VMEM((D, tokens), F32),
            pltpu.VMEM((2, tokens, tokens), F32),
            pltpu.SMEM((2, UNITS), jnp.int32),
            pltpu.SMEM((1,), jnp.int32),
            pltpu.SemaphoreType.DMA((12,)),
        ],
        compiler_params=pltpu.CompilerParams(
            collective_id=0, has_side_effects=True, vmem_limit_bytes=60 * 2**20
        ),
    )(info, owners, x, slots, pack)


def finish_kernel(n_dp, info, dy, sq, vec, late, late_vec, *refs):
    saved_in, (dx_out, out), (stage, *comm), refs = refs[:10], refs[10:12], refs[12:20], refs[20:]
    saved, (dys, dx, bias, dsa, dot, dqt, dkt, dvt, dsq, dvec, vacc, pack, counter, sems) = refs[:10], refs[10:]
    count, tokens = dy.shape[0], dy.shape[2]
    first = lax.axis_index("section") == 0
    early = EARLY - VEC_BLOCKS
    others = SUBS - EARLY

    def order(t):
        return jnp.where(t < others, t + early, jnp.where(t < SUBS - VEC_BLOCKS, t - others, t))

    def late_rows(block, start):
        return pl.ds(pl.multiple_of((block - early) * SUB + start, HALF), HALF)

    def own_early(block, start):
        unit = jnp.minimum(block * SUB // D, 3)
        at = pl.multiple_of((block * SUB) % D + start, HALF)
        value = dsq[unit, pl.ds(at, HALF), :].astype(BF)
        return jnp.where(block >= SUBS - VEC_BLOCKS, pack[pl.ds(pl.multiple_of(start, HALF), HALF), :], value)

    def mine(t, block, start):
        at = jnp.clip((block - early) * SUB, 0, (others - 1) * SUB) + start
        return jnp.where(t < others, late[pl.ds(pl.multiple_of(at, HALF), HALF), :], own_early(block, start))

    total = Total(
        n_dp, order, (others, SUBS), lambda t, block, start: stage.at[t], mine, out, *comm
    )

    def prepare(t):
        stage[t] = mine(t, order(t), HALF * (1 - total.core))

    def run(ticks, end):
        begin = counter[0]
        stop = jnp.minimum(begin + ticks, end)
        loop(begin, stop, lambda now: total.tick(now, prepare))
        counter[0] = stop

    total.greet()
    counter[0] = 0
    dsq[...] = jnp.zeros(dsq.shape, F32)
    dvec[...] = late_vec[...]
    squares = [sq.at[pl.ds(i * D, D)] for i in range(4)]

    def block(b):
        loads = copies([ref.at[b] for ref in saved_in] + [dy.at[b]], saved + (dys,), sems)
        for copy in loads:
            copy.start()
        run(1, others)
        store = pltpu.make_async_copy(
            dx, dx_out.at[pl.ds(pl.multiple_of(b * tokens, tokens), tokens)], sems.at[11]
        )
        pl.when(b > 0)(lambda: store.wait())
        for copy in loads:
            copy.wait()
        self_backward(
            dys, squares, vec, first, info[1 + b], *saved, dx,
            bias, dsa, dot, dqt, dkt, dvt, dsq, dvec, vacc, lambda: run(1, others),
        )
        store.start()

    loop(0, count, block)
    value = dvec[...].T[:PIECE]
    high = value.astype(BF)
    rest = value - high.astype(F32)
    mid = rest.astype(BF)
    pack[...] = jnp.zeros(pack.shape, BF)
    pack[0:PIECE, :] = high
    pack[PIECE : 2 * PIECE, :] = mid
    pack[2 * PIECE : 3 * PIECE, :] = (rest - mid.astype(F32)).astype(BF)
    run(total.ticks, total.ticks)
    pltpu.make_async_copy(dx, dx_out.at[pl.ds(0, tokens)], sems.at[11]).wait()
    loop(0, SUBS, total.arrive)
    loop(0, SUBS, total.settle)


def call_finish(n_dp, info, dy, weights, vec, late, late_vec, saved):
    count, tokens = dy.shape[0], dy.shape[2]
    kept = saved_dims(tokens)
    wide16 = pltpu.VMEM((D, tokens), BF)
    wide32 = pltpu.VMEM((D, tokens), F32)
    return pl.pallas_call(
        functools.partial(finish_kernel, n_dp),
        name="finish",
        out_shape=[shape32(count * tokens, D), shape16(SUBS * SUB, D)],
        grid=(1,),
        in_specs=[
            smem_space(),
            any_space(),
            pl.BlockSpec((4 * D, D), lambda i: (0, 0)),
            vmem_space(),
            vmem_space(),
            vmem_space(),
        ]
        + [any_space()] * 10,
        out_specs=[any_space(), vmem_space()],
        scratch_shapes=[pltpu.VMEM((SUBS, HALF, D), BF)]
        + total_scratch()
        + [pltpu.VMEM(dims, kind) for dims, kind in kept]
        + [wide32, pltpu.VMEM((tokens, D), F32), pltpu.VMEM((tokens, tokens), F32)]
        + [wide16] * 5
        + [
            pltpu.VMEM((4, D, D), F32),
            pltpu.VMEM((D, LANES), F32),
            pltpu.VMEM((4, D, LANES), F32),
            pltpu.VMEM((VEC_ROWS, D), BF),
            pltpu.SMEM((1,), jnp.int32),
            pltpu.SemaphoreType.DMA((12,)),
        ],
        compiler_params=pltpu.CompilerParams(
            collective_id=2, has_side_effects=True, vmem_limit_bytes=60 * 2**20
        ),
    )(info, dy, weights, vec, late, late_vec, *saved)


def middle_kernel(
    info, vec, y, cot, weights, hidden, dy, grads, dvec,
    wts, acc, sent, got, h, mem, hb, act, slope, n2, r2, dfb, dz, vacc,
    ab, cqt, kt, vt, ot, lse, n1, r1, bias, dca, dot, dqt, pair, tok, stage, sems, load_sem,
):
    section = lax.axis_index("section")
    dp = lax.axis_index("dp")
    count, tokens = y.shape[0], y.shape[2]
    other = 1 - section
    barrier = pltpu.get_barrier_semaphore()
    pl.semaphore_signal(barrier, inc=1, device_id=(other, dp), device_id_type=MESH)
    pl.semaphore_wait(barrier, 1)

    def move(source, target):
        copy = pltpu.make_async_copy(source, target, load_sem)
        copy.start()
        copy.wait()

    def swap(b):
        return pltpu.make_async_remote_copy(
            src_ref=sent.at[b],
            dst_ref=got.at[b],
            send_sem=sems.at[0, b],
            recv_sem=sems.at[1, b],
            device_id=(other, dp),
            device_id_type=MESH,
        )

    def each(body):
        def step(b, carry):
            body(b)
            return carry

        lax.fori_loop(0, count, step, 0)

    move(weights.at[pl.ds(4 * D, 10 * D)], wts)
    unit = [wts.at[pl.ds(i * D, D)] for i in range(10)]
    s4, s5, ffn = unit[0], unit[1], unit[2:]
    acc[...] = jnp.zeros(acc.shape, F32)
    dvec[...] = jnp.zeros(dvec.shape, F32)
    cross_acc = [acc.at[i] for i in range(2)]
    ffn_acc = [acc.at[2 + i] for i in range(8)]

    def run_feed_forward():
        feed_forward(h, ffn, vec, hb, act, slope, n2, r2, mem)

    def emit_hidden(b):
        tok[...] = mem[...].T.astype(BF)
        move(tok, hidden.at[pl.ds(pl.multiple_of(b * tokens, tokens), tokens)])

    def load_cotangent(b):
        move(cot.at[pl.ds(pl.multiple_of(b * tokens, tokens), tokens)], tok)
        token = lax.broadcasted_iota(jnp.int32, (D, tokens), 1)
        h[...] = jnp.where(token < info[1 + b], tok[...].astype(F32).T, 0.0)

    def run_feed_backward():
        feed_backward(h, ffn, vec, hb, act, slope, n2, r2, dfb, dz, ffn_acc, dvec, vacc)

    @pl.when(section == 0)
    def _():
        def ahead(b):
            move(y.at[b], h)
            run_feed_forward()
            emit_hidden(b)
            short = mem[...].astype(BF)
            sent[b, 0] = tn(s4[...], short).astype(BF)
            sent[b, 1] = tn(s5[...], short).astype(BF)
            swap(b).start()

        each(ahead)

        def back(b):
            move(y.at[b], h)
            run_feed_forward()
            ab[...] = mem[...].astype(BF)
            load_cotangent(b)
            swap(b).wait_recv()
            for i, matrix in enumerate((s4, s5)):
                h[...] += nn(matrix[...], got[b, i])
                acc[i] += nt(ab[...], got[b, i])
            run_feed_backward()
            move(h, dy.at[b])

        each(back)

    @pl.when(section == 1)
    def _():
        def both(b):
            move(y.at[b], h)
            swap(b).wait_recv()
            kt[...] = got[b, 0]
            vt[...] = got[b, 1]
            cross_forward(h, (s4, s5), vec, info[1 + count + b], ab, cqt, kt, vt, ot, lse, n1, r1, bias, pair)
            run_feed_forward()
            emit_hidden(b)
            load_cotangent(b)
            run_feed_backward()
            cross_backward(
                h, (s4, s5), vec, ab, cqt, kt, vt, ot, lse, n1, r1, bias, dca, dot, dqt,
                sent.at[b, 0], sent.at[b, 1], cross_acc, dvec, vacc,
            )
            swap(b).start()
            move(h, dy.at[b])

        each(both)

    def finish(b):
        swap(b).wait_send()

    each(finish)
    for i in range(10):
        stage[...] = acc[i].astype(BF)
        move(stage, grads.at[pl.ds(i * D, D)])


def call_middle(info, vec, y, cot, weights, count, tokens):
    wide16 = pltpu.VMEM((D, tokens), BF)
    wide32 = pltpu.VMEM((D, tokens), F32)
    row = pltpu.VMEM((1, tokens), F32)
    return pl.pallas_call(
        middle_kernel,
        name="middle",
        out_shape=[
            shape16(count * tokens, D),
            shape32(count, D, tokens),
            shape16(10 * D, D),
            shape32(D, LANES),
        ],
        in_specs=[smem_space(), vmem_space(), any_space(), any_space(), any_space()],
        out_specs=[any_space(), any_space(), any_space(), vmem_space()],
        scratch_shapes=[
            pltpu.VMEM((10 * D, D), BF),
            pltpu.VMEM((10, D, D), F32),
            pltpu.VMEM((count, 2, D, tokens), BF),
            pltpu.VMEM((count, 2, D, tokens), BF),
            wide32, wide32, wide16,
            pltpu.VMEM((FF, tokens), BF), pltpu.VMEM((FF, tokens), BF),
            wide16, row, wide16,
            pltpu.VMEM((FF, tokens), BF),
            pltpu.VMEM((RU + 3, D, LANES), F32),
                wide16, wide16, wide16, wide16, wide16,
            pltpu.VMEM((HEADS, tokens), F32),
            wide16, row,
            pltpu.VMEM((tokens, tokens), F32),
            wide16, wide16, wide16,
            pltpu.VMEM((2, tokens, tokens), F32),
            pltpu.VMEM((tokens, D), BF),
            pltpu.VMEM((D, D), BF),
            pltpu.SemaphoreType.DMA((2, count)),
            pltpu.SemaphoreType.DMA,
        ],
        compiler_params=pltpu.CompilerParams(
            collective_id=1, has_side_effects=True, vmem_limit_bytes=60 * 2**20
        ),
    )(info, vec, y, cot, weights)


matrix_rate = 0.04
vector_rate = 0.25
matrix_decay = 0.01


def adam_update(weight, moment_old, square_old, gradient, learn_rate, decay_rate):
    moment_one = 0.5 * moment_old + 0.5 * gradient
    moment_two = 0.5 * square_old + 0.5 * gradient * gradient
    correction = 1.0 - 0.5**STEP
    adam_step = moment_one / correction / (jnp.sqrt(moment_two / correction) + 1e-08)
    return (weight - learn_rate * (adam_step + decay_rate * weight), moment_one, moment_two)


def adam_kernel(place, grad, weight, first, second, weight_out, first_out, second_out):
    taken = place[pl.program_id(0)] >= 0
    fresh = adam_update(weight[0], first[0], second[0], grad[...].astype(F32), matrix_rate, matrix_decay)
    for new, old, out in zip(fresh, (weight, first, second), (weight_out, first_out, second_out)):
        out[0] = jnp.where(taken, new, old[0])


def call_adam(place, grads, weight, first, second):
    slots = weight.shape[0]
    spec = block_spec(D, D)
    out = shape32(slots, D, D)
    return pl.pallas_call(
        adam_kernel,
        name="adam",
        out_shape=[out] * 3,
        grid_spec=pltpu.PrefetchScalarGridSpec(
            num_scalar_prefetch=1,
            grid=(slots,),
            in_specs=[pl.BlockSpec((D, D), lambda s, place: (jnp.maximum(place[s], 0), 0))] + [spec] * 3,
            out_specs=[spec] * 3,
        ),
    )(place, grads, weight, first, second)


def unit_tables(owner_row):
    tensor_of = np.array(TENSOR_OF)
    first_unit = np.array(FIRST_UNIT)
    owned_by = owner_row[:8]
    earlier = (owned_by[:, None] == owned_by[None, :]) & jnp.asarray(
        np.arange(8)[None, :] < np.arange(8)[:, None]
    )
    prior = jnp.sum(jnp.where(earlier, jnp.array(TENSOR_SIZE, jnp.int32)[None, :], 0), axis=1)
    unit_owner = owned_by[tensor_of]
    unit_slot = prior[tensor_of] + jnp.asarray(np.arange(UNITS) - first_unit[tensor_of], jnp.int32)
    return unit_owner, unit_slot.astype(jnp.int32)


def slot_units(owner_row, dp, slots):
    unit_owner, unit_slot = unit_tables(owner_row)
    hit = (unit_owner[None, :] == dp) & (unit_slot[None, :] == jnp.arange(slots, dtype=jnp.int32)[:, None])
    return jnp.sum(jnp.where(hit, jnp.arange(UNITS, dtype=jnp.int32)[None, :] + 1, 0), axis=1) - 1


def three_pieces(value):
    high = value.astype(BF)
    rest = value - high.astype(F32)
    mid = rest.astype(BF)
    low = (rest - mid.astype(F32)).astype(BF)
    pad = ((0, PIECE - value.shape[0]), (0, 0))
    parts = jnp.concatenate([jnp.pad(part, pad) for part in (high, mid, low)], axis=0)
    return jnp.pad(parts, ((0, VEC_ROWS - 3 * PIECE), (0, 0)))


def local(n_dp, tokens, cotangent, lengths, owners, master_sq, mom1_sq, mom2_sq, master_vec, mom1_vec, mom2_vec):
    section = lax.axis_index("section")
    dp = lax.axis_index("dp")
    count = lengths.shape[1]
    vec_store = master_vec[0, 0]
    vrows = vec_store.shape[0]
    owns_vector = owners[0, 8] == dp
    pack = three_pieces(jnp.where(owns_vector, vec_store, 0.0))
    own = jnp.where(section == 0, lengths[0], lengths[1])
    info = jnp.concatenate([section[None].astype(jnp.int32), own, lengths[0]])
    weights, vec, *saved = call_start(n_dp, info, owners, tokens[0], master_sq[0, 0], pack, count)
    width = tokens.shape[1] // count
    hidden, dy, late, late_vec = call_middle(info, vec, saved[10], cotangent[0], weights, count, width)
    dx, total = call_finish(n_dp, info, dy, weights, vec, late, late_vec, saved[:10])
    pieces = total[UNITS * D : UNITS * D + 3 * PIECE].astype(F32).reshape(3, PIECE, D)[:, :vrows]
    total_vector = pieces[0] + pieces[1] + pieces[2]
    place = slot_units(owners[0], dp, master_sq.shape[2])
    squares_new = call_adam(place, total, master_sq[0, 0], mom1_sq[0, 0], mom2_sq[0, 0])
    vector_new = adam_update(vec_store, mom1_vec[0, 0], mom2_vec[0, 0], total_vector, vector_rate, 0.0)
    vector_new = [
        jnp.where(owns_vector, new, old)
        for new, old in zip(vector_new, (vec_store, mom1_vec[0, 0], mom2_vec[0, 0]))
    ]
    return (
        hidden[None],
        dx[None],
        *[value[None, None] for value in squares_new],
        *[value[None, None] for value in vector_new],
    )


def solution(mesh):
    n_dp = mesh.shape["dp"]
    slots = P("section", "dp", None, None, None)
    packs = P("section", "dp", None, None)
    rows = P("section", "dp", None)
    return jax.shard_map(
        functools.partial(local, n_dp),
        mesh=mesh,
        in_specs=(rows, rows, P(None, "dp"), P("section", None), slots, slots, slots, packs, packs, packs),
        out_specs=(rows, rows, slots, slots, slots, packs, packs, packs),
        check_vma=False,
    )
```

time: 551 us -> 459 us (0.83)
  Pallas kernels: 521 us -> 442 us
  other arithmetic: 18.1 us -> 3.76 us
    pallas_call x4 -> x2, Pallas kernels: 315 us -> 253 us  [the longest x1 141 us: call_finish(): pl.pallas_call(functools.partial(finish_kernel, n_dp), name='finish', out...]
    pallas_call x1, Pallas kernels: 190 us -> 173 us  [call_middle(): pl.pallas_call(middle_kernel, name='middle', out_shape=[shape16(count * t...]
    concatenate x4 -> x1, other arithmetic: 7.73 us -> 0.01 us  [three_pieces(): jnp.concatenate([jnp.pad(part, pad) for part in (high, mid, low)], axis=0)]
where the time goes in v2:
time: 459 us; the launch traced here: 458 us
  Pallas kernels  442 us (96%)
  local copies, waits for them, and re-layouts  10.2 us (2%)
    pallas_call x1, Pallas kernels, call_middle(): pl.pallas_call(middle_kernel, name='middle', out_shape=[shape16(count * t...  173 us
    pallas_call x1, Pallas kernels, call_finish(): pl.pallas_call(functools.partial(finish_kernel, n_dp), name='finish', out...  141 us
    pallas_call x1, Pallas kernels, call_start(): pl.pallas_call(functools.partial(start_kernel, n_dp), name='start', out_s...  112 us
    pallas_call x1, Pallas kernels, call_adam(): pl.pallas_call(adam_kernel, name='adam', out_shape=[out] * 3, grid_spec=p...  16 us

profile of v2, /device:TPU:1, one launch (start us, length us, event | category | flops | bytes accessed | tf_op | source)
XLA Modules:
  0.0 457.7 jit_solution(9770480381284962801)
XLA Ops:
  0.6 0.7 slice_bitcast_fusion.1
  1.3 0.8 broadcast_select_fusion
  2.1 0.6 pad_add_fusion.info
  2.7 1.2 slice.34
  4.6 0.7 fusion.13
  5.3 0.7 fusion.9
  6.0 0.7 pad.17.pack
  6.8 111.6 %start.1 = (bf16[7424,512]{1,0:T(8,128)(2,1)}, f32[512,128]{1,0:T(8,128)}, bf16[4,512,512]{2,1,0:T(8,128)(2,1)}, bf16[4,512,512]{2,1,0:T(8,128)(2,1)}, f32[4,1,5...) custom-call(s32[9]{0:T(128)} %pad_add_fusion.info, ...), custom_call_target="tpu_custom_call" | custom-call | tf_op jit(solution)/shard_map/start/pallas_call | solution.py:746
  118.4 173.3 %middle.1 = (bf16[2048,512]{1,0:T(8,128)(2,1)}, f32[4,512,512]{2,1,0:T(8,128)}, bf16[5120,512]{1,0:T(8,128)(2,1)}, f32[512,128]{1,0:T(8,128)}) custom-call(s32[9]{0:T(128)} %pad_add_fusion.info, f32[512,128]{1,0:T(8,128)} %get-tuple-element.30.vec, f32[4,512,512]{2,1,0:T(8,128)} %get-tuple-element.31.y, bf16[2048,512]{1,0:T(8,128)(2,1)} %bitcast.48, ...), custom_call_target="tpu_custom_call" | custom-call | tf_op jit(solution)/shard_map/middle/pallas_call | solution.py:1006
  291.6 0.0 copy-start.6
  291.6 0.0 copy-start.5
  291.7 0.0 copy-start.8
  291.7 0.0 copy-start.7
  291.7 0.0 copy-start.9
  291.7 141.5 %finish.1 = (f32[2048,512]{1,0:T(8,128)}, bf16[7424,512]{1,0:T(8,128)(2,1)}) custom-call(s32[9]{0:T(128)} %pad_add_fusion.info, f32[4,512,512]{2,1,0:T(8,128)} %get-tuple-element.34.dy, bf16[7424,512]{1,0:T(8,128)(2,1)} %get-tuple-element.32.weights.sq, f32[512,128]{1,0:T(8,128)} %get-tuple-element.30.vec, bf16[5120,512]{1,0:T(8,128)(2,1)} %get-tuple-element.35.late, ...), custom_call_target="tpu_custom_call" | custom-call | tf_op jit(solution)/shard_map/finish/pallas_call | solution.py:853
  433.2 0.0 copy-done.6
  433.2 0.0 copy-done.5
  433.2 0.0 copy-done.8
  433.2 0.2 select_reduce_fusion.1
  433.4 0.0 copy-done.7
  433.4 0.7 gather_fusion.1
  434.1 0.7 gather_fusion
  434.8 0.1 select_reduce_fusion
  434.9 0.5 broadcast_add_fusion.place
  435.4 16.0 %adam.1 = (f32[6,512,512]{2,1,0:T(8,128)}, f32[6,512,512]{2,1,0:T(8,128)}, f32[6,512,512]{2,1,0:T(8,128)}) custom-call(s32[6]{0:T(128)} %broadcast_add_fusion.place, bf16[7424,512]{1,0:T(8,128)(2,1)} %get-tuple-element.48.grad, f32[6,512,512]{2,1,0:T(8,128)} %bitcast.42, f32[6,512,512]{2,1,0:T(8,128)} %bitcast.43, f32[6,512,512]{2,1,0:T(8,128)} %bitcast.44), custom_call_target="tpu_custom_call" | custom-call | tf_op jit(solution)/shard_map/adam/pallas_call | solution.py:1068
  451.4 1.0 slice.37
  452.5 0.6 copy.54
  453.1 0.6 copy.55
  453.7 0.6 copy.56
  454.4 1.3 copy.100
  455.7 0.0 copy-done
  455.7 2.0 copy.101
  (19 shorter events, 0.1 us)
Async XLA Ops:
  291.6 141.6 %copy-start.6 = (s32[1,9]{1,0:T(1,128)S(1)}, s32[1,9]{1,0:T(1,128)}, u32[]{:S(2)}) copy-start(s32[1,9]{1,0:T(1,128)} %owners.1) | copy-start | bytes 112
  291.6 141.6 %copy-start.5 = (pred[8,8]{1,0:T(8,128)(4,1)S(1)}, pred[8,8]{1,0:T(8,128)(4,1)}, u32[]{:S(2)}) copy-start(pred[8,8]{1,0:T(8,128)(4,1)} %constant.43.clone) | copy-start | bytes 196
  291.7 141.6 %copy-start.8 = (s32[8]{0:T(128)S(1)}, s32[8]{0:T(128)}, u32[]{:S(2)}) copy-start(s32[8]{0:T(128)} %constant.44.clone) | copy-start | bytes 100
  291.7 141.7 %copy-start.7 = (s32[14]{0:T(128)S(1)}, s32[14]{0:T(128)}, u32[]{:S(2)}) copy-start(s32[14]{0:T(128)} %constant.67) | copy-start | bytes 172
  291.7 142.4 %copy-start.9 = (s32[14]{0:T(128)S(1)}, s32[14]{0:T(128)}, u32[]{:S(2)}) copy-start(s32[14]{0:T(128)} %constant.47.clone) | copy-start | bytes 172
  435.4 16.9 %copy-start.3 = (f32[1,1,11,512]{3,1,2,0:T(1,128)S(1)}, f32[1,1,11,512]{3,1,2,0:T(1,128)}, u32[]{:S(2)}) copy-start(f32[1,1,11,512]{3,1,2,0:T(1,128)} %param.25) | copy-start | bytes 67588
  435.4 17.0 %copy-start.2 = (f32[1,1,11,512]{3,1,2,0:T(1,128)S(1)}, f32[1,1,11,512]{3,1,2,0:T(1,128)}, u32[]{:S(2)}) copy-start(f32[1,1,11,512]{3,1,2,0:T(1,128)} %param.23) | copy-start | bytes 67588
  435.4 17.0 %copy-start.4 = (f32[1,1,11,512]{3,1,2,0:T(1,128)S(1)}, f32[1,1,11,512]{3,1,2,0:T(1,128)}, u32[]{:S(2)}) copy-start(f32[1,1,11,512]{3,1,2,0:T(1,128)} %param.24) | copy-start | bytes 67588
  435.4 18.9 %copy-start.1 = (bf16[2048,512]{1,0:T(8,128)(2,1)S(1)}, bf16[2048,512]{1,0:T(8,128)(2,1)}, u32[]{:S(2)}) copy-start(bf16[2048,512]{1,0:T(8,128)(2,1)} %get-tuple-element.33) | copy-start | bytes 6291460
  451.4 4.3 copy-start

commit v3 on v2

--- a/solution.py
+++ b/solution.py
@@ -36,7 +36,7 @@
         body(pl.ds(pl.multiple_of(i * LANES, LANES), LANES))
         return carry
 
-    lax.fori_loop(0, count // LANES, step, 0)
+    lax.fori_loop(0, count // LANES, step, 0, unroll=True)
 
 
 def norm_parts(value):
@@ -53,12 +53,13 @@
     return (scaled - mean_one - normed * mean_two) * inv
 
 
-def fill_bias(bias, length, causal):
+def fill_bias(bias, length, causal, key_dim=0):
     rows = bias.shape[0]
 
     def body(lanes):
-        key = lax.broadcasted_iota(jnp.int32, (rows, LANES), 0)
-        query = lax.broadcasted_iota(jnp.int32, (rows, LANES), 1) + lanes.start
+        across = lax.broadcasted_iota(jnp.int32, (rows, LANES), 0)
+        along = lax.broadcasted_iota(jnp.int32, (rows, LANES), 1) + lanes.start
+        key, query = (across, along) if key_dim == 0 else (along, across)
         allowed = key < length
         if causal is not None:
             allowed = allowed & ((key <= query) | jnp.logical_not(causal))
@@ -71,17 +72,28 @@
     return pl.ds(pl.multiple_of(h * HS, HS), HS)
 
 
-def attend(qt, kt, vt, bias, ot, lse, pair, pause=None):
+def attend(qt, kt, vt, bias, length, ot, lse, pair):
+    width = kt.shape[1]
+    index = lax.broadcasted_iota(jnp.int32, (16, width), 0)
+    if bias is None:
+        masked = (index == 0) & (lax.broadcasted_iota(jnp.int32, index.shape, 1) >= length)
+        masks = jnp.where(masked, NEG, 0.0).astype(BF)
+        ones = jnp.where(index == 0, 1.0, 0.0).astype(BF)
+
     def score(h, out):
         rows = head_rows(h)
-        out[...] = tn(kt[rows, :], qt[rows, :] * BF(0.125))
+        keys, queries = kt[rows, :], qt[rows, :] * BF(0.125)
+        if bias is None:
+            keys = jnp.concatenate([keys, masks], axis=0)
+            queries = jnp.concatenate([queries, ones], axis=0)
+        out[...] = tn(keys, queries)
 
     def finish(h, scores):
         rows = head_rows(h)
-        biased = scores[...] + bias[...]
+        biased = scores[...] if bias is None else scores[...] + bias[...]
         top = jnp.max(biased, axis=0, keepdims=True)
         weights = jnp.exp(biased - top).astype(BF)
-        values = jnp.concatenate([vt[rows, :], jnp.ones((16, vt.shape[1]), BF)], axis=0)
+        values = jnp.concatenate([vt[rows, :], jnp.ones((16, width), BF)], axis=0)
         out = nn(values, weights)
         total = out[HS : HS + 1]
         ot[rows, :] = (out[:HS] * (1.0 / total)).astype(BF)
@@ -97,36 +109,43 @@
         finish(2 * i + 1, two)
         return carry
 
-    if pause is None:
-        lax.fori_loop(0, HEADS // 2, body, 0, unroll=True)
-    else:
-        lax.fori_loop(0, HEADS // 4, body, 0, unroll=True)
-        pause()
-        lax.fori_loop(HEADS // 4, HEADS // 2, body, 0, unroll=True)
-
-
-def attend_back(qt, kt, vt, bias, ot, lse, dot, dqt, dkt, dvt, pause=None):
+    lax.fori_loop(0, HEADS // 2, body, 0, unroll=True)
+
+
+def split_rows(row, count):
+    high = row.astype(BF)
+    rest = row - high.astype(F32)
+    mid = rest.astype(BF)
+    low = (rest - mid.astype(F32)).astype(BF)
+    index = lax.broadcasted_iota(jnp.int32, (16, row.shape[1]), 0)
+    parts = jnp.where(index == 0, high, jnp.where(index == 1, mid, low))
+    return jnp.where(index < 3, parts, BF(count))
+
+
+def attend_back(qt, kt, vt, bias, length, ot, lse, dot, dqt, dkt, dvt):
+    index = lax.broadcasted_iota(jnp.int32, (16, kt.shape[1]), 0)
+    ones = jnp.where(index < 3, 1.0, 0.0).astype(BF)
+    masks = ones
+    if bias is None:
+        masked = (index == 3) & (lax.broadcasted_iota(jnp.int32, index.shape, 1) >= length)
+        masks = jnp.where(masked, NEG, ones.astype(F32)).astype(BF)
+
     def head(h, carry):
         rows = head_rows(h)
         keys, grads = kt[rows, :], dot[rows, :]
         queries = qt[rows, :] * BF(0.125)
         delta = jnp.sum(grads.astype(F32) * ot[rows, :].astype(F32), axis=0, keepdims=True)
-        probs = jnp.exp(tn(keys, queries) + bias[...] - lse[pl.ds(h, 1), :])
-        dscores = (probs * (tn(vt[rows, :], grads) - delta)).astype(BF)
-        dvt[rows, :] = nt(grads, probs.astype(BF)).astype(BF)
-        dkt[rows, :] = nt(queries, dscores).astype(BF)
-        dqt[rows, :] = (nn(keys, dscores) * 0.125).astype(BF)
+        left = jnp.concatenate([queries, split_rows(-lse[pl.ds(h, 1), :], 1)], axis=0)
+        scores = tn(left, jnp.concatenate([keys, masks], axis=0))
+        probs = jnp.exp(scores if bias is None else scores + bias[...])
+        left = jnp.concatenate([grads, split_rows(-delta, 0)], axis=0)
+        dscores = (probs * tn(left, jnp.concatenate([vt[rows, :], ones], axis=0))).astype(BF)
+        dvt[rows, :] = nn(grads, probs.astype(BF)).astype(BF)
+        dkt[rows, :] = nn(queries, dscores).astype(BF)
+        dqt[rows, :] = (nt(keys, dscores) * 0.125).astype(BF)
         return carry
 
-    if pause is None:
-        lax.fori_loop(0, HEADS, head, 0, unroll=4)
-    else:
-        def half(i, carry):
-            lax.fori_loop(4 * i, 4 * i + 4, head, 0, unroll=True)
-            pause()
-            return carry
-
-        lax.fori_loop(0, HEADS // 4, half, 0)
+    lax.fori_loop(0, HEADS, head, 0, unroll=True)
 
 
 GAIN, SHIFT, B2, B1 = 0, 3, 6, 7
@@ -162,7 +181,7 @@
     for index, out in enumerate((qt, kt, vt)):
         out[...] = tn(sq[index][...], ut[...]).astype(BF)
     pause()
-    attend(qt, kt, vt, bias, ot, lse, pair, pause)
+    attend(qt, kt, vt, bias, length, ot, lse, pair)
     pause()
     et[...] += tn(sq[3][...], ot[...])
     gain, shift = self_column(vec, first, GAIN), self_column(vec, first, SHIFT)
@@ -193,11 +212,11 @@
         dsa[:, lanes] = grad.astype(BF)
 
     lane_loop(tokens, leave)
-    fill_bias(bias, length, jnp.logical_not(first))
+    fill_bias(bias, length, jnp.logical_not(first), 1)
     dot[...] = nn(sq[3][...], dsa[...]).astype(BF)
     dsq[3] += nt(ot[...], dsa[...])
     pause()
-    attend_back(qt, kt, vt, bias, ot, lse, dot, dqt, dkt, dvt, pause)
+    attend_back(qt, kt, vt, bias, length, ot, lse, dot, dqt, dkt, dvt)
     for index, grad in enumerate((dqt, dkt, dvt)):
         dsq[index] += nt(ut[...], grad[...])
         dy[...] += nn(sq[index][...], grad[...])
@@ -287,11 +306,10 @@
     add_column(dvec, SHIFT + 2, vacc[RU + 2])
 
 
-def cross_forward(a, sq, vec, length, ab, cqt, kt, vt, ot, lse, n1, r1, bias, pair):
+def cross_forward(a, sq, vec, length, ab, cqt, kt, vt, ot, lse, n1, r1, pair):
     ab[...] = a[...].astype(BF)
     cqt[...] = tn(sq[0][...], ab[...]).astype(BF)
-    fill_bias(bias, length, None)
-    attend(cqt, kt, vt, bias, ot, lse, pair)
+    attend(cqt, kt, vt, None, length, ot, lse, pair)
     a[...] += tn(sq[1][...], ot[...])
 
     def leave(lanes):
@@ -304,7 +322,7 @@
 
 
 def cross_backward(
-    dbq, sq, vec, ab, cqt, kt, vt, ot, lse, n1, r1, bias, dca, dot, dqt, dkt, dvt, dsq, dvec, vacc
+    dbq, sq, vec, length, ab, cqt, kt, vt, ot, lse, n1, r1, dca, dot, dqt, dkt, dvt, dsq, dvec, vacc, ready
 ):
     vacc[0] = jnp.zeros(vacc.shape[1:], F32)
     vacc[1] = jnp.zeros(vacc.shape[1:], F32)
@@ -320,7 +338,8 @@
     lane_loop(dbq.shape[1], leave)
     dot[...] = nn(sq[1][...], dca[...]).astype(BF)
     dsq[1][...] += nt(ot[...], dca[...])
-    attend_back(cqt, kt, vt, bias, ot, lse, dot, dqt, dkt, dvt)
+    attend_back(cqt, kt, vt, None, length, ot, lse, dot, dqt, dkt, dvt)
+    ready()
     dsq[0][...] += nt(ab[...], dqt[...])
     dbq[...] += nn(sq[0][...], dqt[...])
     add_column(dvec, GAIN + 1, vacc[0])
@@ -328,7 +347,7 @@
 
 
 SUB = 256
-HOP = 3
+HOP = 4
 HALF = SUB // 2
 QUART = SUB // 4
 UNITS = 6 + 2 * RU
@@ -352,7 +371,7 @@
         far = self.last
         self.ticks = SUBS + HOP * (2 + far + far) + 1
 
-    def greet(self):
+    def greet(self, across=False):
         barrier = pltpu.get_barrier_semaphore()
 
         def signal(index):
@@ -362,7 +381,10 @@
         signal(self.beside)
         pl.when(self.has_left)(lambda: signal(self.dp - 4))
         pl.when(self.has_right)(lambda: signal(self.dp + 4))
-        pl.semaphore_wait(barrier, 2 + self.has_left.astype(jnp.int32) + self.has_right.astype(jnp.int32))
+        if across:
+            pl.semaphore_signal(barrier, inc=1, device_id=(1 - self.section, self.dp), device_id_type=MESH)
+        sides = self.has_left.astype(jnp.int32) + self.has_right.astype(jnp.int32)
+        pl.semaphore_wait(barrier, 2 + int(across) + sides)
 
     def short_route(self, t):
         return ((t & 1) == 0) | ((t >= self.shorts[0]) & (t < self.shorts[1]))
@@ -642,6 +664,7 @@
 FIRST_UNIT = (0, 1, 2, 3, 4, 5, 6, 6 + RU)
 VEC_BLOCKS = VEC_ROWS // SUB
 EARLY = 4 * D // SUB + VEC_BLOCKS
+LINKED = 6 * D // SUB + VEC_BLOCKS
 PIECE = 16
 
 
@@ -656,9 +679,9 @@
     return prior
 
 
-def start_kernel(n_dp, info, owners, x, slots, pack, out, vec, *refs):
+def start_kernel(n_dp, info, owners, x, slots, pack, out, vec, linked, *refs):
     saved_out, (y_out, stage, *comm), refs = refs[:10], refs[10:19], refs[19:]
-    saved, (y, xb, bias, et, pair, places, counter, sems) = refs[:10], refs[10:]
+    saved, (y, xb, bias, et, pair, places, counter, sems, link_sems) = refs[:10], refs[10:]
     count, tokens = saved_out[0].shape[0], saved_out[0].shape[2]
     first = lax.axis_index("section") == 0
     dp = lax.axis_index("dp")
@@ -681,7 +704,7 @@
     total = Total(
         n_dp,
         order,
-        (0, EARLY),
+        (0, LINKED),
         lambda t, block, start: stage.at[t],
         lambda t, block, start: own(block, start),
         out,
@@ -697,7 +720,15 @@
         loop(begin, stop, lambda now: total.tick(now, prepare))
         counter[0] = stop
 
-    total.greet()
+    link = pltpu.make_async_remote_copy(
+        src_ref=out.at[pl.ds(4 * D, 2 * D)],
+        dst_ref=linked,
+        send_sem=link_sems.at[0],
+        recv_sem=link_sems.at[1],
+        device_id=(1 - total.section, dp),
+        device_id_type=MESH,
+    )
+    total.greet(across=True)
     counter[0] = 0
     run(EARLY + HOP * (3 + total.last))
     loop(0, EARLY, total.arrive)
@@ -710,6 +741,12 @@
         return copies(saved + (y,), [ref.at[b] for ref in saved_out + (y_out,)], sems)
 
     def block(b):
+        @pl.when(b == 1)
+        def _():
+            run(jnp.maximum(LINKED + HOP * (3 + total.last) - counter[0], 0))
+            loop(EARLY, LINKED, total.arrive)
+            pl.when(first)(lambda: link.start())
+
         load = pltpu.make_async_copy(x.at[pl.ds(pl.multiple_of(b * tokens, tokens), tokens)], xb, sems.at[11])
         load.start()
 
@@ -730,8 +767,10 @@
     run(total.ticks)
     for copy in outward(count - 1):
         copy.wait()
-    loop(EARLY, SUBS, total.arrive)
+    loop(LINKED, SUBS, total.arrive)
     loop(0, SUBS, total.settle)
+    pl.when(first)(lambda: link.wait_send())
+    pl.when(jnp.logical_not(first))(lambda: link.wait_recv())
 
 
 def saved_dims(tokens):
@@ -746,11 +785,11 @@
     return pl.pallas_call(
         functools.partial(start_kernel, n_dp),
         name="start",
-        out_shape=[shape16(SUBS * SUB, D), shape32(D, LANES)]
+        out_shape=[shape16(SUBS * SUB, D), shape32(D, LANES), shape16(2 * D, D)]
         + [jax.ShapeDtypeStruct((count,) + dims, kind) for dims, kind in kept]
         + [shape32(count, D, tokens)],
         in_specs=[smem_space(), smem_space(), any_space(), vmem_space(), vmem_space()],
-        out_specs=[vmem_space(), vmem_space()] + [any_space()] * 11,
+        out_specs=[vmem_space()] * 3 + [any_space()] * 11,
         scratch_shapes=[pltpu.VMEM((SUBS, HALF, D), BF)]
         + total_scratch()
         + [pltpu.VMEM(dims, kind) for dims, kind in kept]
@@ -763,6 +802,7 @@
             pltpu.SMEM((2, UNITS), jnp.int32),
             pltpu.SMEM((1,), jnp.int32),
             pltpu.SemaphoreType.DMA((12,)),
+            pltpu.SemaphoreType.DMA((2,)),
         ],
         compiler_params=pltpu.CompilerParams(
             collective_id=0, has_side_effects=True, vmem_limit_bytes=60 * 2**20
@@ -770,7 +810,7 @@
     )(info, owners, x, slots, pack)
 
 
-def finish_kernel(n_dp, info, dy, sq, vec, late, late_vec, *refs):
+def finish_kernel(n_dp, info, dy, sq, vec, late, late_vec, dsq_in, dx_in, *refs):
     saved_in, (dx_out, out), (stage, *comm), refs = refs[:10], refs[10:12], refs[12:20], refs[20:]
     saved, (dys, dx, bias, dsa, dot, dqt, dkt, dvt, dsq, dvec, vacc, pack, counter, sems) = refs[:10], refs[10:]
     count, tokens = dy.shape[0], dy.shape[2]
@@ -809,28 +849,35 @@
 
     total.greet()
     counter[0] = 0
-    dsq[...] = jnp.zeros(dsq.shape, F32)
+    load_dsq = pltpu.make_async_copy(dsq_in, dsq, sems.at[12])
+    load_dsq.start()
     dvec[...] = late_vec[...]
+    load_dsq.wait()
+    begin = count // 2
     squares = [sq.at[pl.ds(i * D, D)] for i in range(4)]
 
     def block(b):
         loads = copies([ref.at[b] for ref in saved_in] + [dy.at[b]], saved + (dys,), sems)
         for copy in loads:
             copy.start()
-        run(1, others)
-        store = pltpu.make_async_copy(
-            dx, dx_out.at[pl.ds(pl.multiple_of(b * tokens, tokens), tokens)], sems.at[11]
-        )
-        pl.when(b > 0)(lambda: store.wait())
+        run(4, others)
+
+        def store(b):
+            return pltpu.make_async_copy(
+                dx, dx_out.at[pl.ds(pl.multiple_of(b * tokens, tokens), tokens)], sems.at[11]
+            )
+
+        pl.when(b > begin)(lambda: store(b - 1).wait())
         for copy in loads:
             copy.wait()
         self_backward(
             dys, squares, vec, first, info[1 + b], *saved, dx,
-            bias, dsa, dot, dqt, dkt, dvt, dsq, dvec, vacc, lambda: run(1, others),
+            bias, dsa, dot, dqt, dkt, dvt, dsq, dvec, vacc, lambda: run(3, others),
         )
-        store.start()
-
-    loop(0, count, block)
+        store(b).start()
+        pl.when(b == count - 1)(lambda: store(b).wait())
+
+    loop(begin, count, block)
     value = dvec[...].T[:PIECE]
     high = value.astype(BF)
     rest = value - high.astype(F32)
@@ -840,12 +887,11 @@
     pack[PIECE : 2 * PIECE, :] = mid
     pack[2 * PIECE : 3 * PIECE, :] = (rest - mid.astype(F32)).astype(BF)
     run(total.ticks, total.ticks)
-    pltpu.make_async_copy(dx, dx_out.at[pl.ds(0, tokens)], sems.at[11]).wait()
     loop(0, SUBS, total.arrive)
     loop(0, SUBS, total.settle)
 
 
-def call_finish(n_dp, info, dy, weights, vec, late, late_vec, saved):
+def call_finish(n_dp, info, dy, weights, vec, late, late_vec, dsq, dx, saved):
     count, tokens = dy.shape[0], dy.shape[2]
     kept = saved_dims(tokens)
     wide16 = pltpu.VMEM((D, tokens), BF)
@@ -863,8 +909,9 @@
             vmem_space(),
             vmem_space(),
         ]
-        + [any_space()] * 10,
+        + [any_space()] * 12,
         out_specs=[any_space(), vmem_space()],
+        input_output_aliases={7: 0},
         scratch_shapes=[pltpu.VMEM((SUBS, HALF, D), BF)]
         + total_scratch()
         + [pltpu.VMEM(dims, kind) for dims, kind in kept]
@@ -876,20 +923,25 @@
             pltpu.VMEM((4, D, LANES), F32),
             pltpu.VMEM((VEC_ROWS, D), BF),
             pltpu.SMEM((1,), jnp.int32),
-            pltpu.SemaphoreType.DMA((12,)),
+            pltpu.SemaphoreType.DMA((13,)),
         ],
         compiler_params=pltpu.CompilerParams(
             collective_id=2, has_side_effects=True, vmem_limit_bytes=60 * 2**20
         ),
-    )(info, dy, weights, vec, late, late_vec, *saved)
-
-
-def middle_kernel(
-    info, vec, y, cot, weights, hidden, dy, grads, dvec,
-    wts, acc, sent, got, h, mem, hb, act, slope, n2, r2, dfb, dz, vacc,
-    ab, cqt, kt, vt, ot, lse, n1, r1, bias, dca, dot, dqt, pair, tok, stage, sems, load_sem,
-):
+    )(info, dy, weights, vec, late, late_vec, dsq, dx, *saved)
+
+
+def middle_kernel(info, vec, y, cot, weights, linked, *refs):
+    saved_in, outs, refs = refs[:10], refs[10:16], refs[16:]
+    hidden, dy, dx_out, grads, dsq_out, dvec = outs
+    saved, refs = refs[:10], refs[10:]
+    ut, n0, r0, qt, kt, vt, ot, lse, n1, r1 = saved
+    (
+        wts, acc, dsq, sent, got, hbuf, mem, hb, act, slope, n2, r2, dfb, dz, vacc,
+        bias, dca, dot, dqt, dkt, dvt, pair, cotb, tok, dx, link, swaps, sems, saved_sems, grad_sems,
+    ) = refs
     section = lax.axis_index("section")
+    first = section == 0
     dp = lax.axis_index("dp")
     count, tokens = y.shape[0], y.shape[2]
     other = 1 - section
@@ -897,148 +949,255 @@
     pl.semaphore_signal(barrier, inc=1, device_id=(other, dp), device_id_type=MESH)
     pl.semaphore_wait(barrier, 1)
 
-    def move(source, target):
-        copy = pltpu.make_async_copy(source, target, load_sem)
-        copy.start()
-        copy.wait()
-
-    def swap(b):
+    def remote(source, target, step, b):
         return pltpu.make_async_remote_copy(
-            src_ref=sent.at[b],
-            dst_ref=got.at[b],
-            send_sem=sems.at[0, b],
-            recv_sem=sems.at[1, b],
+            src_ref=source,
+            dst_ref=target,
+            send_sem=swaps.at[step, b],
+            recv_sem=swaps.at[step + 1, b],
             device_id=(other, dp),
             device_id_type=MESH,
         )
 
-    def each(body):
-        def step(b, carry):
-            body(b)
-            return carry
-
-        lax.fori_loop(0, count, step, 0)
-
-    move(weights.at[pl.ds(4 * D, 10 * D)], wts)
-    unit = [wts.at[pl.ds(i * D, D)] for i in range(10)]
-    s4, s5, ffn = unit[0], unit[1], unit[2:]
-    acc[...] = jnp.zeros(acc.shape, F32)
-    dvec[...] = jnp.zeros(dvec.shape, F32)
+    def send_memory(b):
+        return remote(sent.at[b, 0], got.at[b, 0], 0, b)
+
+    def send_back(b):
+        return remote(sent.at[b], got.at[b], 2, b)
+
+    def rows(b):
+        return pl.ds(pl.multiple_of(b * tokens, tokens), tokens)
+
+    def load_y(b):
+        return pltpu.make_async_copy(y.at[b], hbuf.at[b % 2], sems.at[0])
+
+    def load_cot(b):
+        return pltpu.make_async_copy(cot.at[rows(b)], cotb, sems.at[1])
+
+    def store_hidden(b):
+        return pltpu.make_async_copy(tok, hidden.at[rows(b)], sems.at[2])
+
+    def store_dy(b):
+        return pltpu.make_async_copy(hbuf.at[b % 2], dy.at[b], sems.at[3])
+
+    def load_dy(b):
+        return pltpu.make_async_copy(dy.at[b], hbuf.at[b % 2], sems.at[0])
+
+    def store_dx(b):
+        return pltpu.make_async_copy(dx, dx_out.at[rows(b)], sems.at[4])
+
+    def load_saved(b):
+        return copies([ref.at[b] for ref in saved_in], saved, saved_sems)
+
+    unit = [wts.at[pl.ds(i * D, D)] for i in range(UNITS)]
+    part = 6 * D
+    load_rest = pltpu.make_async_copy(
+        weights.at[pl.ds(part, UNITS * D - part)], wts.at[pl.ds(part, UNITS * D - part)], sems.at[5]
+    )
+    load_squares = pltpu.make_async_copy(weights.at[pl.ds(0, part)], wts.at[pl.ds(0, part)], sems.at[6])
+    load_link = pltpu.make_async_copy(linked, link, sems.at[7])
+    load_y(0).start()
+    load_rest.start()
+    pl.when(jnp.logical_not(first))(lambda: load_link.start())
+    load_squares.start()
+    s4, s5, ffn = unit[4], unit[5], unit[6:]
     cross_acc = [acc.at[i] for i in range(2)]
-    ffn_acc = [acc.at[2 + i] for i in range(8)]
-
-    def run_feed_forward():
+    ffn_acc = [acc.at[2 + i] for i in range(2 * RU)]
+
+    def clear():
+        acc[...] = jnp.zeros(acc.shape, F32)
+        dsq[...] = jnp.zeros(dsq.shape, F32)
+        dvec[...] = jnp.zeros(dvec.shape, F32)
+
+    def run_feed_forward(h):
         feed_forward(h, ffn, vec, hb, act, slope, n2, r2, mem)
 
     def emit_hidden(b):
+        pl.when(b > 0)(lambda: store_hidden(b - 1).wait())
         tok[...] = mem[...].T.astype(BF)
-        move(tok, hidden.at[pl.ds(pl.multiple_of(b * tokens, tokens), tokens)])
-
-    def load_cotangent(b):
-        move(cot.at[pl.ds(pl.multiple_of(b * tokens, tokens), tokens)], tok)
+        store_hidden(b).start()
+
+    def take_cotangent(b, h):
+        load_cot(b).wait()
         token = lax.broadcasted_iota(jnp.int32, (D, tokens), 1)
-        h[...] = jnp.where(token < info[1 + b], tok[...].astype(F32).T, 0.0)
-
-    def run_feed_backward():
+        h[...] = jnp.where(token < info[1 + b], cotb[...].astype(F32).T, 0.0)
+
+    def run_feed_backward(h):
         feed_backward(h, ffn, vec, hb, act, slope, n2, r2, dfb, dz, ffn_acc, dvec, vacc)
 
-    @pl.when(section == 0)
+    def run_self_backward(b, h):
+        pl.when(b > 0)(lambda: store_dx(b - 1).wait())
+        self_backward(
+            h, unit[:4], vec, first, info[1 + b], *saved, dx,
+            bias, dca, dot, dqt, dkt, dvt, dsq, dvec, vacc.at[pl.ds(0, 4)], lambda: None,
+        )
+        store_dx(b).start()
+
+    @pl.when(first)
     def _():
+        load_rest.wait()
+
         def ahead(b):
-            move(y.at[b], h)
-            run_feed_forward()
+            h = hbuf.at[b % 2]
+            load_y(b).wait()
+            pl.when(b + 1 < count)(lambda: load_y(b + 1).start())
+            run_feed_forward(h)
+            sent[b, 0] = mem[...].astype(BF)
+            send_memory(b).start()
             emit_hidden(b)
-            short = mem[...].astype(BF)
-            sent[b, 0] = tn(s4[...], short).astype(BF)
-            sent[b, 1] = tn(s5[...], short).astype(BF)
-            swap(b).start()
-
-        each(ahead)
+
+        loop(0, count, ahead)
+        store_hidden(count - 1).wait()
+        load_squares.wait()
+        clear()
+        load_y(0).start()
 
         def back(b):
-            move(y.at[b], h)
-            run_feed_forward()
-            ab[...] = mem[...].astype(BF)
-            load_cotangent(b)
-            swap(b).wait_recv()
+            h = hbuf.at[b % 2]
+            loads = load_saved(b)
+            load_cot(b).start()
+            load_y(b).wait()
+            pl.when(b < count // 2)(lambda: [copy.start() for copy in loads] and None)
+            run_feed_forward(h)
+            take_cotangent(b, h)
+            send_back(b).wait_recv()
             for i, matrix in enumerate((s4, s5)):
                 h[...] += nn(matrix[...], got[b, i])
-                acc[i] += nt(ab[...], got[b, i])
-            run_feed_backward()
-            move(h, dy.at[b])
-
-        each(back)
-
-    @pl.when(section == 1)
+                acc[i] += nt(sent[b, 0], got[b, i])
+            run_feed_backward(h)
+
+            @pl.when(b < count // 2)
+            def _():
+                load_y(b + 1).start()
+                for copy in loads:
+                    copy.wait()
+                run_self_backward(b, h)
+
+            @pl.when(b >= count // 2)
+            def _():
+                store_dy(b).start()
+
+                @pl.when(b + 1 < count)
+                def _():
+                    load_y(b + 1).start()
+                    store_dy(b).wait()
+
+        loop(0, count, back)
+        store_dy(count - 1).wait()
+        store_dx(count // 2 - 1).wait()
+
+    @pl.when(jnp.logical_not(first))
     def _():
+        clear()
+        load_rest.wait()
+        load_squares.wait()
+        load_link.wait()
+
         def both(b):
-            move(y.at[b], h)
-            swap(b).wait_recv()
-            kt[...] = got[b, 0]
-            vt[...] = got[b, 1]
-            cross_forward(h, (s4, s5), vec, info[1 + count + b], ab, cqt, kt, vt, ot, lse, n1, r1, bias, pair)
-            run_feed_forward()
+            h = hbuf.at[b % 2]
+            load_cot(b).start()
+            load_y(b).wait()
+            send_memory(b).wait_recv()
+            for i, target in enumerate((kt, vt)):
+                target[...] = tn(link[pl.ds(i * D, D), :], got[b, 0]).astype(BF)
+            cross = (ut, qt, kt, vt, ot, lse, n1, r1)
+            cross_forward(h, (s4, s5), vec, info[1 + count + b], *cross, pair)
+            run_feed_forward(h)
             emit_hidden(b)
-            load_cotangent(b)
-            run_feed_backward()
+            take_cotangent(b, h)
+
+            pl.when(b > 0)(lambda: store_dy(b - 1).wait())
+            pl.when(b + 1 < count)(lambda: load_y(b + 1).start())
+            run_feed_backward(h)
             cross_backward(
-                h, (s4, s5), vec, ab, cqt, kt, vt, ot, lse, n1, r1, bias, dca, dot, dqt,
-                sent.at[b, 0], sent.at[b, 1], cross_acc, dvec, vacc,
+                h, (s4, s5), vec, info[1 + count + b], *cross, dca, dot, dqt,
+                sent.at[b, 0], sent.at[b, 1], cross_acc, dvec, vacc, lambda: send_back(b).start(),
             )
-            swap(b).start()
-            move(h, dy.at[b])
-
-        each(both)
-
-    def finish(b):
-        swap(b).wait_send()
-
-    each(finish)
+            store_dy(b).start()
+
+        loop(0, count, both)
+        store_hidden(count - 1).wait()
+        store_dy(count - 1).wait()
+
+        def back(b):
+            loads = load_saved(b)
+            for copy in loads + [load_dy(b)]:
+                copy.start()
+            for copy in loads + [load_dy(b)]:
+                copy.wait()
+            run_self_backward(b, hbuf.at[b % 2])
+
+        loop(0, count // 2, back)
+        store_dx(count // 2 - 1).wait()
+
+    @pl.when(first)
+    def _():
+        loop(0, count, lambda b: send_memory(b).wait_send())
+
+    @pl.when(jnp.logical_not(first))
+    def _():
+        loop(0, count, lambda b: send_back(b).wait_send())
+
+    out_dsq = pltpu.make_async_copy(dsq, dsq_out, sems.at[6])
+    out_dsq.start()
+    out_grads = []
     for i in range(10):
-        stage[...] = acc[i].astype(BF)
-        move(stage, grads.at[pl.ds(i * D, D)])
-
-
-def call_middle(info, vec, y, cot, weights, count, tokens):
+        rows_i = pl.ds(i * D, D)
+        wts[rows_i, :] = acc[i].astype(BF)
+        out_grads.append(pltpu.make_async_copy(wts.at[rows_i], grads.at[rows_i], grad_sems.at[i]))
+        out_grads[-1].start()
+    for copy in out_grads:
+        copy.wait()
+    out_dsq.wait()
+
+
+def call_middle(info, vec, y, cot, weights, linked, saved):
+    count, tokens = y.shape[0], y.shape[2]
+    kept = saved_dims(tokens)
     wide16 = pltpu.VMEM((D, tokens), BF)
     wide32 = pltpu.VMEM((D, tokens), F32)
-    row = pltpu.VMEM((1, tokens), F32)
+    tall16 = pltpu.VMEM((FF, tokens), BF)
     return pl.pallas_call(
         middle_kernel,
         name="middle",
         out_shape=[
             shape16(count * tokens, D),
             shape32(count, D, tokens),
+            shape32(count * tokens, D),
             shape16(10 * D, D),
+            shape32(4, D, D),
             shape32(D, LANES),
         ],
-        in_specs=[smem_space(), vmem_space(), any_space(), any_space(), any_space()],
-        out_specs=[any_space(), any_space(), any_space(), vmem_space()],
-        scratch_shapes=[
-            pltpu.VMEM((10 * D, D), BF),
+        in_specs=[smem_space(), vmem_space()] + [any_space()] * 14,
+        out_specs=[any_space()] * 5 + [vmem_space()],
+        scratch_shapes=[pltpu.VMEM(dims, kind) for dims, kind in kept]
+        + [
+            pltpu.VMEM((UNITS * D, D), BF),
             pltpu.VMEM((10, D, D), F32),
+            pltpu.VMEM((4, D, D), F32),
             pltpu.VMEM((count, 2, D, tokens), BF),
             pltpu.VMEM((count, 2, D, tokens), BF),
-            wide32, wide32, wide16,
-            pltpu.VMEM((FF, tokens), BF), pltpu.VMEM((FF, tokens), BF),
-            wide16, row, wide16,
-            pltpu.VMEM((FF, tokens), BF),
+            pltpu.VMEM((2, D, tokens), F32),
+            wide32, wide16, tall16, tall16, wide16,
+            pltpu.VMEM((1, tokens), F32),
+            wide16, tall16,
             pltpu.VMEM((RU + 3, D, LANES), F32),
-                wide16, wide16, wide16, wide16, wide16,
-            pltpu.VMEM((HEADS, tokens), F32),
-            wide16, row,
             pltpu.VMEM((tokens, tokens), F32),
-            wide16, wide16, wide16,
+            wide16, wide16, wide16, wide16, wide16,
             pltpu.VMEM((2, tokens, tokens), F32),
             pltpu.VMEM((tokens, D), BF),
-            pltpu.VMEM((D, D), BF),
-            pltpu.SemaphoreType.DMA((2, count)),
-            pltpu.SemaphoreType.DMA,
+            pltpu.VMEM((tokens, D), BF),
+            pltpu.VMEM((tokens, D), F32),
+            pltpu.VMEM((2 * D, D), BF),
+            pltpu.SemaphoreType.DMA((4, count)),
+            pltpu.SemaphoreType.DMA((8,)),
+            pltpu.SemaphoreType.DMA((10,)),
+            pltpu.SemaphoreType.DMA((10,)),
         ],
         compiler_params=pltpu.CompilerParams(
-            collective_id=1, has_side_effects=True, vmem_limit_bytes=60 * 2**20
+            collective_id=1, has_side_effects=True, vmem_limit_bytes=62 * 2**20
         ),
-    )(info, vec, y, cot, weights)
+    )(info, vec, y, cot, weights, linked, *saved)
 
 
 matrix_rate = 0.04
@@ -1117,10 +1276,11 @@
     pack = three_pieces(jnp.where(owns_vector, vec_store, 0.0))
     own = jnp.where(section == 0, lengths[0], lengths[1])
     info = jnp.concatenate([section[None].astype(jnp.int32), own, lengths[0]])
-    weights, vec, *saved = call_start(n_dp, info, owners, tokens[0], master_sq[0, 0], pack, count)
-    width = tokens.shape[1] // count
-    hidden, dy, late, late_vec = call_middle(info, vec, saved[10], cotangent[0], weights, count, width)
-    dx, total = call_finish(n_dp, info, dy, weights, vec, late, late_vec, saved[:10])
+    weights, vec, linked, *saved = call_start(n_dp, info, owners, tokens[0], master_sq[0, 0], pack, count)
+    hidden, dy, dx, late, dsq, late_vec = call_middle(
+        info, vec, saved[10], cotangent[0], weights, linked, saved[:10]
+    )
+    dx, total = call_finish(n_dp, info, dy, weights, vec, late, late_vec, dsq, dx, saved[:10])
     pieces = total[UNITS * D : UNITS * D + 3 * PIECE].astype(F32).reshape(3, PIECE, D)[:, :vrows]
     total_vector = pieces[0] + pieces[1] + pieces[2]
     place = slot_units(owners[0], dp, master_sq.shape[2])

time: 459 us -> 429 us (0.935)
  the two profiles are of different devices: /device:TPU:1 before, /device:TPU:0 now
where the time goes in v3:
time: 429 us; the launch traced here: 421 us
  Pallas kernels  405 us (94%)
  local copies, waits for them, and re-layouts  10.2 us (2%)
    pallas_call x1, Pallas kernels, call_middle(): pl.pallas_call(middle_kernel, name='middle', out_shape=[shape16(count * t...  176 us
    pallas_call x1, Pallas kernels, call_finish(): pl.pallas_call(functools.partial(finish_kernel, n_dp), name='finish', out...  107 us
    pallas_call x1, Pallas kernels, call_start(): pl.pallas_call(functools.partial(start_kernel, n_dp), name='start', out_s...  107 us
    pallas_call x1, Pallas kernels, call_adam(): pl.pallas_call(adam_kernel, name='adam', out_shape=[out] * 3, grid_spec=p...  16 us

profile of v3, /device:TPU:0, one launch (start us, length us, event | category | flops | bytes accessed | tf_op | source)
XLA Modules:
  0.0 420.9 jit_solution(613212619512691132)
XLA Ops:
  0.6 0.7 slice_bitcast_fusion.1
  1.3 0.8 broadcast_select_fusion
  2.1 0.6 pad_add_fusion.info
  2.7 1.2 slice.34
  4.6 0.7 fusion.13
  5.3 0.7 fusion.9
  6.0 0.7 pad.17.pack
  6.8 106.7 %start.1 = (bf16[7424,512]{1,0:T(8,128)(2,1)}, f32[512,128]{1,0:T(8,128)}, bf16[1024,512]{1,0:T(8,128)(2,1)}, bf16[4,512,512]{2,1,0:T(8,128)(2,1)}, bf16[4,512,5...) custom-call(s32[9]{0:T(128)} %pad_add_fusion.info, ...), custom_call_target="tpu_custom_call" | custom-call | tf_op jit(solution)/shard_map/start/pallas_call | solution.py:785
  113.4 175.9 %middle.1 = (bf16[2048,512]{1,0:T(8,128)(2,1)}, f32[4,512,512]{2,1,0:T(8,128)}, f32[2048,512]{1,0:T(8,128)}, bf16[5120,512]{1,0:T(8,128)(2,1)}, f32[4,512,512]{2,1,0:T(8,128)}, /*index=5*/f32[512,128]{1,0:T(8,128)}) custom-call(s32[9]{0:T(128)} %pad_add_fusion.info, f32[512,128]{1,0:T(8,128)} %get-tuple-element.33.vec, f32[4,512,512]{2,1,0:T(8,128)} %get-tuple-element.34.y, ...), custom_call_target="tpu_custom_call" | custom-call | tf_op jit(solution)/shard_map/middle/pallas_call | solution.py:1160
  289.4 0.0 copy-start.6
  289.4 0.0 copy-start.5
  289.4 0.0 copy-start.8
  289.4 0.0 copy-start.7
  289.4 0.0 copy-start.9
  289.5 106.7 %finish.1 = (f32[2048,512]{1,0:T(8,128)}, bf16[7424,512]{1,0:T(8,128)(2,1)}) custom-call(s32[9]{0:T(128)} %pad_add_fusion.info, f32[4,512,512]{2,1,0:T(8,128)} %get-tuple-element.48.dy, bf16[7424,512]{1,0:T(8,128)(2,1)} %get-tuple-element.35.weights.sq, f32[512,128]{1,0:T(8,128)} %get-tuple-element.33.vec, ...), custom_call_target="tpu_custom_call", output_to_operand_aliasing={{0}: (7, {})} | custom-call | tf_op jit(solution)/shard_map/finish/pallas_call | solution.py:899
  396.2 0.0 copy-done.6
  396.2 0.2 select_reduce_fusion.1
  396.4 0.0 copy-done.7
  396.4 0.7 gather_fusion.1
  397.1 0.0 copy-done.9
  397.1 0.7 gather_fusion
  397.7 0.1 select_reduce_fusion
  397.9 0.5 broadcast_add_fusion.place
  398.4 16.0 %adam.1 = (f32[6,512,512]{2,1,0:T(8,128)}, f32[6,512,512]{2,1,0:T(8,128)}, f32[6,512,512]{2,1,0:T(8,128)}) custom-call(s32[6]{0:T(128)} %broadcast_add_fusion.place, bf16[7424,512]{1,0:T(8,128)(2,1)} %get-tuple-element.54.grad, f32[6,512,512]{2,1,0:T(8,128)} %bitcast.42, f32[6,512,512]{2,1,0:T(8,128)} %bitcast.44, f32[6,512,512]{2,1,0:T(8,128)} %bitcast.45), custom_call_target="tpu_custom_call" | custom-call | tf_op jit(solution)/shard_map/adam/pallas_call | solution.py:1227
  414.4 1.0 slice.37
  415.4 0.0 copy-done.2
  415.4 0.0 copy-done.4
  415.4 0.6 copy.55
  416.1 0.6 copy.56
  416.7 0.6 copy.57
  417.3 1.3 copy.102
  418.7 2.0 copy.103
  (19 shorter events, 0.1 us)
Async XLA Ops:
  289.4 106.8 %copy-start.6 = (s32[1,9]{1,0:T(1,128)S(1)}, s32[1,9]{1,0:T(1,128)}, u32[]{:S(2)}) copy-start(s32[1,9]{1,0:T(1,128)} %owners.1) | copy-start | bytes 112
  289.4 106.8 %copy-start.5 = (pred[8,8]{1,0:T(8,128)(4,1)S(1)}, pred[8,8]{1,0:T(8,128)(4,1)}, u32[]{:S(2)}) copy-start(pred[8,8]{1,0:T(8,128)(4,1)} %constant.43.clone) | copy-start | bytes 196
  289.4 106.8 %copy-start.8 = (s32[8]{0:T(128)S(1)}, s32[8]{0:T(128)}, u32[]{:S(2)}) copy-start(s32[8]{0:T(128)} %constant.44.clone) | copy-start | bytes 100
  289.4 106.9 %copy-start.7 = (s32[14]{0:T(128)S(1)}, s32[14]{0:T(128)}, u32[]{:S(2)}) copy-start(s32[14]{0:T(128)} %constant.67) | copy-start | bytes 172
  289.4 107.6 %copy-start.9 = (s32[14]{0:T(128)S(1)}, s32[14]{0:T(128)}, u32[]{:S(2)}) copy-start(s32[14]{0:T(128)} %constant.47.clone) | copy-start | bytes 172
  398.4 16.9 %copy-start.3 = (f32[1,1,11,512]{3,1,2,0:T(1,128)S(1)}, f32[1,1,11,512]{3,1,2,0:T(1,128)}, u32[]{:S(2)}) copy-start(f32[1,1,11,512]{3,1,2,0:T(1,128)} %param.25) | copy-start | bytes 67588
  398.4 17.0 %copy-start.2 = (f32[1,1,11,512]{3,1,2,0:T(1,128)S(1)}, f32[1,1,11,512]{3,1,2,0:T(1,128)}, u32[]{:S(2)}) copy-start(f32[1,1,11,512]{3,1,2,0:T(1,128)} %param.23) | copy-start | bytes 67588
  398.4 17.0 %copy-start.4 = (f32[1,1,11,512]{3,1,2,0:T(1,128)S(1)}, f32[1,1,11,512]{3,1,2,0:T(1,128)}, u32[]{:S(2)}) copy-start(f32[1,1,11,512]{3,1,2,0:T(1,128)} %param.24) | copy-start | bytes 67588
  398.4 18.9 %copy-start.1 = (bf16[2048,512]{1,0:T(8,128)(2,1)S(1)}, bf16[2048,512]{1,0:T(8,128)(2,1)}, u32[]{:S(2)}) copy-start(bf16[2048,512]{1,0:T(8,128)(2,1)} %get-tuple-element.47) | copy-start | bytes 6291460
  414.4 4.3 %copy-start = (f32[2048,512]{1,0:T(8,128)S(1)}, f32[2048,512]{1,0:T(8,128)}, u32[]{:S(2)}) copy-start(f32[2048,512]{1,0:T(8,128)} %get-tuple-element.53) | copy-start | bytes 12582916

commit v4 on v3

--- a/solution.py
+++ b/solution.py
@@ -347,7 +347,7 @@
 
 
 SUB = 256
-HOP = 4
+HOP = 3
 HALF = SUB // 2
 QUART = SUB // 4
 UNITS = 6 + 2 * RU
@@ -810,19 +810,20 @@
     )(info, owners, x, slots, pack)
 
 
-def finish_kernel(n_dp, info, dy, sq, vec, late, late_vec, dsq_in, dx_in, *refs):
-    saved_in, (dx_out, out), (stage, *comm), refs = refs[:10], refs[10:12], refs[12:20], refs[20:]
-    saved, (dys, dx, bias, dsa, dot, dqt, dkt, dvt, dsq, dvec, vacc, pack, counter, sems) = refs[:10], refs[10:]
+def finish_kernel(n_dp, info, dy, sq, vec, late_in, late_vec, dsq_in, dx_in, *refs):
+    saved_in, (dx_out, out), (late, stage, *comm), refs = refs[:10], refs[10:12], refs[12:21], refs[21:]
+    saved, (dys, dx, bias, dsa, dot, dqt, dkt, dvt, dsq, dvec, vacc, pack, counter, sems, link_sems) = refs[:10], refs[10:]
     count, tokens = dy.shape[0], dy.shape[2]
     first = lax.axis_index("section") == 0
     early = EARLY - VEC_BLOCKS
     others = SUBS - EARLY
 
+    mixed = 2 * D // SUB
+    plain = others - mixed
+
     def order(t):
-        return jnp.where(t < others, t + early, jnp.where(t < SUBS - VEC_BLOCKS, t - others, t))
-
-    def late_rows(block, start):
-        return pl.ds(pl.multiple_of((block - early) * SUB + start, HALF), HALF)
+        block = jnp.where(t < plain, t + early + mixed, t - plain + early)
+        return jnp.where(t < others, block, jnp.where(t < SUBS - VEC_BLOCKS, t - others, t))
 
     def own_early(block, start):
         unit = jnp.minimum(block * SUB // D, 3)
@@ -830,15 +831,18 @@
         value = dsq[unit, pl.ds(at, HALF), :].astype(BF)
         return jnp.where(block >= SUBS - VEC_BLOCKS, pack[pl.ds(pl.multiple_of(start, HALF), HALF), :], value)
 
+    def own_late(block, start):
+        return late[pl.ds(pl.multiple_of((block - early) * SUB + start, HALF), HALF), :]
+
     def mine(t, block, start):
-        at = jnp.clip((block - early) * SUB, 0, (others - 1) * SUB) + start
-        return jnp.where(t < others, late[pl.ds(pl.multiple_of(at, HALF), HALF), :], own_early(block, start))
+        return lax.cond(t < others, lambda: own_late(block, start), lambda: own_early(block, start))
 
     total = Total(
         n_dp, order, (others, SUBS), lambda t, block, start: stage.at[t], mine, out, *comm
     )
 
     def prepare(t):
+        pl.when((t == plain) & first)(lambda: link.wait_recv())
         stage[t] = mine(t, order(t), HALF * (1 - total.core))
 
     def run(ticks, end):
@@ -847,12 +851,27 @@
         loop(begin, stop, lambda now: total.tick(now, prepare))
         counter[0] = stop
 
-    total.greet()
+    link = pltpu.make_async_remote_copy(
+        src_ref=late_in.at[pl.ds(10 * D, 2 * D)],
+        dst_ref=late.at[pl.ds(0, 2 * D)],
+        send_sem=link_sems.at[0],
+        recv_sem=link_sems.at[1],
+        device_id=(1 - total.section, total.dp),
+        device_id_type=MESH,
+    )
     counter[0] = 0
     load_dsq = pltpu.make_async_copy(dsq_in, dsq, sems.at[12])
     load_dsq.start()
+    load_late = pltpu.make_async_copy(late_in.at[pl.ds(2 * D, 8 * D)], late.at[pl.ds(2 * D, 8 * D)], sems.at[13])
+    load_mixed = pltpu.make_async_copy(late_in.at[pl.ds(0, 2 * D)], late.at[pl.ds(0, 2 * D)], sems.at[14])
+    load_late.start()
+    pl.when(jnp.logical_not(first))(lambda: load_mixed.start())
     dvec[...] = late_vec[...]
+    total.greet(across=True)
+    pl.when(jnp.logical_not(first))(lambda: link.start())
     load_dsq.wait()
+    load_late.wait()
+    pl.when(jnp.logical_not(first))(lambda: load_mixed.wait())
     begin = count // 2
     squares = [sq.at[pl.ds(i * D, D)] for i in range(4)]
 
@@ -889,6 +908,7 @@
     run(total.ticks, total.ticks)
     loop(0, SUBS, total.arrive)
     loop(0, SUBS, total.settle)
+    pl.when(jnp.logical_not(first))(lambda: link.wait_send())
 
 
 def call_finish(n_dp, info, dy, weights, vec, late, late_vec, dsq, dx, saved):
@@ -906,13 +926,13 @@
             any_space(),
             pl.BlockSpec((4 * D, D), lambda i: (0, 0)),
             vmem_space(),
-            vmem_space(),
+            any_space(),
             vmem_space(),
         ]
         + [any_space()] * 12,
         out_specs=[any_space(), vmem_space()],
         input_output_aliases={7: 0},
-        scratch_shapes=[pltpu.VMEM((SUBS, HALF, D), BF)]
+        scratch_shapes=[pltpu.VMEM((10 * D, D), BF), pltpu.VMEM((SUBS, HALF, D), BF)]
         + total_scratch()
         + [pltpu.VMEM(dims, kind) for dims, kind in kept]
         + [wide32, pltpu.VMEM((tokens, D), F32), pltpu.VMEM((tokens, tokens), F32)]
@@ -923,7 +943,8 @@
             pltpu.VMEM((4, D, LANES), F32),
             pltpu.VMEM((VEC_ROWS, D), BF),
             pltpu.SMEM((1,), jnp.int32),
-            pltpu.SemaphoreType.DMA((13,)),
+            pltpu.SemaphoreType.DMA((15,)),
+            pltpu.SemaphoreType.DMA((2,)),
         ],
         compiler_params=pltpu.CompilerParams(
             collective_id=2, has_side_effects=True, vmem_limit_bytes=60 * 2**20
@@ -960,7 +981,7 @@
         )
 
     def send_memory(b):
-        return remote(sent.at[b, 0], got.at[b, 0], 0, b)
+        return remote(sent.at[b], got.at[b], 0, b)
 
     def send_back(b):
         return remote(sent.at[b], got.at[b], 2, b)
@@ -1002,7 +1023,10 @@
     load_squares.start()
     s4, s5, ffn = unit[4], unit[5], unit[6:]
     cross_acc = [acc.at[i] for i in range(2)]
+    link_acc = acc.at[pl.ds(10, 2)]
     ffn_acc = [acc.at[2 + i] for i in range(2 * RU)]
+
+    out_dsq = pltpu.make_async_copy(dsq, dsq_out, sems.at[6])
 
     def clear():
         acc[...] = jnp.zeros(acc.shape, F32)
@@ -1042,7 +1066,7 @@
             load_y(b).wait()
             pl.when(b + 1 < count)(lambda: load_y(b + 1).start())
             run_feed_forward(h)
-            sent[b, 0] = mem[...].astype(BF)
+            sent[b] = mem[...].astype(BF)
             send_memory(b).start()
             emit_hidden(b)
 
@@ -1061,9 +1085,7 @@
             run_feed_forward(h)
             take_cotangent(b, h)
             send_back(b).wait_recv()
-            for i, matrix in enumerate((s4, s5)):
-                h[...] += nn(matrix[...], got[b, i])
-                acc[i] += nt(sent[b, 0], got[b, i])
+            h[...] += got[b].astype(F32)
             run_feed_backward(h)
 
             @pl.when(b < count // 2)
@@ -1072,6 +1094,7 @@
                 for copy in loads:
                     copy.wait()
                 run_self_backward(b, h)
+                pl.when(b == count // 2 - 1)(lambda: out_dsq.start())
 
             @pl.when(b >= count // 2)
             def _():
@@ -1093,13 +1116,18 @@
         load_squares.wait()
         load_link.wait()
 
+        def give_back(b):
+            grad = nn(link[0:D, :], dkt[...]) + nn(link[D : 2 * D, :], dvt[...])
+            sent[b] = grad.astype(BF)
+            send_back(b).start()
+
         def both(b):
             h = hbuf.at[b % 2]
             load_cot(b).start()
             load_y(b).wait()
             send_memory(b).wait_recv()
             for i, target in enumerate((kt, vt)):
-                target[...] = tn(link[pl.ds(i * D, D), :], got[b, 0]).astype(BF)
+                target[...] = tn(link[pl.ds(i * D, D), :], got[b]).astype(BF)
             cross = (ut, qt, kt, vt, ot, lse, n1, r1)
             cross_forward(h, (s4, s5), vec, info[1 + count + b], *cross, pair)
             run_feed_forward(h)
@@ -1111,8 +1139,10 @@
             run_feed_backward(h)
             cross_backward(
                 h, (s4, s5), vec, info[1 + count + b], *cross, dca, dot, dqt,
-                sent.at[b, 0], sent.at[b, 1], cross_acc, dvec, vacc, lambda: send_back(b).start(),
+                dkt, dvt, cross_acc, dvec, vacc, lambda: give_back(b),
             )
+            for i, grad in enumerate((dkt, dvt)):
+                link_acc[i] += nt(got[b], grad[...])
             store_dy(b).start()
 
         loop(0, count, both)
@@ -1128,6 +1158,7 @@
             run_self_backward(b, hbuf.at[b % 2])
 
         loop(0, count // 2, back)
+        out_dsq.start()
         store_dx(count // 2 - 1).wait()
 
     @pl.when(first)
@@ -1138,10 +1169,8 @@
     def _():
         loop(0, count, lambda b: send_back(b).wait_send())
 
-    out_dsq = pltpu.make_async_copy(dsq, dsq_out, sems.at[6])
-    out_dsq.start()
     out_grads = []
-    for i in range(10):
+    for i in range(12):
         rows_i = pl.ds(i * D, D)
         wts[rows_i, :] = acc[i].astype(BF)
         out_grads.append(pltpu.make_async_copy(wts.at[rows_i], grads.at[rows_i], grad_sems.at[i]))
@@ -1164,7 +1193,7 @@
             shape16(count * tokens, D),
             shape32(count, D, tokens),
             shape32(count * tokens, D),
-            shape16(10 * D, D),
+            shape16(12 * D, D),
             shape32(4, D, D),
             shape32(D, LANES),
         ],
@@ -1173,10 +1202,10 @@
         scratch_shapes=[pltpu.VMEM(dims, kind) for dims, kind in kept]
         + [
             pltpu.VMEM((UNITS * D, D), BF),
-            pltpu.VMEM((10, D, D), F32),
+            pltpu.VMEM((12, D, D), F32),
             pltpu.VMEM((4, D, D), F32),
-            pltpu.VMEM((count, 2, D, tokens), BF),
-            pltpu.VMEM((count, 2, D, tokens), BF),
+            pltpu.VMEM((count, D, tokens), BF),
+            pltpu.VMEM((count, D, tokens), BF),
             pltpu.VMEM((2, D, tokens), F32),
             wide32, wide16, tall16, tall16, wide16,
             pltpu.VMEM((1, tokens), F32),
@@ -1192,7 +1221,7 @@
             pltpu.SemaphoreType.DMA((4, count)),
             pltpu.SemaphoreType.DMA((8,)),
             pltpu.SemaphoreType.DMA((10,)),
-            pltpu.SemaphoreType.DMA((10,)),
+            pltpu.SemaphoreType.DMA((12,)),
         ],
         compiler_params=pltpu.CompilerParams(
             collective_id=1, has_side_effects=True, vmem_limit_bytes=62 * 2**20

time: 429 us -> 414 us (0.965)
  the two profiles are of different devices: /device:TPU:0 before, /device:TPU:1 now
where the time goes in v4:
time: 414 us; the launch traced here: 406 us
  Pallas kernels  390 us (94%)
  local copies, waits for them, and re-layouts  10.2 us (2%)
    pallas_call x1, Pallas kernels, call_middle(): pl.pallas_call(middle_kernel, name='middle', out_shape=[shape16(count * t...  163 us
    pallas_call x1, Pallas kernels, call_start(): pl.pallas_call(functools.partial(start_kernel, n_dp), name='start', out_s...  110 us
    pallas_call x1, Pallas kernels, call_finish(): pl.pallas_call(functools.partial(finish_kernel, n_dp), name='finish', out...  101 us
    pallas_call x1, Pallas kernels, call_adam(): pl.pallas_call(adam_kernel, name='adam', out_shape=[out] * 3, grid_spec=p...  16 us

profile of v4, /device:TPU:1, one launch (start us, length us, event | category | flops | bytes accessed | tf_op | source)
XLA Modules:
  0.0 406.0 jit_solution(12909138232503792922)
XLA Ops:
  0.6 0.7 slice_bitcast_fusion.1
  1.3 0.8 broadcast_select_fusion
  2.1 0.6 pad_add_fusion.info
  2.7 1.2 slice.34
  4.6 0.7 fusion.13
  5.3 0.7 fusion.9
  6.0 0.7 pad.17.pack
  6.8 110.0 %start.1 = (bf16[7424,512]{1,0:T(8,128)(2,1)}, f32[512,128]{1,0:T(8,128)}, bf16[1024,512]{1,0:T(8,128)(2,1)}, bf16[4,512,512]{2,1,0:T(8,128)(2,1)}, bf16[4,512,5...) custom-call(s32[9]{0:T(128)} %pad_add_fusion.info, ...), custom_call_target="tpu_custom_call" | custom-call | tf_op jit(solution)/shard_map/start/pallas_call | solution.py:785
  116.8 163.3 %middle.1 = (bf16[2048,512]{1,0:T(8,128)(2,1)}, f32[4,512,512]{2,1,0:T(8,128)}, f32[2048,512]{1,0:T(8,128)}, bf16[6144,512]{1,0:T(8,128)(2,1)}, f32[4,512,512]{2,1,0:T(8,128)}, /*index=5*/f32[512,128]{1,0:T(8,128)}) custom-call(s32[9]{0:T(128)} %pad_add_fusion.info, f32[512,128]{1,0:T(8,128)} %get-tuple-element.33.vec, f32[4,512,512]{2,1,0:T(8,128)} %get-tuple-element.34.y, ...), custom_call_target="tpu_custom_call" | custom-call | tf_op jit(solution)/shard_map/middle/pallas_call | solution.py:1189
  280.1 0.0 copy-start.6
  280.1 0.0 copy-start.5
  280.1 0.0 copy-start.8
  280.1 0.0 copy-start.7
  280.1 0.0 copy-start.9
  280.2 101.1 %finish.1 = (f32[2048,512]{1,0:T(8,128)}, bf16[7424,512]{1,0:T(8,128)(2,1)}) custom-call(s32[9]{0:T(128)} %pad_add_fusion.info, f32[4,512,512]{2,1,0:T(8,128)} %get-tuple-element.48.dy, bf16[7424,512]{1,0:T(8,128)(2,1)} %get-tuple-element.35.weights.sq, f32[512,128]{1,0:T(8,128)} %get-tuple-element.33.vec, ...), custom_call_target="tpu_custom_call", output_to_operand_aliasing={{0}: (7, {})} | custom-call | tf_op jit(solution)/shard_map/finish/pallas_call | solution.py:919
  381.2 0.0 copy-done.6
  381.3 0.0 copy-done.5
  381.3 0.0 copy-done.8
  381.3 0.2 select_reduce_fusion.1
  381.5 0.0 copy-done.7
  381.5 0.7 gather_fusion.1
  382.2 0.7 gather_fusion
  382.8 0.1 select_reduce_fusion
  383.0 0.5 broadcast_add_fusion.place
  383.5 16.0 %adam.1 = (f32[6,512,512]{2,1,0:T(8,128)}, f32[6,512,512]{2,1,0:T(8,128)}, f32[6,512,512]{2,1,0:T(8,128)}) custom-call(s32[6]{0:T(128)} %broadcast_add_fusion.place, bf16[7424,512]{1,0:T(8,128)(2,1)} %get-tuple-element.54.grad, f32[6,512,512]{2,1,0:T(8,128)} %bitcast.42, f32[6,512,512]{2,1,0:T(8,128)} %bitcast.44, f32[6,512,512]{2,1,0:T(8,128)} %bitcast.45), custom_call_target="tpu_custom_call" | custom-call | tf_op jit(solution)/shard_map/adam/pallas_call | solution.py:1256
  399.5 1.0 slice.37
  400.4 0.0 copy-done.3
  400.5 0.6 copy.55
  401.2 0.6 copy.56
  401.8 0.6 copy.57
  402.4 1.3 copy.102
  403.7 2.0 copy.103
  (19 shorter events, 0.1 us)
Async XLA Ops:
  280.1 101.2 %copy-start.6 = (s32[1,9]{1,0:T(1,128)S(1)}, s32[1,9]{1,0:T(1,128)}, u32[]{:S(2)}) copy-start(s32[1,9]{1,0:T(1,128)} %owners.1) | copy-start | bytes 112
  280.1 101.2 %copy-start.5 = (pred[8,8]{1,0:T(8,128)(4,1)S(1)}, pred[8,8]{1,0:T(8,128)(4,1)}, u32[]{:S(2)}) copy-start(pred[8,8]{1,0:T(8,128)(4,1)} %constant.43.clone) | copy-start | bytes 196
  280.1 101.2 %copy-start.8 = (s32[8]{0:T(128)S(1)}, s32[8]{0:T(128)}, u32[]{:S(2)}) copy-start(s32[8]{0:T(128)} %constant.44.clone) | copy-start | bytes 100
  280.1 101.3 %copy-start.7 = (s32[14]{0:T(128)S(1)}, s32[14]{0:T(128)}, u32[]{:S(2)}) copy-start(s32[14]{0:T(128)} %constant.67) | copy-start | bytes 172
  280.1 102.0 %copy-start.9 = (s32[14]{0:T(128)S(1)}, s32[14]{0:T(128)}, u32[]{:S(2)}) copy-start(s32[14]{0:T(128)} %constant.47.clone) | copy-start | bytes 172
  383.5 16.9 %copy-start.3 = (f32[1,1,11,512]{3,1,2,0:T(1,128)S(1)}, f32[1,1,11,512]{3,1,2,0:T(1,128)}, u32[]{:S(2)}) copy-start(f32[1,1,11,512]{3,1,2,0:T(1,128)} %param.25) | copy-start | bytes 67588
  383.5 17.0 %copy-start.2 = (f32[1,1,11,512]{3,1,2,0:T(1,128)S(1)}, f32[1,1,11,512]{3,1,2,0:T(1,128)}, u32[]{:S(2)}) copy-start(f32[1,1,11,512]{3,1,2,0:T(1,128)} %param.23) | copy-start | bytes 67588
  383.5 17.0 %copy-start.4 = (f32[1,1,11,512]{3,1,2,0:T(1,128)S(1)}, f32[1,1,11,512]{3,1,2,0:T(1,128)}, u32[]{:S(2)}) copy-start(f32[1,1,11,512]{3,1,2,0:T(1,128)} %param.24) | copy-start | bytes 67588
  383.5 18.9 %copy-start.1 = (bf16[2048,512]{1,0:T(8,128)(2,1)S(1)}, bf16[2048,512]{1,0:T(8,128)(2,1)}, u32[]{:S(2)}) copy-start(bf16[2048,512]{1,0:T(8,128)(2,1)} %get-tuple-element.47) | copy-start | bytes 6291460
  399.5 4.3 %copy-start = (f32[2048,512]{1,0:T(8,128)S(1)}, f32[2048,512]{1,0:T(8,128)}, u32[]{:S(2)}) copy-start(f32[2048,512]{1,0:T(8,128)} %get-tuple-element.53) | copy-start | bytes 12582916

commit v5 on v4

--- a/solution.py
+++ b/solution.py
@@ -261,7 +261,8 @@
         rows = slice(c * D, (c + 1) * D)
         a, s = gelu_parts(tn(units[c][...], hb[...]) + column(vec, B1 + c))
         act[rows, :] = a.astype(BF)
-        slope[rows, :] = s.astype(BF)
+        if slope is not None:
+            slope[rows, :] = s.astype(BF)
     for c in range(RU):
         rows = slice(c * D, (c + 1) * D)
         h[...] += tn(units[RU + c][...], act[rows, :])
@@ -347,7 +348,6 @@
 
 
 SUB = 256
-HOP = 3
 HALF = SUB // 2
 QUART = SUB // 4
 UNITS = 6 + 2 * RU
@@ -357,8 +357,9 @@
 
 
 class Total:
-    def __init__(self, n_dp, order, shorts, other, mine, out, core_in, half, x_in, right_in, left_in, passed, sems):
+    def __init__(self, n_dp, hop, order, shorts, other, mine, out, core_in, half, x_in, right_in, left_in, passed, sems):
         self.length = n_dp // 4
+        self.hop = hop
         self.last = self.length - 1
         self.section = lax.axis_index("section")
         self.dp = lax.axis_index("dp")
@@ -369,7 +370,7 @@
         self.out, self.core_in, self.half, self.x_in = out, core_in, half, x_in
         self.right_in, self.left_in, self.passed, self.sems = right_in, left_in, passed, sems
         far = self.last
-        self.ticks = SUBS + HOP * (2 + far + far) + 1
+        self.ticks = SUBS + self.hop * (2 + far + far) + 1
 
     def greet(self, across=False):
         barrier = pltpu.get_barrier_semaphore()
@@ -577,7 +578,7 @@
             self.copy_core(prepared).start()
 
         def due(step, lag, short):
-            t = now - HOP * lag
+            t = now - self.hop * lag
             fits = (t >= 0) & (t < SUBS)
             kind = self.short_route(t) if short else jnp.logical_not(self.short_route(t))
             pl.when(fits & kind)(lambda: step(t))
@@ -595,7 +596,7 @@
         due(self.long_x, 2 + far, False)
         for home in range(self.length):
             lag = 2 + max(home, last - home) + jnp.abs(z - home)
-            t = now - HOP * lag
+            t = now - self.hop * lag
             fits = (t >= 0) & (t < SUBS) & jnp.logical_not(self.short_route(t)) & (self.home(t) == home)
             pl.when(fits & (z != home))(lambda t=t: self.long_back(t))
 
@@ -703,6 +704,7 @@
 
     total = Total(
         n_dp,
+        4,
         order,
         (0, LINKED),
         lambda t, block, start: stage.at[t],
@@ -730,7 +732,7 @@
     )
     total.greet(across=True)
     counter[0] = 0
-    run(EARLY + HOP * (3 + total.last))
+    run(EARLY + total.hop * (3 + total.last))
     loop(0, EARLY, total.arrive)
     rows = [out[pl.ds(UNITS * D + i * PIECE, PIECE), :].astype(F32) for i in range(3)]
     whole = jnp.concatenate([rows[0] + rows[1] + rows[2], jnp.zeros((LANES - PIECE, D), F32)], axis=0)
@@ -743,7 +745,7 @@
     def block(b):
         @pl.when(b == 1)
         def _():
-            run(jnp.maximum(LINKED + HOP * (3 + total.last) - counter[0], 0))
+            run(jnp.maximum(LINKED + total.hop * (3 + total.last) - counter[0], 0))
             loop(EARLY, LINKED, total.arrive)
             pl.when(first)(lambda: link.start())
 
@@ -838,7 +840,7 @@
         return lax.cond(t < others, lambda: own_late(block, start), lambda: own_early(block, start))
 
     total = Total(
-        n_dp, order, (others, SUBS), lambda t, block, start: stage.at[t], mine, out, *comm
+        n_dp, 3, order, (others, SUBS), lambda t, block, start: stage.at[t], mine, out, *comm
     )
 
     def prepare(t):
@@ -861,15 +863,14 @@
     )
     counter[0] = 0
     load_dsq = pltpu.make_async_copy(dsq_in, dsq, sems.at[12])
-    load_dsq.start()
     load_late = pltpu.make_async_copy(late_in.at[pl.ds(2 * D, 8 * D)], late.at[pl.ds(2 * D, 8 * D)], sems.at[13])
     load_mixed = pltpu.make_async_copy(late_in.at[pl.ds(0, 2 * D)], late.at[pl.ds(0, 2 * D)], sems.at[14])
     load_late.start()
     pl.when(jnp.logical_not(first))(lambda: load_mixed.start())
+    load_dsq.start()
     dvec[...] = late_vec[...]
     total.greet(across=True)
     pl.when(jnp.logical_not(first))(lambda: link.start())
-    load_dsq.wait()
     load_late.wait()
     pl.when(jnp.logical_not(first))(lambda: load_mixed.wait())
     begin = count // 2
@@ -886,6 +887,7 @@
                 dx, dx_out.at[pl.ds(pl.multiple_of(b * tokens, tokens), tokens)], sems.at[11]
             )
 
+        pl.when(b == begin)(lambda: load_dsq.wait())
         pl.when(b > begin)(lambda: store(b - 1).wait())
         for copy in loads:
             copy.wait()
@@ -1033,8 +1035,8 @@
         dsq[...] = jnp.zeros(dsq.shape, F32)
         dvec[...] = jnp.zeros(dvec.shape, F32)
 
-    def run_feed_forward(h):
-        feed_forward(h, ffn, vec, hb, act, slope, n2, r2, mem)
+    def run_feed_forward(h, kept=slope):
+        feed_forward(h, ffn, vec, hb, act, kept, n2, r2, mem)
 
     def emit_hidden(b):
         pl.when(b > 0)(lambda: store_hidden(b - 1).wait())
@@ -1065,7 +1067,7 @@
             h = hbuf.at[b % 2]
             load_y(b).wait()
             pl.when(b + 1 < count)(lambda: load_y(b + 1).start())
-            run_feed_forward(h)
+            run_feed_forward(h, None)
             sent[b] = mem[...].astype(BF)
             send_memory(b).start()
             emit_hidden(b)
@@ -1169,14 +1171,31 @@
     def _():
         loop(0, count, lambda b: send_back(b).wait_send())
 
-    out_grads = []
-    for i in range(12):
-        rows_i = pl.ds(i * D, D)
-        wts[rows_i, :] = acc[i].astype(BF)
-        out_grads.append(pltpu.make_async_copy(wts.at[rows_i], grads.at[rows_i], grad_sems.at[i]))
-        out_grads[-1].start()
-    for copy in out_grads:
-        copy.wait()
+    def out_grad(i):
+        place = pl.ds(i * D, D)
+        return pltpu.make_async_copy(wts.at[place], grads.at[place], grad_sems.at[i])
+
+    def emit(i):
+        wts[pl.ds(i * D, D), :] = acc[i].astype(BF)
+        out_grad(i).start()
+
+    crossed = (0, 1, 10, 11)
+
+    @pl.when(jnp.logical_not(first))
+    def _():
+        for i in crossed:
+            emit(i)
+
+    for i in range(2, 10):
+        emit(i)
+
+    @pl.when(jnp.logical_not(first))
+    def _():
+        for i in crossed:
+            out_grad(i).wait()
+
+    for i in range(2, 10):
+        out_grad(i).wait()
     out_dsq.wait()
 
 

time: 414 us -> 409 us (0.988)
  no operation moved by 1% of the time
where the time goes in v5:
time: 409 us; the launch traced here: 401 us
  Pallas kernels  386 us (94%)
  local copies, waits for them, and re-layouts  10.2 us (2%)
    pallas_call x1, Pallas kernels, call_middle(): pl.pallas_call(middle_kernel, name='middle', out_shape=[shape16(count * t...  162 us
    pallas_call x1, Pallas kernels, call_start(): pl.pallas_call(functools.partial(start_kernel, n_dp), name='start', out_s...  107 us
    pallas_call x1, Pallas kernels, call_finish(): pl.pallas_call(functools.partial(finish_kernel, n_dp), name='finish', out...  101 us
    pallas_call x1, Pallas kernels, call_adam(): pl.pallas_call(adam_kernel, name='adam', out_shape=[out] * 3, grid_spec=p...  16 us

profile of v5, /device:TPU:1, one launch (start us, length us, event | category | flops | bytes accessed | tf_op | source)
XLA Modules:
  0.0 401.3 jit_solution(13528882819354693920)
XLA Ops:
  0.6 0.7 slice_bitcast_fusion.1
  1.3 0.8 broadcast_select_fusion
  2.1 0.6 pad_add_fusion.info
  2.7 1.2 slice.34
  4.6 0.7 fusion.13
  5.3 0.7 fusion.9
  6.0 0.7 pad.17.pack
  6.8 107.3 %start.1 = (bf16[7424,512]{1,0:T(8,128)(2,1)}, f32[512,128]{1,0:T(8,128)}, bf16[1024,512]{1,0:T(8,128)(2,1)}, bf16[4,512,512]{2,1,0:T(8,128)(2,1)}, bf16[4,512,5...) custom-call(s32[9]{0:T(128)} %pad_add_fusion.info, ...), custom_call_target="tpu_custom_call" | custom-call | tf_op jit(solution)/shard_map/start/pallas_call | solution.py:787
  114.1 161.7 %middle.1 = (bf16[2048,512]{1,0:T(8,128)(2,1)}, f32[4,512,512]{2,1,0:T(8,128)}, f32[2048,512]{1,0:T(8,128)}, bf16[6144,512]{1,0:T(8,128)(2,1)}, f32[4,512,512]{2,1,0:T(8,128)}, /*index=5*/f32[512,128]{1,0:T(8,128)}) custom-call(s32[9]{0:T(128)} %pad_add_fusion.info, f32[512,128]{1,0:T(8,128)} %get-tuple-element.33.vec, f32[4,512,512]{2,1,0:T(8,128)} %get-tuple-element.34.y, ...), custom_call_target="tpu_custom_call" | custom-call | tf_op jit(solution)/shard_map/middle/pallas_call | solution.py:1208
  275.8 0.0 copy-start.6
  275.8 0.0 copy-start.5
  275.8 0.0 copy-start.8
  275.8 0.0 copy-start.7
  275.8 0.0 copy-start.9
  275.8 100.7 %finish.1 = (f32[2048,512]{1,0:T(8,128)}, bf16[7424,512]{1,0:T(8,128)(2,1)}) custom-call(s32[9]{0:T(128)} %pad_add_fusion.info, f32[4,512,512]{2,1,0:T(8,128)} %get-tuple-element.48.dy, bf16[7424,512]{1,0:T(8,128)(2,1)} %get-tuple-element.35.weights.sq, f32[512,128]{1,0:T(8,128)} %get-tuple-element.33.vec, ...), custom_call_target="tpu_custom_call", output_to_operand_aliasing={{0}: (7, {})} | custom-call | tf_op jit(solution)/shard_map/finish/pallas_call | solution.py:921
  376.5 0.0 copy-done.5
  376.6 0.0 copy-done.8
  376.6 0.2 select_reduce_fusion.1
  376.7 0.0 copy-done.7
  376.8 0.7 gather_fusion.1
  377.4 0.7 gather_fusion
  378.1 0.1 select_reduce_fusion
  378.2 0.5 broadcast_add_fusion.place
  378.8 16.0 %adam.1 = (f32[6,512,512]{2,1,0:T(8,128)}, f32[6,512,512]{2,1,0:T(8,128)}, f32[6,512,512]{2,1,0:T(8,128)}) custom-call(s32[6]{0:T(128)} %broadcast_add_fusion.place, bf16[7424,512]{1,0:T(8,128)(2,1)} %get-tuple-element.54.grad, f32[6,512,512]{2,1,0:T(8,128)} %bitcast.42, f32[6,512,512]{2,1,0:T(8,128)} %bitcast.44, f32[6,512,512]{2,1,0:T(8,128)} %bitcast.45), custom_call_target="tpu_custom_call" | custom-call | tf_op jit(solution)/shard_map/adam/pallas_call | solution.py:1275
  394.7 1.0 slice.37
  395.7 0.0 copy-done.2
  395.7 0.0 copy-done.4
  395.8 0.6 copy.55
  396.4 0.6 copy.56
  397.1 0.6 copy.57
  397.7 1.3 copy.102
  399.0 2.0 copy.103
  (19 shorter events, 0.1 us)
Async XLA Ops:
  275.8 100.8 %copy-start.6 = (s32[1,9]{1,0:T(1,128)S(1)}, s32[1,9]{1,0:T(1,128)}, u32[]{:S(2)}) copy-start(s32[1,9]{1,0:T(1,128)} %owners.1) | copy-start | bytes 112
  275.8 100.8 %copy-start.5 = (pred[8,8]{1,0:T(8,128)(4,1)S(1)}, pred[8,8]{1,0:T(8,128)(4,1)}, u32[]{:S(2)}) copy-start(pred[8,8]{1,0:T(8,128)(4,1)} %constant.43.clone) | copy-start | bytes 196
  275.8 100.8 %copy-start.8 = (s32[8]{0:T(128)S(1)}, s32[8]{0:T(128)}, u32[]{:S(2)}) copy-start(s32[8]{0:T(128)} %constant.44.clone) | copy-start | bytes 100
  275.8 100.9 %copy-start.7 = (s32[14]{0:T(128)S(1)}, s32[14]{0:T(128)}, u32[]{:S(2)}) copy-start(s32[14]{0:T(128)} %constant.67) | copy-start | bytes 172
  275.8 101.6 %copy-start.9 = (s32[14]{0:T(128)S(1)}, s32[14]{0:T(128)}, u32[]{:S(2)}) copy-start(s32[14]{0:T(128)} %constant.47.clone) | copy-start | bytes 172
  378.8 16.9 %copy-start.3 = (f32[1,1,11,512]{3,1,2,0:T(1,128)S(1)}, f32[1,1,11,512]{3,1,2,0:T(1,128)}, u32[]{:S(2)}) copy-start(f32[1,1,11,512]{3,1,2,0:T(1,128)} %param.25) | copy-start | bytes 67588
  378.8 17.0 %copy-start.2 = (f32[1,1,11,512]{3,1,2,0:T(1,128)S(1)}, f32[1,1,11,512]{3,1,2,0:T(1,128)}, u32[]{:S(2)}) copy-start(f32[1,1,11,512]{3,1,2,0:T(1,128)} %param.23) | copy-start | bytes 67588
  378.8 17.0 %copy-start.4 = (f32[1,1,11,512]{3,1,2,0:T(1,128)S(1)}, f32[1,1,11,512]{3,1,2,0:T(1,128)}, u32[]{:S(2)}) copy-start(f32[1,1,11,512]{3,1,2,0:T(1,128)} %param.24) | copy-start | bytes 67588
  378.8 18.9 %copy-start.1 = (bf16[2048,512]{1,0:T(8,128)(2,1)S(1)}, bf16[2048,512]{1,0:T(8,128)(2,1)}, u32[]{:S(2)}) copy-start(bf16[2048,512]{1,0:T(8,128)(2,1)} %get-tuple-element.47) | copy-start | bytes 6291460
  394.7 4.3 %copy-start = (f32[2048,512]{1,0:T(8,128)S(1)}, f32[2048,512]{1,0:T(8,128)}, u32[]{:S(2)}) copy-start(f32[2048,512]{1,0:T(8,128)} %get-tuple-element.53) | copy-start | bytes 12582916
